TPU v7x, 128 devices: a whole 4x4x4 slice. The times are simulated.
128 devices in a mesh: wide: 16 (over x, y), narrow: 8 (over z, core).
Axes of the slice: x: 4, y: 4, z: 4, core: 2. Of those that a mesh axis runs over, the one named last changes fastest.
Arguments:
- query_proj: bfloat16 [32768, 2048], P(('wide', 'narrow')), may hold values from -20 to 20
- key_proj: bfloat16 [32768, 2048], P(('wide', 'narrow')), may hold values from -20 to 20
- value_proj: bfloat16 [32768, 2048], P(('wide', 'narrow')), may hold values from -6 to 6
- positions: int32 [3, 32768], P(None, ('wide', 'narrow')), may hold values from 0 to 142, as said below
- key_lists: int32 [256, 24], replicated, may hold values from 0 to 255, as said below
- key_counts: int32 [256], replicated, may hold values from 6 to 24
Outputs:
- attended: bfloat16 [32768, 2048], P(('wide', 'narrow'))
Inputs may be any that keep to these rules, and one draw needn't show every extreme that they name: `key_lists`: each list holds distinct key blocks and always its own query block; entries after the first key_counts ones repeat the own block. Over the query blocks of one frame of 16 blocks, at most 4 distinct blocks of any other frame are listed, and exactly 4 of each adjacent frame; a query block may list no block of some farther frames. `positions`: Rows: frame id, height id, width id.
All inputs are finite; a program needn't handle non-finite values.
Results may differ from a plain program's by a relative error of at most 0.012.
Values may be sent and summed in bfloat16 or wider, within the bound.
No kernel may reach another device: no remote copies, remote signals or barrier semaphores. Data moves between devices by JAX's collectives and lax.ppermute only.
A program may use at most 128 MiB of HBM per device.

v0:
```python
import jax
import jax.numpy as jnp
from jax import lax
from jax.sharding import PartitionSpec as P

HEADS = 16
HD = 128
BLOCK = 128
CAP = 4


def rotate(values, positions):
    head_dim = values.shape[-1]
    first_size = head_dim // 4
    second_size = 3 * head_dim // 8
    bounds = (0, first_size, first_size + second_size, head_dim)
    pieces = []
    for axis_row in range(3):
        begin_at = bounds[axis_row]
        end_at = bounds[axis_row + 1]
        section = end_at - begin_at
        half_size = section // 2
        inverse_freq = 10000.0 ** (-2.0 * jnp.arange(half_size, dtype=jnp.float32) / section)
        angles = positions[axis_row].astype(jnp.float32)[:, None] * inverse_freq[None, :]
        cosine = jnp.cos(angles)[:, None, :]
        sines = jnp.sin(angles)[:, None, :]
        lower_half = values[..., begin_at : begin_at + half_size]
        upper_half = values[..., begin_at + half_size : end_at]
        pieces.append(lower_half * cosine - upper_half * sines)
        pieces.append(upper_half * cosine + lower_half * sines)
    return jnp.concatenate(pieces, axis=-1)


def shards(query_proj, key_proj, value_proj, positions, key_lists, key_counts):
    narrow_size = lax.axis_size("narrow")
    wide_size = lax.axis_size("wide")
    tok_rows = query_proj.shape[0]
    local_heads = HEADS // narrow_size
    frame_rows = tok_rows * narrow_size
    frame_blocks = frame_rows // BLOCK
    frame_index = lax.axis_index("wide")
    scale = HD ** (-0.5)
    q_local = rotate(query_proj.astype(jnp.float32).reshape(tok_rows, HEADS, HD), positions).astype(
        jnp.bfloat16
    )
    k_local = rotate(key_proj.astype(jnp.float32).reshape(tok_rows, HEADS, HD), positions).astype(
        jnp.bfloat16
    )
    v_local = value_proj.reshape(tok_rows, HEADS, HD)
    q_frame, k_frame, v_frame = (
        lax.all_to_all(q_local, "narrow", split_axis=1, concat_axis=0, tiled=True),
        lax.all_to_all(k_local, "narrow", split_axis=1, concat_axis=0, tiled=True),
        lax.all_to_all(v_local, "narrow", split_axis=1, concat_axis=0, tiled=True),
    )
    list_width = key_lists.shape[1]
    all_blocks = key_lists.shape[0]
    live = jnp.arange(list_width, dtype=jnp.int32)[None, :] < key_counts[:, None]
    hits = (key_lists[:, :, None] == jnp.arange(all_blocks, dtype=jnp.int32)[None, None, :]) & live[
        :, :, None
    ]
    dense = jnp.any(hits, axis=1)
    union = jnp.any(dense.reshape(wide_size, frame_blocks, wide_size, frame_blocks), axis=1)
    ranks = jnp.cumsum(union.astype(jnp.int32), axis=-1) - 1
    slot_pick = union[..., None] & (
        ranks[..., None] == jnp.arange(CAP, dtype=jnp.int32)[None, None, None, :]
    )
    slot_block = jnp.sum(
        slot_pick.astype(jnp.int32)
        * jnp.arange(frame_blocks, dtype=jnp.int32)[None, None, :, None],
        axis=2,
    )
    slot_live = jnp.any(slot_pick, axis=2)
    k_blocks = k_frame.reshape(frame_blocks, BLOCK, local_heads, HD)
    v_blocks = v_frame.reshape(frame_blocks, BLOCK, local_heads, HD)
    my_slots = lax.dynamic_index_in_dim(slot_block, frame_index, 0, keepdims=False)
    all_k, all_v = (
        lax.all_gather(k_frame, "wide", axis=0, tiled=True),
        lax.all_gather(v_frame, "wide", axis=0, tiled=True),
    )
    block_ids = (jnp.arange(wide_size, dtype=jnp.int32)[:, None] * frame_blocks + my_slots).reshape(
        -1
    )
    got_k = jnp.take(
        all_k.reshape(wide_size * frame_blocks, BLOCK, local_heads, HD), block_ids, axis=0
    )
    got_v = jnp.take(
        all_v.reshape(wide_size * frame_blocks, BLOCK, local_heads, HD), block_ids, axis=0
    )
    my_live = lax.dynamic_index_in_dim(slot_live, frame_index, 0, keepdims=False)
    my_live = my_live & (jnp.arange(wide_size, dtype=jnp.int32) != frame_index)[:, None]
    cand_ids = jnp.concatenate(
        [
            frame_index * frame_blocks + jnp.arange(frame_blocks, dtype=jnp.int32),
            (jnp.arange(wide_size, dtype=jnp.int32)[:, None] * frame_blocks + my_slots).reshape(-1),
        ]
    )
    cand_live = jnp.concatenate([jnp.ones((frame_blocks,), dtype=bool), my_live.reshape(-1)])
    key_rows = jnp.concatenate([k_blocks, got_k], axis=0)
    value_rows = jnp.concatenate([v_blocks, got_v], axis=0)
    cand_blocks = key_rows.shape[0]
    key_rows = key_rows.reshape(cand_blocks * BLOCK, local_heads, HD)
    value_rows = value_rows.reshape(cand_blocks * BLOCK, local_heads, HD)
    rows_mine = lax.dynamic_slice_in_dim(dense, frame_index * frame_blocks, frame_blocks, 0)
    allowed = jnp.take(rows_mine, cand_ids, axis=1) & cand_live[None, :]
    row_count = min(512, frame_rows)
    turn_count = frame_rows // row_count
    per_turn = row_count // BLOCK
    outputs = []
    for head_index in range(local_heads):
        query_head = q_frame[:, head_index, :]
        key_head = key_rows[:, head_index, :]
        value_head = value_rows[:, head_index, :]

        def attend(row_block):
            query_now = lax.dynamic_slice_in_dim(query_head, row_block * row_count, row_count, 0)
            scores = (
                jnp.einsum("qd,kd->qk", query_now, key_head, preferred_element_type=jnp.float32)
                * scale
            )
            allowed_now = lax.dynamic_slice_in_dim(allowed, row_block * per_turn, per_turn, 0)
            scores = scores.reshape(per_turn, BLOCK, cand_blocks, BLOCK)
            scores = jnp.where(allowed_now[:, None, :, None], scores, -jnp.inf)
            scores = scores.reshape(row_count, cand_blocks * BLOCK)
            row_max = jnp.max(scores, axis=-1, keepdims=True)
            weights = jnp.exp(scores - row_max)
            row_total = jnp.sum(weights, axis=-1)
            weights_low = weights.astype(jnp.bfloat16)
            mixed = jnp.dot(weights_low, value_head, preferred_element_type=jnp.float32)
            return (mixed / row_total[:, None]).astype(jnp.bfloat16)

        head_out = lax.map(attend, jnp.arange(turn_count, dtype=jnp.int32))
        outputs.append(head_out.reshape(frame_rows, HD))
    attended_frame = jnp.stack(outputs, axis=1)
    attended = lax.all_to_all(attended_frame, "narrow", split_axis=0, concat_axis=1, tiled=True)
    return attended.reshape(tok_rows, HEADS * HD)


def solution(mesh):
    return jax.shard_map(
        shards,
        mesh=mesh,
        in_specs=(
            P(("wide", "narrow"), None),
            P(("wide", "narrow"), None),
            P(("wide", "narrow"), None),
            P(None, ("wide", "narrow")),
            P(),
            P(),
        ),
        out_specs=P(("wide", "narrow"), None),
        check_vma=False,
    )
```

profile of v0, /device:TPU:0, one launch (start us, length us, event | category | flops | bytes accessed | tf_op | source)
XLA Modules:
  0.0 545.5 jit_solution(15379587852609958293)
XLA Ops:
  15.2 21.3 %all_to_all.69 = bf16[256,16,128]{0,2,1:T(8,128)(2,1)S(1)} all-to-all(bf16[256,16,128]{0,2,1:T(8,128)(2,1)S(1)} %get-tuple-element.234), channel_id=1, replica_groups=mesh['wide'=16,'narrow'=8] {'narrow'}, dimensions={1} | all-to-all | bytes 2097152 | tf_op jit(solution)/shard_map/all_to_all | solution.py:52
  38.5 18.5 %all_to_all.70 = bf16[256,16,128]{0,2,1:T(8,128)(2,1)S(1)} all-to-all(bf16[256,16,128]{0,2,1:T(8,128)(2,1)S(1)} %bitcast.120), channel_id=1, replica_groups=mesh['wide'=16,'narrow'=8] {'narrow'}, dimensions={1} | all-to-all | bytes 2097152 | tf_op jit(solution)/shard_map/all_to_all | solution.py:53
  58.3 3.9 all-to-all-start
  73.1 4.9 all-to-all-done
  79.8 68.9 %all-gather.3.cloned.1.call-done = bf16[32768,2,128]{2,0,1:T(8,128)(2,1)} async-done(((bf16[2048,2,128]{2,0,1:T(8,128)(2,1)}), bf16[32768,2,128]{2,0,1:T(8,128)(2,1)}) %all-gather.3.cloned.1.call-update) | async-done | bytes 16777232 | tf_op jit(solution)/shard_map/all_gather | solution.py:77
  148.7 14.3 %copy.128 = bf16[256,128,2,128]{3,1,2,0:T(8,128)(2,1)} copy(bf16[256,128,2,128]{3,1,0,2:T(8,128)(2,1)} %bitcast.106) | data formatting | bytes 33554432 | tf_op jit(solution)/shard_map/reshape | solution.py:84
  163.0 98.9 %all-gather.5.cloned.1.call-done = bf16[32768,2,128]{2,0,1:T(8,128)(2,1)} async-done(((bf16[2048,2,128]{2,0,1:T(8,128)(2,1)}), bf16[32768,2,128]{2,0,1:T(8,128)(2,1)}) %all-gather.5.cloned.1.call-update) | async-done | bytes 16777232 | tf_op jit(solution)/shard_map/all_gather | solution.py:78
  261.8 14.1 %copy.135 = bf16[256,128,2,128]{3,1,2,0:T(8,128)(2,1)} copy(bf16[256,128,2,128]{3,1,0,2:T(8,128)(2,1)} %bitcast.107) | data formatting | bytes 33554432 | tf_op jit(solution)/shard_map/reshape | solution.py:87
  275.9 8.8 %gather_fusion.1 = bf16[64,128,2,128]{3,1,2,0:T(8,128)(2,1)} fusion(bf16[256,128,2,128]{3,1,2,0:T(8,128)(2,1)} %copy.128, s32[1024]{0:T(1024)S(1)} %pad_clamp_fusion), kind=kCustom, calls=%fused_computation.clone | custom fusion | bytes 8388864 | tf_op jit(solution)/shard_map/jit(_take)/gather | solution.py:83
  284.7 8.8 %gather_fusion.2 = bf16[64,128,2,128]{3,1,2,0:T(8,128)(2,1)} fusion(bf16[256,128,2,128]{3,1,2,0:T(8,128)(2,1)} %copy.135, s32[1024]{0:T(1024)S(1)} %pad_clamp_fusion), kind=kCustom, calls=%fused_computation.1.clone | custom fusion | bytes 8388864 | tf_op jit(solution)/shard_map/jit(_take)/gather | solution.py:86
  293.6 4.1 broadcast_select_fusion
  297.7 4.6 pad_maximum_fusion
  312.5 96.4 %while.20 = (s32[]{:T(128)}, bf16[4,512,128]{2,1,0:T(8,128)(2,1)}, s32[4]{0:T(128)S(1)}, pred[16,80]{1,0:T(8,128)(4,1)S(1)}, bf16[2048,128]{1,0:T(8,128)(2,1)}, ...) while((s32[]{:T(128)}, bf16[4,512,128]{2,1,0:T(8,128)(2,1)}, ...), condition=%wide.region_8.10_spmd, body=%wide.region_5.9_spmd.sunk | while | flops 2721184768 | bytes 78917296 | solution.py:131
  318.4 9.5 %fusion.79 = (f32[512]{0:T(512)S(1)}, f32[512,10240]{1,0:T(8,128)S(1)}) fusion(bf16[10240,128]{1,0:T(8,128)(2,1)} %get-tuple-element.425, bf16[2048,128]{1,0:T(8,128)(2,1)} %get-tuple-element.424, s32[]{:T(128)S(6)} %select_n.87, pred[64,8,80,128]{3,2,1,0:T(8,128)(4,1)} %bitcast.102), kind=kOutput, calls=%fused_computation.100.clone.1 | convolution fusion | flops 1357905408 | bytes 28968964 | tf_op jit(solution)/shard_map/while/body/eval_jaxpr/qd,kd->qk/dot_general | solution.py:117
  331.5 5.4 fusion.81
  342.4 9.5 %fusion.79 = (f32[512]{0:T(512)S(1)}, f32[512,10240]{1,0:T(8,128)S(1)}) fusion(bf16[10240,128]{1,0:T(8,128)(2,1)} %get-tuple-element.425, bf16[2048,128]{1,0:T(8,128)(2,1)} %get-tuple-element.424, s32[]{:T(128)S(6)} %select_n.87, pred[64,8,80,128]{3,2,1,0:T(8,128)(4,1)} %bitcast.102), kind=kOutput, calls=%fused_computation.100.clone.1 | convolution fusion | flops 1357905408 | bytes 28968964 | tf_op jit(solution)/shard_map/while/body/eval_jaxpr/qd,kd->qk/dot_general | solution.py:117
  355.4 5.4 fusion.81
  366.4 9.5 %fusion.79 = (f32[512]{0:T(512)S(1)}, f32[512,10240]{1,0:T(8,128)S(1)}) fusion(bf16[10240,128]{1,0:T(8,128)(2,1)} %get-tuple-element.425, bf16[2048,128]{1,0:T(8,128)(2,1)} %get-tuple-element.424, s32[]{:T(128)S(6)} %select_n.87, pred[64,8,80,128]{3,2,1,0:T(8,128)(4,1)} %bitcast.102), kind=kOutput, calls=%fused_computation.100.clone.1 | convolution fusion | flops 1357905408 | bytes 28968964 | tf_op jit(solution)/shard_map/while/body/eval_jaxpr/qd,kd->qk/dot_general | solution.py:117
  379.4 5.4 fusion.81
  390.4 9.5 %fusion.79 = (f32[512]{0:T(512)S(1)}, f32[512,10240]{1,0:T(8,128)S(1)}) fusion(bf16[10240,128]{1,0:T(8,128)(2,1)} %get-tuple-element.425, bf16[2048,128]{1,0:T(8,128)(2,1)} %get-tuple-element.424, s32[]{:T(128)S(6)} %select_n.87, pred[64,8,80,128]{3,2,1,0:T(8,128)(4,1)} %bitcast.102), kind=kOutput, calls=%fused_computation.100.clone.1 | convolution fusion | flops 1357905408 | bytes 28968964 | tf_op jit(solution)/shard_map/while/body/eval_jaxpr/qd,kd->qk/dot_general | solution.py:117
  403.4 5.4 fusion.81
  409.7 96.1 %while.21 = (s32[]{:T(128)}, bf16[4,512,128]{2,1,0:T(8,128)(2,1)}, s32[4]{0:T(128)S(1)}, pred[16,80]{1,0:T(8,128)(4,1)S(1)}, bf16[2048,128]{1,0:T(8,128)(2,1)}, ...) while((s32[]{:T(128)}, bf16[4,512,128]{2,1,0:T(8,128)(2,1)}, ...), condition=%wide.region_12.14_spmd, body=%wide.region_9.13_spmd.sunk | while | flops 2721184768 | bytes 78917296 | solution.py:131
  415.3 9.5 %fusion.85 = (f32[512]{0:T(512)S(1)}, f32[512,10240]{1,0:T(8,128)S(1)}) fusion(bf16[10240,128]{1,0:T(8,128)(2,1)} %get-tuple-element.386, bf16[2048,128]{1,0:T(8,128)(2,1)} %get-tuple-element.385, s32[]{:T(128)S(6)} %select_n.89, pred[64,8,80,128]{3,2,1,0:T(8,128)(4,1)} %bitcast.103), kind=kOutput, calls=%fused_computation.101.clone.1 | convolution fusion | flops 1357905408 | bytes 28968964 | tf_op jit(solution)/shard_map/while/body/eval_jaxpr/qd,kd->qk/dot_general | solution.py:117
  428.4 5.5 fusion.87
  439.3 9.5 %fusion.85 = (f32[512]{0:T(512)S(1)}, f32[512,10240]{1,0:T(8,128)S(1)}) fusion(bf16[10240,128]{1,0:T(8,128)(2,1)} %get-tuple-element.386, bf16[2048,128]{1,0:T(8,128)(2,1)} %get-tuple-element.385, s32[]{:T(128)S(6)} %select_n.89, pred[64,8,80,128]{3,2,1,0:T(8,128)(4,1)} %bitcast.103), kind=kOutput, calls=%fused_computation.101.clone.1 | convolution fusion | flops 1357905408 | bytes 28968964 | tf_op jit(solution)/shard_map/while/body/eval_jaxpr/qd,kd->qk/dot_general | solution.py:117
  452.3 5.5 fusion.87
  463.3 9.5 %fusion.85 = (f32[512]{0:T(512)S(1)}, f32[512,10240]{1,0:T(8,128)S(1)}) fusion(bf16[10240,128]{1,0:T(8,128)(2,1)} %get-tuple-element.386, bf16[2048,128]{1,0:T(8,128)(2,1)} %get-tuple-element.385, s32[]{:T(128)S(6)} %select_n.89, pred[64,8,80,128]{3,2,1,0:T(8,128)(4,1)} %bitcast.103), kind=kOutput, calls=%fused_computation.101.clone.1 | convolution fusion | flops 1357905408 | bytes 28968964 | tf_op jit(solution)/shard_map/while/body/eval_jaxpr/qd,kd->qk/dot_general | solution.py:117
  476.3 5.5 fusion.87
  487.2 9.5 %fusion.85 = (f32[512]{0:T(512)S(1)}, f32[512,10240]{1,0:T(8,128)S(1)}) fusion(bf16[10240,128]{1,0:T(8,128)(2,1)} %get-tuple-element.386, bf16[2048,128]{1,0:T(8,128)(2,1)} %get-tuple-element.385, s32[]{:T(128)S(6)} %select_n.89, pred[64,8,80,128]{3,2,1,0:T(8,128)(4,1)} %bitcast.103), kind=kOutput, calls=%fused_computation.101.clone.1 | convolution fusion | flops 1357905408 | bytes 28968964 | tf_op jit(solution)/shard_map/while/body/eval_jaxpr/qd,kd->qk/dot_general | solution.py:117
  500.3 5.5 fusion.87
  507.1 8.9 %copy.140 = bf16[2048,2,128]{2,1,0:T(2,128)(2,1)S(1)} copy(bf16[2048,2,128]{2,0,1:T(8,128)(2,1)S(1)} %pad_maximum_fusion.2) | data formatting | bytes 2097152 | tf_op jit(solution)/shard_map/stack | solution.py:133
  515.9 20.3 %all_to_all.71 = bf16[2048,2,128]{2,1,0:T(2,128)(2,1)S(1)} all-to-all(bf16[2048,2,128]{2,1,0:T(2,128)(2,1)S(1)} %copy.140), channel_id=1, replica_groups=mesh['wide'=16,'narrow'=8] {'narrow'}, dimensions={0} | all-to-all | bytes 2097152 | tf_op jit(solution)/shard_map/all_to_all | solution.py:134
  (119 shorter events, 101.4 us)
Async XLA Ops:
  6.5 142.2 %all-gather.3.cloned.1.call-start = ((), (), s32[]{:S(2)}) async-start(), calls=%async_computation.4 | async-start | bytes 17825792 | tf_op jit(solution)/shard_map/all_gather | solution.py:77
  6.6 3.4 copy-start.4
  12.8 25.1 %copy-start.2 = (bf16[256,2048]{1,0:T(8,128)(2,1)S(1)}, bf16[256,2048]{1,0:T(8,128)(2,1)}, u32[]{:S(2)}) copy-start(bf16[256,2048]{1,0:T(8,128)(2,1)} %param.14) | copy-start | bytes 3145732
  37.8 24.4 %copy-start.3 = (s32[256,24]{0,1:T(8,128)S(1)}, s32[256,24]{0,1:T(8,128)}, u32[]{:S(2)}) copy-start(s32[256,24]{0,1:T(8,128)} %param.16) | copy-start | bytes 73732
  37.8 24.5 %copy-start.5 = (s32[256]{0:T(256)S(1)}, s32[256]{0:T(256)}, u32[]{:S(2)}) copy-start(s32[256]{0:T(256)} %param.17) | copy-start | bytes 3076
  37.9 224.0 %all-gather.5.cloned.1.call-start = ((), (), s32[]{:S(2)}) async-start(), calls=%async_computation.5 | async-start | bytes 17825792 | tf_op jit(solution)/shard_map/all_gather | solution.py:78
  58.3 19.8 %all-to-all-start = ((bf16[256,16,128]{0,2,1:T(8,128)(2,1)}), bf16[256,16,128]{0,2,1:T(8,128)(2,1)S(1)}, u32[]{:S(2)}, u32[]{:S(2)}) async-start(bf16[256,16,128]{0,2,1:T(8,128)(2,1)} %get-tuple-element.235), calls=%async_computation | async-start | bytes 2097152 | tf_op jit(solution)/shard_map/all_to_all | solution.py:51
  293.6 4.1 copy-start
  293.6 4.1 copy-start.1
Sparse Core Ops, SparseCore 0:
  38.0 110.6 all-gather.2
  150.9 110.8 all-gather.4
where the time goes:
time: 550 us; the launch traced here: 545 us
  waiting for transfers between devices  173 us (31%)
  matrix products  120 us (22%)
  local copies, waits for them, and re-layouts  113 us (21%)
  blocking collectives  60.1 us (11%)
  other arithmetic  51.7 us (9%)
  between operations  13.9 us (3%)
  loops' own time  9.92 us (2%)
    all_gather x1, waiting for transfers between devices, shards(): lax.all_gather(v_frame, 'wide', axis=0, tiled=True)  98.9 us
    dot_general x8, matrix products, attend(): jnp.einsum('qd,kd->qk', query_now, key_head, preferred_element_type=jnp.f...  76.3 us
    all_gather x1, waiting for transfers between devices, shards(): lax.all_gather(k_frame, 'wide', axis=0, tiled=True)  68.9 us
    dot_general x8, matrix products, attend(): mixed = jnp.dot(weights_low, value_head, preferred_element_type=jnp.float32)  43.6 us
    broadcast_in_dim x8, local copies, waits for them, and re-layouts, attend(): scores = jnp.where(allowed_now[:, None, :, None], scores, -jnp.inf)  29.8 us
    reduce_sum x8, other arithmetic, attend(): row_total = jnp.sum(weights, axis=-1)  28.1 us
    all_to_all x1, blocking collectives, shards(): lax.all_to_all(k_local, 'narrow', split_axis=1, concat_axis=0, tiled=True)  21.3 us
    all_to_all x1, blocking collectives, shards(): lax.all_to_all(attended_frame, 'narrow', split_axis=0, concat_axis=1, til...  20.3 us
  transfers between devices with their start and end apart: 3, of which 3 were waited for; matrix products, arithmetic and copies ran while one was open for 5% of the time, Pallas kernels for 0%

commit v1 on v0

v1 whole, which is shorter than its diff:
```python
import functools
import math

import jax
import jax.numpy as jnp
import numpy as np
from jax import lax
from jax.experimental import pallas as pl
from jax.experimental.pallas import tpu as pltpu
from jax.sharding import PartitionSpec as P

HEADS = 16
HD = 128
BLOCK = 128
KMAX = 24
MIN_LISTED = 6
F32 = jnp.float32
BF16 = jnp.bfloat16
TO_EXP2 = HD**-0.5 * math.log2(math.e)
SECTIONS = ((0, 32), (32, 80), (80, 128))
ROWS_BY_COLS = (((1,), (0,)), ((), ()))
ROWS_BY_ROWS = (((1,), (1,)), ((), ()))


def pair_matrix():
    pairs = np.zeros((HD, HD), np.float32)
    for begin, end in SECTIONS:
        half = (end - begin) // 2
        for j in range(half):
            pairs[begin + half + j, begin + j] = -1.0
            pairs[begin + j, begin + half + j] = 1.0
    return pairs


def lane_frequencies():
    pieces = []
    for begin, end in SECTIONS:
        section = end - begin
        half = section // 2
        inverse = 10000.0 ** (-2.0 * jnp.arange(half, dtype=F32) / section)
        pieces += [inverse, inverse]
    return jnp.concatenate(pieces)


def rope_kernel(pos_ref, freq_ref, pairs_ref, x_ref, out_ref):
    angles = lax.dot_general(
        pos_ref[...].astype(F32),
        freq_ref[...],
        (((0,), (0,)), ((), ())),
        precision=lax.Precision.HIGHEST,
        preferred_element_type=F32,
    )
    cosine = jnp.cos(angles)
    sine = jnp.sin(angles)
    for head in range(HEADS):
        x = x_ref[:, head * HD : (head + 1) * HD]
        partner = lax.dot_general(x, pairs_ref[...], ROWS_BY_COLS, preferred_element_type=F32)
        out_ref[head] = (x.astype(F32) * cosine + partner * sine).astype(BF16)


def rope(x, positions, freqs, pairs):
    rows = x.shape[0]
    return pl.pallas_call(
        rope_kernel,
        out_shape=jax.ShapeDtypeStruct((HEADS, rows, HD), BF16),
        compiler_params=pltpu.CompilerParams(vmem_limit_bytes=24 * 2**20),
        name="rope",
    )(positions, freqs, pairs, x)


def attend_kernel(
    lists_ref, counts_ref, q_ref, k_hbm, v_hbm, out_ref, k_ref, v_ref, s_ref, m_ref, sems
):
    blocks = q_ref.shape[0]
    pair_count = KMAX // 2
    k_copy = pltpu.make_async_copy(k_hbm, k_ref, sems.at[0])
    v_copy = pltpu.make_async_copy(v_hbm, v_ref, sems.at[1])
    k_copy.start()
    v_copy.start()
    k_copy.wait()
    v_copy.wait()

    def pair_of(ref, row, pair):
        at = row * KMAX + 2 * pair
        return jnp.concatenate([ref[lists_ref[at]], ref[lists_ref[at + 1]]], axis=0)

    def step(row, carry):
        query = q_ref[row]
        largest = None
        for pair in range(pair_count):
            scores = lax.dot_general(
                query, pair_of(k_ref, row, pair), ROWS_BY_ROWS, preferred_element_type=F32
            )
            s_ref[pair] = scores
            for half in range(2):
                part = scores[:, half * BLOCK : (half + 1) * BLOCK]
                largest = part if largest is None else jnp.maximum(largest, part)
        shift = jnp.broadcast_to(
            jnp.max(largest, axis=1, keepdims=True) * TO_EXP2, (BLOCK, BLOCK)
        )
        count = counts_ref[row]
        total = None
        mixed = None
        for pair in range(pair_count):
            weights = []
            for half in range(2):
                entry = 2 * pair + half
                shift_here = shift
                if entry >= MIN_LISTED:
                    shift_here = shift + jnp.where(entry < count, 0.0, 1e30)
                part = jnp.exp2(
                    s_ref[pair, :, half * BLOCK : (half + 1) * BLOCK] * TO_EXP2 - shift_here
                )
                total = part if total is None else total + part
                weights.append(part.astype(BF16))
            product = lax.dot_general(
                jnp.concatenate(weights, axis=1),
                pair_of(v_ref, row, pair),
                ROWS_BY_COLS,
                preferred_element_type=F32,
            )
            mixed = product if mixed is None else mixed + product
        out_ref[row] = (mixed / jnp.sum(total, axis=1, keepdims=True)).astype(BF16)
        return carry

    lax.fori_loop(0, blocks, step, 0)


def attend(lists, counts, q, k, v):
    blocks = q.shape[0]
    all_blocks = k.shape[0]
    whole = pl.BlockSpec((blocks, BLOCK, HD), lambda g, *_: (0, 0, 0))
    anywhere = pl.BlockSpec(memory_space=pl.ANY)
    return pl.pallas_call(
        attend_kernel,
        grid_spec=pltpu.PrefetchScalarGridSpec(
            num_scalar_prefetch=2,
            grid=(1,),
            in_specs=[whole, anywhere, anywhere],
            out_specs=whole,
            scratch_shapes=[
                pltpu.VMEM((all_blocks, BLOCK, HD), BF16),
                pltpu.VMEM((all_blocks, BLOCK, HD), BF16),
                pltpu.VMEM((KMAX // 2, BLOCK, 2 * BLOCK), F32),
                pltpu.VMEM((8, BLOCK), F32),
                pltpu.SemaphoreType.DMA((2,)),
            ],
        ),
        out_shape=jax.ShapeDtypeStruct((blocks, BLOCK, HD), BF16),
        compiler_params=pltpu.CompilerParams(vmem_limit_bytes=48 * 2**20),
        name="attend",
    )(lists, counts, q, k, v)


def shards(query_proj, key_proj, value_proj, positions, key_lists, key_counts):
    frames = lax.axis_size("wide")
    parts = lax.axis_size("narrow")
    part = lax.axis_index("narrow")
    rows = query_proj.shape[0]
    halves = rows // BLOCK
    frame_blocks = parts * halves

    lane = np.arange(HD)
    axis_of = np.searchsorted([32, 80], lane, side="right")
    freqs = jnp.where(
        jnp.asarray(axis_of[None, :] == np.arange(3)[:, None]), lane_frequencies()[None, :], 0.0
    )
    pairs = jnp.asarray(pair_matrix(), BF16)

    def heads_out(x):
        return lax.all_to_all(x, "wide", split_axis=0, concat_axis=0, tiled=True)

    def all_parts(x):
        return lax.all_gather(x, "narrow", axis=0).reshape(
            parts * frames * halves, BLOCK, HD
        )

    k_all = all_parts(heads_out(rope(key_proj, positions, freqs, pairs)))
    v_heads = value_proj.reshape(rows, HEADS, HD).transpose(1, 0, 2)
    v_all = all_parts(heads_out(v_heads))
    q = heads_out(rope(query_proj, positions, freqs, pairs)).reshape(frames * halves, BLOCK, HD)

    frame = key_lists // frame_blocks
    inner = key_lists % frame_blocks
    places = (inner // halves) * (frames * halves) + frame * halves + inner % halves
    mine = lax.dynamic_index_in_dim(
        places.reshape(frames, parts, halves * KMAX), part, 1, keepdims=False
    ).reshape(-1)
    counts = lax.dynamic_index_in_dim(
        key_counts.reshape(frames, parts, halves), part, 1, keepdims=False
    ).reshape(-1)

    mixed = attend(mine, counts, q, k_all, v_all).reshape(frames, rows, HD)
    back = heads_out(mixed)
    return back.transpose(1, 0, 2).reshape(rows, HEADS * HD)


def solution(mesh):
    return jax.shard_map(
        shards,
        mesh=mesh,
        in_specs=(
            P(("wide", "narrow"), None),
            P(("wide", "narrow"), None),
            P(("wide", "narrow"), None),
            P(None, ("wide", "narrow")),
            P(),
            P(),
        ),
        out_specs=P(("wide", "narrow"), None),
        check_vma=False,
    )
```

time: 550 us -> 207 us (0.38)
  matrix products: 120 us -> 0 us
  local copies, waits for them, and re-layouts: 113 us -> 7.22 us
  waiting for transfers between devices: 173 us -> 72 us
  other arithmetic: 51.7 us -> 0.74 us
  Pallas kernels: 0 us -> 41.6 us
  loops' own time: 9.92 us -> 0 us
  blocking collectives: 60.1 us -> 67.6 us
    dot_general x16 -> x0, matrix products: 120 us -> none  [the longest x8 76.3 us: attend(): jnp.einsum('qd,kd->qk', query_now, key_head, preferred_element_type=jnp.f...]
    all_gather x2, waiting for transfers between devices: 168 us -> 57.5 us  [all_parts(): lax.all_gather(x, 'narrow', axis=0)]
    pallas_call x0 -> x3, Pallas kernels: none -> 41.6 us  [the longest x1 38.1 us: attend(): pl.pallas_call(attend_kernel, grid_spec=pltpu.PrefetchScalarGridSpec(num_...]
    broadcast_in_dim x8 -> x0, local copies, waits for them, and re-layouts: 29.8 us -> none  [attend(): scores = jnp.where(allowed_now[:, None, :, None], scores, -jnp.inf)]
    reduce_sum x9 -> x0, other arithmetic: 29.2 us -> none  [the longest x8 28.1 us: attend(): row_total = jnp.sum(weights, axis=-1)]
    reshape x4 -> x5, local copies, waits for them, and re-layouts: 30.6 us -> 1.5 us  [the longest x1 1.13 us: shards(): return back.transpose(1, 0, 2).reshape(rows, HEADS * HD)]
    gather x3 -> x0, local copies, waits for them, and re-layouts: 18.3 us -> none  [the longest x1 8.82 us: shards(): jnp.take(all_v.reshape(wide_size * frame_blocks, BLOCK, local_heads, HD),...]
    another operation x3 -> x0, local copies, waits for them, and re-layouts: 10.6 us -> none  [the longest x1 8.89 us: shards(): attended_frame = jnp.stack(outputs, axis=1)]
  transfers between devices with their start and end apart: 3 -> 3, of which waited for: 3 -> 3; matrix products, arithmetic and copies ran while one was open for 5% -> 2% of each run, Pallas kernels for 0% -> 1%
where the time goes in v1:
time: 207 us; the launch traced here: 206 us
  waiting for transfers between devices  72 us (35%)
  blocking collectives  67.6 us (33%)
  Pallas kernels  41.6 us (20%)
  between operations  13.5 us (7%)
  local copies, waits for them, and re-layouts  7.22 us (3%)
  starting transfers between devices  3.7 us (2%)
    all_to_all x3, blocking collectives, heads_out(): return lax.all_to_all(x, 'wide', split_axis=0, concat_axis=0, tiled=True)  67.6 us
    all_gather x2, waiting for transfers between devices, all_parts(): lax.all_gather(x, 'narrow', axis=0)  57.5 us
    pallas_call x1, Pallas kernels, attend(): pl.pallas_call(attend_kernel, grid_spec=pltpu.PrefetchScalarGridSpec(num_...  38.1 us
    all_to_all x1, waiting for transfers between devices, heads_out(): return lax.all_to_all(x, 'wide', split_axis=0, concat_axis=0, tiled=True)  14.5 us
    unnamed x17, local copies, waits for them, and re-layouts  4.17 us
  transfers between devices with their start and end apart: 3, of which 3 were waited for; matrix products, arithmetic and copies ran while one was open for 2% of the time, Pallas kernels for 1%

profile of v1, /device:TPU:0, one launch (start us, length us, event | category | flops | bytes accessed | tf_op | source)
XLA Modules:
  0.0 206.4 jit_solution(18147958729457761238)
XLA Ops:
  6.5 0.0 all-gather.5.cloned.1.call-start
  6.6 0.1 concatenate.3
  6.6 0.7 broadcast_select_fusion.freq_ref
  7.3 1.2 copy-done
  8.5 0.8 copy-done.2
  9.3 0.7 copy-done.4
  10.0 1.3 rope.3
  11.3 23.9 %all_to_all.20 = bf16[16,256,128]{2,1,0:T(8,128)(2,1)} all-to-all(bf16[16,256,128]{2,1,0:T(8,128)(2,1)S(1)} %rope.3), channel_id=1, replica_groups=mesh['wide'=16,'narrow'=8] {'wide'}, dimensions={0} | all-to-all | bytes 2097152 | tf_op jit(solution)/shard_map/all_to_all | solution.py:171
  35.1 0.0 all-gather.5.cloned.1.call-update
  35.2 0.0 all-gather.7.cloned.1.call-start
  35.2 1.5 copy.17
  36.7 19.6 %all_to_all.21 = bf16[16,256,128]{1,2,0:T(8,128)(2,1)S(1)} all-to-all(bf16[16,256,128]{1,2,0:T(8,128)(2,1)S(1)} %bitcast.17), channel_id=1, replica_groups=mesh['wide'=16,'narrow'=8] {'wide'}, dimensions={0} | all-to-all | bytes 2097152 | tf_op jit(solution)/shard_map/all_to_all | solution.py:171
  56.3 1.3 copy.18
  57.6 0.0 all-gather.7.cloned.1.call-update
  57.6 0.0 copy-done.5
  57.6 0.0 copy-done.1
  57.6 0.0 copy-done.3
  57.6 2.2 %rope.2 = bf16[16,256,128]{2,1,0:T(8,128)(2,1)} custom-call(s32[3,256]{1,0:T(4,128)S(1)} %copy-done.5, f32[3,128]{1,0:T(4,128)S(1)} %broadcast_select_fusion.freq_ref, bf16[128,128]{1,0:T(8,128)(2,1)S(1)} %copy-done.3, bf16[256,2048]{1,0:T(8,128)(2,1)S(1)} %copy-done.1), custom_call_target="tpu_custom_call" | custom-call | tf_op jit(solution)/shard_map/rope/pallas_call | solution.py:63
  59.8 3.7 %all-to-all-start = ((bf16[16,256,128]{2,1,0:T(8,128)(2,1)}), bf16[16,256,128]{2,1,0:T(8,128)(2,1)S(1)}, u32[]{:S(2)}, u32[]{:S(2)}) async-start(bf16[16,256,128]{2,1,0:T(8,128)(2,1)} %rope.2), calls=%async_computation | async-start | bytes 2097152 | tf_op jit(solution)/shard_map/all_to_all | solution.py:171
  63.5 0.0 copy-done.7
  63.5 0.1 reshape.35
  63.7 0.1 reshape.36.counts_ref
  63.8 0.1 fusion.2
  63.9 0.1 copy.16
  64.0 0.1 reshape.33
  64.1 0.1 reshape.34.lists_ref
  64.2 14.5 %all-to-all-done = bf16[16,256,128]{2,1,0:T(8,128)(2,1)S(1)} async-done(((bf16[16,256,128]{2,1,0:T(8,128)(2,1)}), bf16[16,256,128]{2,1,0:T(8,128)(2,1)S(1)}, u32[]{:S(2)}, u32[]{:S(2)}) %all-to-all-start) | async-done | bytes 1048608 | tf_op jit(solution)/shard_map/all_to_all | solution.py:171
  78.6 5.8 %all-gather.5.cloned.1.call-done = bf16[128,256,128]{2,1,0:T(8,128)(2,1)} async-done(((bf16[16,256,128]{2,1,0:T(8,128)(2,1)}), bf16[128,256,128]{2,1,0:T(8,128)(2,1)}) %all-gather.5.cloned.1.call-update) | async-done | bytes 8388624 | tf_op jit(solution)/shard_map/all_gather | solution.py:174
  84.4 51.7 %all-gather.7.cloned.1.call-done = bf16[128,256,128]{2,1,0:T(8,128)(2,1)} async-done(((bf16[16,256,128]{2,1,0:T(8,128)(2,1)}), bf16[128,256,128]{2,1,0:T(8,128)(2,1)}) %all-gather.7.cloned.1.call-update) | async-done | bytes 8388624 | tf_op jit(solution)/shard_map/all_gather | solution.py:174
  136.2 38.1 %attend.1 = bf16[32,128,128]{2,1,0:T(8,128)(2,1)S(1)} custom-call(s32[768]{0:T(1024)S(1)} %reshape.34.lists_ref, s32[32]{0:T(128)S(1)} %reshape.36.counts_ref, bf16[32,128,128]{2,1,0:T(8,128)(2,1)S(1)} %bitcast.13, bf16[256,128,128]{2,1,0:T(8,128)(2,1)} %bitcast.15, bf16[256,128,128]{2,1,0:T(8,128)(2,1)} %bitcast.16), custom_call_target="tpu_custom_call" | custom-call | tf_op jit(solution)/shard_map/attend/pallas_call | solution.py:134
  174.3 24.1 %all_to_all.22 = bf16[16,256,128]{2,1,0:T(8,128)(2,1)S(1)} all-to-all(bf16[16,256,128]{2,1,0:T(8,128)(2,1)S(1)} %bitcast.14), channel_id=1, replica_groups=mesh['wide'=16,'narrow'=8] {'wide'}, dimensions={0} | all-to-all | bytes 2097152 | tf_op jit(solution)/shard_map/all_to_all | solution.py:171
  198.4 1.1 copy_bitcast_fusion
  (13 shorter events, 0.1 us)
Async XLA Ops:
  6.5 51.1 %copy-start.5 = (s32[3,256]{1,0:T(4,128)S(1)}, s32[3,256]{1,0:T(4,128)}, u32[]{:S(2)}) copy-start(s32[3,256]{1,0:T(4,128)} %pos_ref.3) | copy-start | bytes 9220
  6.5 77.9 %all-gather.5.cloned.1.call-start = ((), (), s32[]{:S(2)}) async-start(), calls=%async_computation.4 | async-start | bytes 9437184 | tf_op jit(solution)/shard_map/all_gather | solution.py:174
  7.3 1.2 copy-start
  8.5 0.8 copy-start.2
  9.3 0.7 copy-start.4
  10.0 47.6 %copy-start.1 = (bf16[256,2048]{1,0:T(8,128)(2,1)S(1)}, bf16[256,2048]{1,0:T(8,128)(2,1)}, u32[]{:S(2)}) copy-start(bf16[256,2048]{1,0:T(8,128)(2,1)} %x_ref.2) | copy-start | bytes 3145732
  10.0 47.6 %copy-start.3 = (bf16[128,128]{1,0:T(8,128)(2,1)S(1)}, bf16[128,128]{1,0:T(8,128)(2,1)}, u32[]{:S(2)}) copy-start(bf16[128,128]{1,0:T(8,128)(2,1)} %constant.82.clone.pairs_ref) | copy-start | bytes 98308
  10.0 53.5 %copy-start.7 = (s32[256]{0:T(256)S(1)}, s32[256]{0:T(256)}, u32[]{:S(2)}) copy-start(s32[256]{0:T(256)} %param.13) | copy-start | bytes 3076
  10.0 53.8 %copy-start.6 = (s32[256,24]{0,1:T(8,128)S(1)}, s32[256,24]{0,1:T(8,128)}, u32[]{:S(2)}) copy-start(s32[256,24]{0,1:T(8,128)} %param.12) | copy-start | bytes 73732
  35.2 101.0 %all-gather.7.cloned.1.call-start = ((), (), s32[]{:S(2)}) async-start(), calls=%async_computation.5 | async-start | bytes 9437184 | tf_op jit(solution)/shard_map/all_gather | solution.py:174
  59.8 18.8 %all-to-all-start = ((bf16[16,256,128]{2,1,0:T(8,128)(2,1)}), bf16[16,256,128]{2,1,0:T(8,128)(2,1)S(1)}, u32[]{:S(2)}, u32[]{:S(2)}) async-start(bf16[16,256,128]{2,1,0:T(8,128)(2,1)} %rope.2), calls=%async_computation | async-start | bytes 2097152 | tf_op jit(solution)/shard_map/all_to_all | solution.py:171
Sparse Core Ops, SparseCore 0:
  35.3 49.1 all-gather.4
  86.2 49.9 all-gather.6

commit v2 on v1

v2 whole, which is shorter than its diff:
```python
import functools
import math

import jax
import jax.numpy as jnp
import numpy as np
from jax import lax
from jax.experimental import pallas as pl
from jax.experimental.pallas import tpu as pltpu
from jax.sharding import PartitionSpec as P

HEADS = 16
HD = 128
BLOCK = 128
KMAX = 24
MIN_LISTED = 6
F32 = jnp.float32
BF16 = jnp.bfloat16
TO_EXP2 = HD**-0.5 * math.log2(math.e)
SECTIONS = ((0, 32), (32, 80), (80, 128))
ROWS_BY_COLS = (((1,), (0,)), ((), ()))
ROWS_BY_ROWS = (((1,), (1,)), ((), ()))


def pair_matrix():
    pairs = np.zeros((HD, HD), np.float32)
    for begin, end in SECTIONS:
        half = (end - begin) // 2
        for j in range(half):
            pairs[begin + half + j, begin + j] = -1.0
            pairs[begin + j, begin + half + j] = 1.0
    return pairs


def lane_frequencies():
    pieces = []
    for begin, end in SECTIONS:
        section = end - begin
        half = section // 2
        inverse = 10000.0 ** (-2.0 * jnp.arange(half, dtype=F32) / section)
        pieces += [inverse, inverse]
    return jnp.concatenate(pieces)


def rope_kernel(pos_ref, freq_ref, pairs_ref, x_ref, out_ref):
    angles = lax.dot_general(
        pos_ref[...].astype(F32),
        freq_ref[...],
        (((0,), (0,)), ((), ())),
        precision=lax.Precision.HIGHEST,
        preferred_element_type=F32,
    )
    cosine = jnp.cos(angles)
    sine = jnp.sin(angles)
    for head in range(HEADS):
        x = x_ref[:, head * HD : (head + 1) * HD]
        partner = lax.dot_general(x, pairs_ref[...], ROWS_BY_COLS, preferred_element_type=F32)
        out_ref[head] = (x.astype(F32) * cosine + partner * sine).astype(BF16)


def rope(x, positions, freqs, pairs):
    rows = x.shape[0]
    return pl.pallas_call(
        rope_kernel,
        out_shape=jax.ShapeDtypeStruct((HEADS, rows, HD), BF16),
        compiler_params=pltpu.CompilerParams(vmem_limit_bytes=24 * 2**20),
        name="rope",
    )(positions, freqs, pairs, x)


def load_blocks(sources, target, sems):
    copies = []
    at = 0
    for n, source in enumerate(sources):
        blocks = source.shape[0]
        copies.append(pltpu.make_async_copy(source, target.at[pl.ds(at, blocks)], sems.at[n]))
        at += blocks
    for copy in copies:
        copy.start()
    for copy in copies:
        copy.wait()


def listed_pair(ref, lists_ref, row, pair):
    at = row * KMAX + 2 * pair
    return jnp.concatenate([ref[lists_ref[at]], ref[lists_ref[at + 1]]], axis=0)


def weights_kernel(sources, unroll, lists_ref, counts_ref, q_ref, *refs):
    k_parts = refs[:sources]
    weights_ref, inverse_ref, k_ref, s_ref, sems = refs[sources:]
    load_blocks(k_parts, k_ref, sems)

    def row_weights(row, turn):
        query = q_ref[row]
        largest = None
        for pair in range(KMAX // 2):
            scores = lax.dot_general(
                query,
                listed_pair(k_ref, lists_ref, row, pair),
                ROWS_BY_ROWS,
                preferred_element_type=F32,
            )
            s_ref[turn, pair] = scores
            for half in range(2):
                part = scores[:, half * BLOCK : (half + 1) * BLOCK]
                largest = part if largest is None else jnp.maximum(largest, part)
        shift = jnp.broadcast_to(
            jnp.max(largest, axis=1, keepdims=True) * TO_EXP2, (BLOCK, BLOCK)
        )
        count = counts_ref[row]
        total = None
        for entry in range(KMAX):
            pair, half = divmod(entry, 2)
            shift_here = shift
            if entry >= MIN_LISTED:
                shift_here = shift + jnp.where(entry < count, 0.0, 1e30)
            lanes = slice(half * BLOCK, (half + 1) * BLOCK)
            part = jnp.exp2(s_ref[turn, pair, :, lanes] * TO_EXP2 - shift_here)
            total = part if total is None else total + part
            weights_ref[row, pair, :, lanes] = part.astype(BF16)
        inverse_ref[row] = jnp.broadcast_to(
            1.0 / jnp.sum(total, axis=1, keepdims=True), (BLOCK, BLOCK)
        )

    def step(turn, carry):
        for n in range(unroll):
            row_weights(turn * unroll + n, n)
        return carry

    lax.fori_loop(0, q_ref.shape[0] // unroll, step, 0)


SMEM_SPEC = pl.BlockSpec(memory_space=pltpu.SMEM)
VMEM_SPEC = pl.BlockSpec(memory_space=pltpu.VMEM)
ANY_SPEC = pl.BlockSpec(memory_space=pl.ANY)


def weights_of(lists, counts, q, k_parts, unroll=4):
    rows = q.shape[0]
    blocks = sum(part.shape[0] for part in k_parts)
    return pl.pallas_call(
        functools.partial(weights_kernel, len(k_parts), unroll),
        in_specs=[SMEM_SPEC, SMEM_SPEC, VMEM_SPEC] + [ANY_SPEC] * len(k_parts),
        out_specs=[VMEM_SPEC, VMEM_SPEC],
        scratch_shapes=[
            pltpu.VMEM((blocks, BLOCK, HD), BF16),
            pltpu.VMEM((unroll, KMAX // 2, BLOCK, 2 * BLOCK), F32),
            pltpu.SemaphoreType.DMA((len(k_parts),)),
        ],
        out_shape=[
            pltpu.VMEM((rows, KMAX // 2, BLOCK, 2 * BLOCK), BF16),
            pltpu.VMEM((rows, BLOCK, BLOCK), F32),
        ],
        compiler_params=pltpu.CompilerParams(vmem_limit_bytes=20 * 2**20),
        name="weights",
    )(lists, counts, q, *k_parts)


def mix_of(lists, halves, v_parts, unroll=8):
    rows = sum(weights.shape[0] for weights, _ in halves)
    blocks = sum(part.shape[0] for part in v_parts)

    def kernel(lists_ref, *refs):
        groups = [refs[2 * n : 2 * n + 2] for n in range(len(halves))]
        v_refs = refs[2 * len(halves) : 2 * len(halves) + len(v_parts)]
        out_ref, v_ref, sems = refs[2 * len(halves) + len(v_parts) :]
        load_blocks(v_refs, v_ref, sems)
        first = 0
        for weights_ref, inverse_ref in groups:

            def step(turn, carry, weights_ref=weights_ref, inverse_ref=inverse_ref, first=first):
                for n in range(unroll):
                    row = turn * unroll + n
                    mixed = None
                    for pair in range(KMAX // 2):
                        product = lax.dot_general(
                            weights_ref[row, pair],
                            listed_pair(v_ref, lists_ref, first + row, pair),
                            ROWS_BY_COLS,
                            preferred_element_type=F32,
                        )
                        mixed = product if mixed is None else mixed + product
                    out_ref[first + row] = (mixed * inverse_ref[row]).astype(BF16)
                return carry

            lax.fori_loop(0, weights_ref.shape[0] // unroll, step, 0)
            first += weights_ref.shape[0]

    return pl.pallas_call(
        kernel,
        in_specs=[SMEM_SPEC] + [VMEM_SPEC] * (2 * len(halves)) + [ANY_SPEC] * len(v_parts),
        out_specs=VMEM_SPEC,
        scratch_shapes=[
            pltpu.VMEM((blocks, BLOCK, HD), BF16),
            pltpu.SemaphoreType.DMA((len(v_parts),)),
        ],
        out_shape=jax.ShapeDtypeStruct((rows, BLOCK, HD), BF16),
        compiler_params=pltpu.CompilerParams(vmem_limit_bytes=14 * 2**20),
        name="mix",
    )(lists, *[ref for pair in halves for ref in pair], *v_parts)


def around(own):
    chips = lax.axis_size("narrow") // 2

    def along(x):
        steps = [(2 * z, 2 * ((z + 1) % chips)) for z in range(chips)]
        steps += [(2 * z + 1, 2 * ((z - 1) % chips) + 1) for z in range(chips)]
        return lax.ppermute(x, "narrow", steps)

    def across(x):
        return lax.ppermute(x, "narrow", [(n, n ^ 1) for n in range(2 * chips)])

    near_same = along(own)
    other = across(own)
    near_other = along(other)
    far_same = along(near_same)
    side_other = across(near_same)
    side_same = across(near_other)
    far_other = across(far_same)
    return [own, other, near_same, near_other, far_same, far_other, side_other, side_same]


def slots_of(source, part, chips):
    chip, core = part // 2, part % 2
    apart = (source // 2 - chip) % chips
    same = (source % 2) == core
    near = jnp.where(core == 0, chips - 1, 1)
    slot = jnp.where(same, 7, 6)
    slot = jnp.where(apart == near, jnp.where(same, 2, 3), slot)
    slot = jnp.where(apart == 2, jnp.where(same, 4, 5), slot)
    return jnp.where(apart == 0, jnp.where(same, 0, 1), slot)


def shards(query_proj, key_proj, value_proj, positions, key_lists, key_counts):
    frames = lax.axis_size("wide")
    parts = lax.axis_size("narrow")
    part = lax.axis_index("narrow")
    rows = query_proj.shape[0]
    halves = rows // BLOCK
    frame_blocks = parts * halves

    lane = np.arange(HD)
    axis_of = np.searchsorted([32, 80], lane, side="right")
    freqs = jnp.where(
        jnp.asarray(axis_of[None, :] == np.arange(3)[:, None]), lane_frequencies()[None, :], 0.0
    )
    pairs = jnp.asarray(pair_matrix(), BF16)

    def heads_out(x):
        return lax.all_to_all(x, "wide", split_axis=0, concat_axis=0, tiled=True)

    def blocks_of(x):
        return x.reshape(frames * halves, BLOCK, HD)

    k_heads = heads_out(rope(key_proj, positions, freqs, pairs))
    v_heads = heads_out(value_proj.reshape(rows, HEADS, HD).transpose(1, 0, 2))
    q_heads = heads_out(rope(query_proj, positions, freqs, pairs))
    k_parts = [blocks_of(x) for x in around(k_heads)]
    v_parts = [blocks_of(x) for x in around(v_heads)]
    q = blocks_of(q_heads)

    frame = key_lists // frame_blocks
    inner = key_lists % frame_blocks
    slot = slots_of(inner // halves, part, parts // 2)
    places = slot * (frames * halves) + frame * halves + inner % halves
    mine = lax.dynamic_index_in_dim(
        places.reshape(frames, parts, halves * KMAX), part, 1, keepdims=False
    ).reshape(-1)
    counts = lax.dynamic_index_in_dim(
        key_counts.reshape(frames, parts, halves), part, 1, keepdims=False
    ).reshape(-1)

    half = frames * halves // 2
    first = weights_of(mine[: half * KMAX], counts[:half], q[:half], k_parts)
    second = weights_of(mine[half * KMAX :], counts[half:], q[half:], k_parts)
    mixed = mix_of(mine, [first, second], v_parts).reshape(frames, rows, HD)
    back = heads_out(mixed)
    return back.transpose(1, 0, 2).reshape(rows, HEADS * HD)


def solution(mesh):
    return jax.shard_map(
        shards,
        mesh=mesh,
        in_specs=(
            P(("wide", "narrow"), None),
            P(("wide", "narrow"), None),
            P(("wide", "narrow"), None),
            P(None, ("wide", "narrow")),
            P(),
            P(),
        ),
        out_specs=P(("wide", "narrow"), None),
        check_vma=False,
    )
```

time: 207 us -> 191 us (0.923)
  blocking collectives: 67.6 us -> 21 us
  starting transfers between devices: 3.7 us -> 26.2 us
  local copies, waits for them, and re-layouts: 7.22 us -> 29 us
  between operations: 13.5 us -> 0.21 us
  Pallas kernels: 41.6 us -> 39.5 us
    all_gather x2 -> x0, waiting for transfers between devices: 57.5 us -> none  [all_parts(): lax.all_gather(x, 'narrow', axis=0)]
    all_to_all x3 -> x1, blocking collectives: 67.6 us -> 21 us  [heads_out(): return lax.all_to_all(x, 'wide', split_axis=0, concat_axis=0, tiled=True)]
    ppermute x0 -> x14, waiting for transfers between devices: none -> 44.5 us  [the longest x6 44.5 us: along(): return lax.ppermute(x, 'narrow', steps)]
    unnamed x17 -> x28, local copies, waits for them, and re-layouts: 4.17 us -> 24.5 us
    all_to_all x1 -> x3, waiting for transfers between devices: 14.5 us -> 29.5 us  [heads_out(): return lax.all_to_all(x, 'wide', split_axis=0, concat_axis=0, tiled=True)]
    all_to_all x1 -> x3, starting transfers between devices: 3.66 us -> 15.8 us  [heads_out(): return lax.all_to_all(x, 'wide', split_axis=0, concat_axis=0, tiled=True)]
    ppermute x0 -> x14, starting transfers between devices: none -> 10.3 us  [the longest x6 9.27 us: along(): return lax.ppermute(x, 'narrow', steps)]
    pallas_call x1 -> x3, Pallas kernels: 38.1 us -> 36 us  [the longest x2 24.7 us: weights_of(): pl.pallas_call(functools.partial(weights_kernel, len(k_parts), unroll), i...]
  transfers between devices with their start and end apart: 3 -> 17, of which waited for: 3 -> 7; matrix products, arithmetic and copies ran while one was open for 2% -> 2% of each run, Pallas kernels for 1% -> 14%
where the time goes in v2:
time: 191 us
  waiting for transfers between devices  74 us (39%)
  Pallas kernels  39.5 us (21%)
  local copies, waits for them, and re-layouts  29 us (15%)
  starting transfers between devices  26.2 us (14%)
  blocking collectives  21 us (11%)
    ppermute x6, waiting for transfers between devices, along(): return lax.ppermute(x, 'narrow', steps)  44.5 us
    all_to_all x3, waiting for transfers between devices, heads_out(): return lax.all_to_all(x, 'wide', split_axis=0, concat_axis=0, tiled=True)  29.5 us
    pallas_call x2, Pallas kernels, weights_of(): pl.pallas_call(functools.partial(weights_kernel, len(k_parts), unroll), i...  24.7 us
    unnamed x28, local copies, waits for them, and re-layouts  24.5 us
    all_to_all x1, blocking collectives, heads_out(): return lax.all_to_all(x, 'wide', split_axis=0, concat_axis=0, tiled=True)  21 us
    all_to_all x3, starting transfers between devices, heads_out(): return lax.all_to_all(x, 'wide', split_axis=0, concat_axis=0, tiled=True)  15.8 us
    pallas_call x1, Pallas kernels, mix_of(): pl.pallas_call(kernel, in_specs=[SMEM_SPEC] + [VMEM_SPEC] * (2 * len(halv...  11.2 us
    ppermute x6, starting transfers between devices, along(): return lax.ppermute(x, 'narrow', steps)  9.27 us
  transfers between devices with their start and end apart: 17, of which 7 were waited for; matrix products, arithmetic and copies ran while one was open for 2% of the time, Pallas kernels for 14%

profile of v2, /device:TPU:0, one launch (start us, length us, event | category | flops | bytes accessed | tf_op | source)
XLA Modules:
  0.0 190.7 jit_solution(3206561525407279506)
XLA Ops:
  0.8 1.2 copy-done.6
  2.1 0.8 copy-done.8
  3.5 2.2 %rope.3 = bf16[16,256,128]{2,1,0:T(8,128)(2,1)} custom-call(s32[3,256]{1,0:T(4,128)S(1)} %copy-done.10, f32[3,128]{1,0:T(4,128)S(1)} %broadcast_select_fusion.freq_ref, bf16[128,128]{1,0:T(8,128)(2,1)S(1)} %copy-done.8, bf16[256,2048]{1,0:T(8,128)(2,1)S(1)} %copy-done.6), custom_call_target="tpu_custom_call" | custom-call | tf_op jit(solution)/shard_map/rope/pallas_call | solution.py:63
  5.7 7.1 %all-to-all-start.1 = ((bf16[16,256,128]{2,1,0:T(8,128)(2,1)}), bf16[16,256,128]{2,1,0:T(8,128)(2,1)S(1)}, u32[]{:S(2)}, u32[]{:S(2)}) async-start(bf16[16,256,128]{2,1,0:T(8,128)(2,1)} %rope.3), calls=%async_computation.1 | async-start | bytes 2097152 | tf_op jit(solution)/shard_map/all_to_all | solution.py:252
  12.9 1.3 bitcast_bitcast_fusion
  14.1 16.4 %all-to-all-done.1 = bf16[16,256,128]{2,1,0:T(8,128)(2,1)S(1)} async-done(((bf16[16,256,128]{2,1,0:T(8,128)(2,1)}), bf16[16,256,128]{2,1,0:T(8,128)(2,1)S(1)}, u32[]{:S(2)}, u32[]{:S(2)}) %all-to-all-start.1) | async-done | bytes 1048608 | tf_op jit(solution)/shard_map/all_to_all | solution.py:252
  30.6 4.3 %all-to-all-start.2 = ((bf16[16,256,128]{2,1,0:T(8,128)(2,1)}), bf16[16,256,128]{2,1,0:T(8,128)(2,1)}, u32[]{:S(2)}, u32[]{:S(2)}) async-start(bf16[16,256,128]{2,1,0:T(8,128)(2,1)} %bitcast_bitcast_fusion), calls=%async_computation.2 | async-start | bytes 2097152 | tf_op jit(solution)/shard_map/all_to_all | solution.py:252
  34.9 2.0 %collective-permute-start.1 = (bf16[16,256,128]{2,1,0:T(8,128)(2,1)S(1)}, bf16[16,256,128]{2,1,0:T(8,128)(2,1)S(1)}, u32[]{:S(2)}, u32[]{:S(2)}) collective-permute-start(bf16[16,256,128]{2,1,0:T(8,128)(2,1)S(1)} %all-to-all-done.1), channel_id=1, source_target_pairs={{0,2},{2,4},{4,6},{6,0},{1,7},{3,1},{5,3},{7,5},{8,10},{10,12},{12... | collective-permute-start | bytes 3145736 | tf_op jit(solution)/shard_map/ppermute | solution.py:210
  36.9 13.1 %all-to-all-done.2 = bf16[16,256,128]{2,1,0:T(8,128)(2,1)} async-done(((bf16[16,256,128]{2,1,0:T(8,128)(2,1)}), bf16[16,256,128]{2,1,0:T(8,128)(2,1)}, u32[]{:S(2)}, u32[]{:S(2)}) %all-to-all-start.2) | async-done | bytes 1048608 | tf_op jit(solution)/shard_map/all_to_all | solution.py:252
  50.0 1.9 %collective-permute-start.8 = (bf16[16,256,128]{2,1,0:T(8,128)(2,1)}, bf16[16,256,128]{2,1,0:T(8,128)(2,1)}, u32[]{:S(2)}, u32[]{:S(2)}) collective-permute-start(bf16[16,256,128]{2,1,0:T(8,128)(2,1)} %all-to-all-done.2), channel_id=1, source_target_pairs={{0,2},{2,4},{4,6},{6,0},{1,7},{3,1},{5,3},{7,5},{8,10},{10,12},{12... | collective-permute-start | bytes 3145736 | tf_op jit(solution)/shard_map/ppermute | solution.py:210
  51.9 1.9 %collective-permute-start.3 = (bf16[16,256,128]{2,1,0:T(8,128)(2,1)S(1)}, bf16[16,256,128]{2,1,0:T(8,128)(2,1)}, u32[]{:S(2)}, u32[]{:S(2)}) collective-permute-start(bf16[16,256,128]{2,1,0:T(8,128)(2,1)S(1)} %collective-permute-done.1), channel_id=1, source_target_pairs={{0,2},{2,4},{4,6},{6,0},{1,7},{3,1},{5,3},{7,5},{8,10},{10,12},{12... | collective-permute-start | bytes 3145736 | tf_op jit(solution)/shard_map/ppermute | solution.py:210
  53.8 1.6 collective-permute-start.2
  56.0 11.1 %collective-permute-done.8 = bf16[16,256,128]{2,1,0:T(8,128)(2,1)} collective-permute-done((bf16[16,256,128]{2,1,0:T(8,128)(2,1)}, bf16[16,256,128]{2,1,0:T(8,128)(2,1)}, u32[]{:S(2)}, u32[]{:S(2)}) %collective-permute-start.8) | collective-permute-done | bytes 1048608 | tf_op jit(solution)/shard_map/ppermute | solution.py:210
  67.1 1.8 collective-permute-start.9
  68.9 1.2 copy-done.7
  70.2 0.8 copy-done.9
  71.6 1.2 rope.2
  72.9 1.0 copy-done.5
  73.8 4.3 %all-to-all-start = ((bf16[16,256,128]{2,1,0:T(8,128)(2,1)}), bf16[16,256,128]{2,1,0:T(8,128)(2,1)}, u32[]{:S(2)}, u32[]{:S(2)}) async-start(bf16[16,256,128]{2,1,0:T(8,128)(2,1)} %copy-done.5), calls=%async_computation | async-start | bytes 2097152 | tf_op jit(solution)/shard_map/all_to_all | solution.py:252
  78.4 11.2 %collective-permute-done.2 = bf16[16,256,128]{2,1,0:T(8,128)(2,1)} collective-permute-done((bf16[16,256,128]{2,1,0:T(8,128)(2,1)}, bf16[16,256,128]{2,1,0:T(8,128)(2,1)}, u32[]{:S(2)}, u32[]{:S(2)}) %collective-permute-start.2) | collective-permute-done | bytes 1048608 | tf_op jit(solution)/shard_map/ppermute | solution.py:210
  90.1 10.7 %collective-permute-done.10 = bf16[16,256,128]{2,1,0:T(8,128)(2,1)} collective-permute-done((bf16[16,256,128]{2,1,0:T(8,128)(2,1)}, bf16[16,256,128]{2,1,0:T(8,128)(2,1)}, u32[]{:S(2)}, u32[]{:S(2)}) %collective-permute-start.10) | collective-permute-done | bytes 1048608 | tf_op jit(solution)/shard_map/ppermute | solution.py:210
  100.8 11.2 %collective-permute-done.9 = bf16[16,256,128]{2,1,0:T(8,128)(2,1)} collective-permute-done((bf16[16,256,128]{2,1,0:T(8,128)(2,1)}, bf16[16,256,128]{2,1,0:T(8,128)(2,1)}, u32[]{:S(2)}, u32[]{:S(2)}) %collective-permute-start.9) | collective-permute-done | bytes 1048608 | tf_op jit(solution)/shard_map/ppermute | solution.py:210
  113.0 1.3 fusion.10
  114.3 12.4 %weights.3 = (bf16[16,12,128,256]{3,2,1,0:T(8,128)(2,1)S(1)}, f32[16,128,128]{2,1,0:T(8,128)S(1)}) custom-call(s32[384]{0:T(512)S(1)} %slice.43.lists_ref, s32[16]{0:T(128)S(1)} %slice.45.counts_ref, bf16[16,128,128]{2,1,0:T(8,128)(2,1)S(1)} %bitcast.38, bf16[32,128,128]{2,1,0:T(8,128)(2,1)S(1)} %bitcast.32, bf16[32,128,128]{2,1,0:T(8,128)(2,1)} %bitcast.2.refs_1_, ...), custom_call_target="tpu_custom_call" | custom-call | tf_op jit(solution)/shard_map/weights/pallas_call | solution.py:142
  126.7 4.5 %copy-done.1 = bf16[16,12,128,256]{3,2,1,0:T(8,128)(2,1)} copy-done((bf16[16,12,128,256]{3,2,1,0:T(8,128)(2,1)}, bf16[16,12,128,256]{3,2,1,0:T(8,128)(2,1)S(1)}, u32[]{:S(2)}) %copy-start.1) | copy-done | bytes 12582936
  131.2 12.4 %weights.2 = (bf16[16,12,128,256]{3,2,1,0:T(8,128)(2,1)S(1)}, f32[16,128,128]{2,1,0:T(8,128)S(1)}) custom-call(s32[384]{0:T(512)S(1)} %slice.37.lists_ref, s32[16]{0:T(128)S(1)} %slice.39.counts_ref, bf16[16,128,128]{2,1,0:T(8,128)(2,1)S(1)} %bitcast.37, bf16[32,128,128]{2,1,0:T(8,128)(2,1)S(1)} %bitcast.33, bf16[32,128,128]{2,1,0:T(8,128)(2,1)} %bitcast.2.refs_1_, ...), custom_call_target="tpu_custom_call" | custom-call | tf_op jit(solution)/shard_map/weights/pallas_call | solution.py:142
  143.6 4.5 %copy-done.3 = bf16[16,12,128,256]{3,2,1,0:T(8,128)(2,1)} copy-done((bf16[16,12,128,256]{3,2,1,0:T(8,128)(2,1)}, bf16[16,12,128,256]{3,2,1,0:T(8,128)(2,1)S(1)}, u32[]{:S(2)}) %copy-start.3) | copy-done | bytes 12582936
  148.1 4.6 %copy-done.2 = bf16[16,12,128,256]{3,2,1,0:T(8,128)(2,1)S(1)} copy-done((bf16[16,12,128,256]{3,2,1,0:T(8,128)(2,1)S(1)}, bf16[16,12,128,256]{3,2,1,0:T(8,128)(2,1)}, u32[]{:S(2)}) %copy-start.2) | copy-done | bytes 12582936
  152.7 4.6 %copy-done.4 = bf16[16,12,128,256]{3,2,1,0:T(8,128)(2,1)S(1)} copy-done((bf16[16,12,128,256]{3,2,1,0:T(8,128)(2,1)S(1)}, bf16[16,12,128,256]{3,2,1,0:T(8,128)(2,1)}, u32[]{:S(2)}) %copy-start.4) | copy-done | bytes 12582936
  157.3 11.2 %mix.1 = bf16[32,128,128]{2,1,0:T(8,128)(2,1)S(1)} custom-call(s32[768]{0:T(1024)S(1)} %reshape.78.lists_ref, bf16[16,12,128,256]{3,2,1,0:T(8,128)(2,1)S(1)} %copy-done.4, f32[16,128,128]{2,1,0:T(8,128)S(1)} %get-tuple-element.10.refs_1_, bf16[16,12,128,256]{3,2,1,0:T(8,128)(2,1)S(1)} %copy-done.2, f32[16,128,128]{2,1,0:T(8,128)S(1)} %get-tuple-element.12.refs_3_, ...), custom_call_target="tpu_custom_call" | custom-call | tf_op jit(solution)/shard_map/mix/pallas_call | solution.py:190
  168.5 21.0 %all_to_all.20 = bf16[16,256,128]{2,1,0:T(8,128)(2,1)S(1)} all-to-all(bf16[16,256,128]{2,1,0:T(8,128)(2,1)S(1)} %bitcast.36), channel_id=1, replica_groups=mesh['wide'=16,'narrow'=8] {'wide'}, dimensions={0} | all-to-all | bytes 2097152 | tf_op jit(solution)/shard_map/all_to_all | solution.py:252
  189.6 1.1 copy_bitcast_fusion
  (55 shorter events, 4.4 us)
Async XLA Ops:
  0.0 12.9 %copy-start = (bf16[256,2048]{1,0:T(8,128)(2,1)S(1)}, bf16[256,2048]{1,0:T(8,128)(2,1)}, u32[]{:S(2)}) copy-start(bf16[256,2048]{1,0:T(8,128)(2,1)} %param.10) | copy-start | bytes 3145732
  0.0 112.5 %copy-start.13 = (s32[256]{0:T(256)S(1)}, s32[256]{0:T(256)}, u32[]{:S(2)}) copy-start(s32[256]{0:T(256)} %param.13) | copy-start | bytes 3076
  0.8 1.2 copy-start.6
  2.1 0.8 copy-start.8
  2.8 0.7 copy-start.10
  3.5 108.5 %copy-start.12 = (s32[256,24]{0,1:T(8,128)S(1)}, s32[256,24]{0,1:T(8,128)}, u32[]{:S(2)}) copy-start(s32[256,24]{0,1:T(8,128)} %param.12) | copy-start | bytes 73732
  5.7 24.8 %all-to-all-start.1 = ((bf16[16,256,128]{2,1,0:T(8,128)(2,1)}), bf16[16,256,128]{2,1,0:T(8,128)(2,1)S(1)}, u32[]{:S(2)}, u32[]{:S(2)}) async-start(bf16[16,256,128]{2,1,0:T(8,128)(2,1)} %rope.3), calls=%async_computation.1 | async-start | bytes 2097152 | tf_op jit(solution)/shard_map/all_to_all | solution.py:252
  30.6 19.4 %all-to-all-start.2 = ((bf16[16,256,128]{2,1,0:T(8,128)(2,1)}), bf16[16,256,128]{2,1,0:T(8,128)(2,1)}, u32[]{:S(2)}, u32[]{:S(2)}) async-start(bf16[16,256,128]{2,1,0:T(8,128)(2,1)} %bitcast_bitcast_fusion), calls=%async_computation.2 | async-start | bytes 2097152 | tf_op jit(solution)/shard_map/all_to_all | solution.py:252
  34.9 17.0 %collective-permute-start.1 = (bf16[16,256,128]{2,1,0:T(8,128)(2,1)S(1)}, bf16[16,256,128]{2,1,0:T(8,128)(2,1)S(1)}, u32[]{:S(2)}, u32[]{:S(2)}) collective-permute-start(bf16[16,256,128]{2,1,0:T(8,128)(2,1)S(1)} %all-to-all-done.1), channel_id=1, source_target_pairs={{0,2},{2,4},{4,6},{6,0},{1,7},{3,1},{5,3},{7,5},{8,10},{10,12},{12... | collective-permute-start | bytes 3145736 | tf_op jit(solution)/shard_map/ppermute | solution.py:210
  36.9 16.9 %collective-permute-start = (bf16[16,256,128]{2,1,0:T(8,128)(2,1)S(1)}, bf16[16,256,128]{2,1,0:T(8,128)(2,1)}, u32[]{:S(2)}, u32[]{:S(2)}) collective-permute-start(bf16[16,256,128]{2,1,0:T(8,128)(2,1)S(1)} %all-to-all-done.1), channel_id=1, source_target_pairs={{0,1},{1,0},{2,3},{3,2},{4,5},{5,4},{6,7},{7,6},{8,9},{9,8},{10,11... | collective-permute-start | bytes 3145736 | tf_op jit(solution)/shard_map/ppermute | solution.py:213
  50.0 17.1 %collective-permute-start.8 = (bf16[16,256,128]{2,1,0:T(8,128)(2,1)}, bf16[16,256,128]{2,1,0:T(8,128)(2,1)}, u32[]{:S(2)}, u32[]{:S(2)}) collective-permute-start(bf16[16,256,128]{2,1,0:T(8,128)(2,1)} %all-to-all-done.2), channel_id=1, source_target_pairs={{0,2},{2,4},{4,6},{6,0},{1,7},{3,1},{5,3},{7,5},{8,10},{10,12},{12... | collective-permute-start | bytes 3145736 | tf_op jit(solution)/shard_map/ppermute | solution.py:210
  51.9 15.2 %collective-permute-start.7 = (bf16[16,256,128]{2,1,0:T(8,128)(2,1)}, bf16[16,256,128]{2,1,0:T(8,128)(2,1)}, u32[]{:S(2)}, u32[]{:S(2)}) collective-permute-start(bf16[16,256,128]{2,1,0:T(8,128)(2,1)} %all-to-all-done.2), channel_id=1, source_target_pairs={{0,1},{1,0},{2,3},{3,2},{4,5},{5,4},{6,7},{7,6},{8,9},{9,8},{10,11... | collective-permute-start | bytes 3145736 | tf_op jit(solution)/shard_map/ppermute | solution.py:213
  51.9 26.4 %collective-permute-start.3 = (bf16[16,256,128]{2,1,0:T(8,128)(2,1)S(1)}, bf16[16,256,128]{2,1,0:T(8,128)(2,1)}, u32[]{:S(2)}, u32[]{:S(2)}) collective-permute-start(bf16[16,256,128]{2,1,0:T(8,128)(2,1)S(1)} %collective-permute-done.1), channel_id=1, source_target_pairs={{0,2},{2,4},{4,6},{6,0},{1,7},{3,1},{5,3},{7,5},{8,10},{10,12},{12... | collective-permute-start | bytes 3145736 | tf_op jit(solution)/shard_map/ppermute | solution.py:210
  53.8 35.8 %collective-permute-start.2 = (bf16[16,256,128]{2,1,0:T(8,128)(2,1)}, bf16[16,256,128]{2,1,0:T(8,128)(2,1)}, u32[]{:S(2)}, u32[]{:S(2)}) collective-permute-start(bf16[16,256,128]{2,1,0:T(8,128)(2,1)} %collective-permute-done), channel_id=1, source_target_pairs={{0,2},{2,4},{4,6},{6,0},{1,7},{3,1},{5,3},{7,5},{8,10},{10,12},{12... | collective-permute-start | bytes 3145736 | tf_op jit(solution)/shard_map/ppermute | solution.py:210
  55.5 34.1 %collective-permute-start.5 = (bf16[16,256,128]{2,1,0:T(8,128)(2,1)S(1)}, bf16[16,256,128]{2,1,0:T(8,128)(2,1)}, u32[]{:S(2)}, u32[]{:S(2)}) collective-permute-start(bf16[16,256,128]{2,1,0:T(8,128)(2,1)S(1)} %collective-permute-done.1), channel_id=1, source_target_pairs={{0,1},{1,0},{2,3},{3,2},{4,5},{5,4},{6,7},{7,6},{8,9},{9,8},{10,11... | collective-permute-start | bytes 3145736 | tf_op jit(solution)/shard_map/ppermute | solution.py:213
  67.1 33.7 %collective-permute-start.10 = (bf16[16,256,128]{2,1,0:T(8,128)(2,1)}, bf16[16,256,128]{2,1,0:T(8,128)(2,1)}, u32[]{:S(2)}, u32[]{:S(2)}) collective-permute-start(bf16[16,256,128]{2,1,0:T(8,128)(2,1)} %collective-permute-done.8), channel_id=1, source_target_pairs={{0,2},{2,4},{4,6},{6,0},{1,7},{3,1},{5,3},{7,5},{8,10},{10,12},{12... | collective-permute-start | bytes 3145736 | tf_op jit(solution)/shard_map/ppermute | solution.py:210
  67.1 44.9 %collective-permute-start.9 = (bf16[16,256,128]{2,1,0:T(8,128)(2,1)}, bf16[16,256,128]{2,1,0:T(8,128)(2,1)}, u32[]{:S(2)}, u32[]{:S(2)}) collective-permute-start(bf16[16,256,128]{2,1,0:T(8,128)(2,1)} %collective-permute-done.7), channel_id=1, source_target_pairs={{0,2},{2,4},{4,6},{6,0},{1,7},{3,1},{5,3},{7,5},{8,10},{10,12},{12... | collective-permute-start | bytes 3145736 | tf_op jit(solution)/shard_map/ppermute | solution.py:210
  68.9 1.2 copy-start.7
  70.2 0.8 copy-start.9
  70.9 0.7 copy-start.11
  72.9 1.0 copy-start.5
  73.8 39.2 %all-to-all-start = ((bf16[16,256,128]{2,1,0:T(8,128)(2,1)}), bf16[16,256,128]{2,1,0:T(8,128)(2,1)}, u32[]{:S(2)}, u32[]{:S(2)}) async-start(bf16[16,256,128]{2,1,0:T(8,128)(2,1)} %copy-done.5), calls=%async_computation | async-start | bytes 2097152 | tf_op jit(solution)/shard_map/all_to_all | solution.py:252
  78.4 36.0 %collective-permute-start.4 = (bf16[16,256,128]{2,1,0:T(8,128)(2,1)}, bf16[16,256,128]{2,1,0:T(8,128)(2,1)}, u32[]{:S(2)}, u32[]{:S(2)}) collective-permute-start(bf16[16,256,128]{2,1,0:T(8,128)(2,1)} %collective-permute-done.3), channel_id=1, source_target_pairs={{0,1},{1,0},{2,3},{3,2},{4,5},{5,4},{6,7},{7,6},{8,9},{9,8},{10,11... | collective-permute-start | bytes 3145736 | tf_op jit(solution)/shard_map/ppermute | solution.py:213
  89.6 24.7 %collective-permute-start.6 = (bf16[16,256,128]{2,1,0:T(8,128)(2,1)}, bf16[16,256,128]{2,1,0:T(8,128)(2,1)}, u32[]{:S(2)}, u32[]{:S(2)}) collective-permute-start(bf16[16,256,128]{2,1,0:T(8,128)(2,1)} %collective-permute-done.2), channel_id=1, source_target_pairs={{0,1},{1,0},{2,3},{3,2},{4,5},{5,4},{6,7},{7,6},{8,9},{9,8},{10,11... | collective-permute-start | bytes 3145736 | tf_op jit(solution)/shard_map/ppermute | solution.py:213
  89.6 58.5 %collective-permute-start.12 = (bf16[16,256,128]{2,1,0:T(8,128)(2,1)}, bf16[16,256,128]{2,1,0:T(8,128)(2,1)}, u32[]{:S(2)}, u32[]{:S(2)}) collective-permute-start(bf16[16,256,128]{2,1,0:T(8,128)(2,1)} %collective-permute-done.8), channel_id=1, source_target_pairs={{0,1},{1,0},{2,3},{3,2},{4,5},{5,4},{6,7},{7,6},{8,9},{9,8},{10,11... | collective-permute-start | bytes 3145736 | tf_op jit(solution)/shard_map/ppermute | solution.py:213
  100.8 47.3 %collective-permute-start.11 = (bf16[16,256,128]{2,1,0:T(8,128)(2,1)}, bf16[16,256,128]{2,1,0:T(8,128)(2,1)}, u32[]{:S(2)}, u32[]{:S(2)}) collective-permute-start(bf16[16,256,128]{2,1,0:T(8,128)(2,1)} %collective-permute-done.10), channel_id=1, source_target_pairs={{0,1},{1,0},{2,3},{3,2},{4,5},{5,4},{6,7},{7,6},{8,9},{9,8},{10,11... | collective-permute-start | bytes 3145736 | tf_op jit(solution)/shard_map/ppermute | solution.py:213
  112.1 36.1 %collective-permute-start.13 = (bf16[16,256,128]{2,1,0:T(8,128)(2,1)}, bf16[16,256,128]{2,1,0:T(8,128)(2,1)}, u32[]{:S(2)}, u32[]{:S(2)}) collective-permute-start(bf16[16,256,128]{2,1,0:T(8,128)(2,1)} %collective-permute-done.9), channel_id=1, source_target_pairs={{0,1},{1,0},{2,3},{3,2},{4,5},{5,4},{6,7},{7,6},{8,9},{9,8},{10,11... | collective-permute-start | bytes 3145736 | tf_op jit(solution)/shard_map/ppermute | solution.py:213
  126.7 4.5 %copy-start.1 = (bf16[16,12,128,256]{3,2,1,0:T(8,128)(2,1)}, bf16[16,12,128,256]{3,2,1,0:T(8,128)(2,1)S(1)}, u32[]{:S(2)}) copy-start(bf16[16,12,128,256]{3,2,1,0:T(8,128)(2,1)S(1)} %get-tuple-element.11.refs_2_) | copy-start | bytes 37748740
  143.6 4.5 %copy-start.3 = (bf16[16,12,128,256]{3,2,1,0:T(8,128)(2,1)}, bf16[16,12,128,256]{3,2,1,0:T(8,128)(2,1)S(1)}, u32[]{:S(2)}) copy-start(bf16[16,12,128,256]{3,2,1,0:T(8,128)(2,1)S(1)} %get-tuple-element.9.refs_0_) | copy-start | bytes 37748740
  148.1 4.6 %copy-start.2 = (bf16[16,12,128,256]{3,2,1,0:T(8,128)(2,1)S(1)}, bf16[16,12,128,256]{3,2,1,0:T(8,128)(2,1)}, u32[]{:S(2)}) copy-start(bf16[16,12,128,256]{3,2,1,0:T(8,128)(2,1)} %copy-done.1) | copy-start | bytes 37748740
  152.7 4.6 %copy-start.4 = (bf16[16,12,128,256]{3,2,1,0:T(8,128)(2,1)S(1)}, bf16[16,12,128,256]{3,2,1,0:T(8,128)(2,1)}, u32[]{:S(2)}) copy-start(bf16[16,12,128,256]{3,2,1,0:T(8,128)(2,1)} %copy-done.3) | copy-start | bytes 37748740

commit v3 on v2

v3 whole, which is shorter than its diff:
```python
import functools
import math

import jax
import jax.numpy as jnp
from jax import lax
from jax.experimental import pallas as pl
from jax.experimental.pallas import tpu as pltpu
from jax.sharding import PartitionSpec as P

HEADS = 16
HD = 128
BLOCK = 128
KMAX = 24
MIN_LISTED = 6
F32 = jnp.float32
BF16 = jnp.bfloat16
TO_EXP2 = HD**-0.5 * math.log2(math.e)
SECTIONS = ((0, 32), (32, 80), (80, 128))
ROWS_BY_COLS = (((1,), (0,)), ((), ()))
ROWS_BY_ROWS = (((1,), (1,)), ((), ()))


def section_of(lane):
    second = lane >= SECTIONS[1][0]
    third = lane >= SECTIONS[2][0]
    begin = jnp.where(third, SECTIONS[2][0], jnp.where(second, SECTIONS[1][0], 0))
    length = jnp.where(second, SECTIONS[1][1] - SECTIONS[1][0], SECTIONS[0][1])
    number = jnp.where(third, 2, jnp.where(second, 1, 0))
    return begin, length, number


def rotation_of(pos_ref):
    lane = lax.broadcasted_iota(jnp.int32, (3, HD), 1)
    begin, length, number = section_of(lane)
    half = lax.shift_right_logical(length, 1)
    at = lane - begin
    at = jnp.where(at >= half, at - half, at)
    exponent = at.astype(F32) * (-2.0 * math.log(10000.0)) / length.astype(F32)
    mine = number == lax.broadcasted_iota(jnp.int32, (3, HD), 0)
    freqs = jnp.where(mine, jnp.exp(exponent), 0.0)
    angles = lax.dot_general(
        pos_ref[...].astype(F32),
        freqs,
        (((0,), (0,)), ((), ())),
        precision=lax.Precision.HIGHEST,
        preferred_element_type=F32,
    )
    source = lax.broadcasted_iota(jnp.int32, (HD, HD), 0)
    target = lax.broadcasted_iota(jnp.int32, (HD, HD), 1)
    begin, length, number = section_of(target)
    half = lax.shift_right_logical(length, 1)
    lower = target - begin < half
    partner = jnp.where(lower, target + half, target - half)
    sign = jnp.where(lower, -1.0, 1.0)
    pairs = jnp.where(source == partner, sign, 0.0).astype(BF16)
    return jnp.cos(angles), jnp.sin(angles), pairs


def rotate_heads(x_ref, out_ref, cosine, sine, pairs):
    for head in range(HEADS):
        x = x_ref[:, head * HD : (head + 1) * HD]
        partner = lax.dot_general(x, pairs, ROWS_BY_COLS, preferred_element_type=F32)
        out_ref[head] = (x.astype(F32) * cosine + partner * sine).astype(BF16)


def keys_kernel(pos_ref, k_ref, out_ref):
    rotate_heads(k_ref, out_ref, *rotation_of(pos_ref))


def others_kernel(pos_ref, q_ref, v_ref, q_out, v_out):
    for head in range(HEADS):
        v_out[head] = v_ref[:, head * HD : (head + 1) * HD]
    rotate_heads(q_ref, q_out, *rotation_of(pos_ref))


def by_heads(kernel, name, positions, *xs):
    heads = jax.ShapeDtypeStruct((HEADS, xs[0].shape[0], HD), BF16)
    return pl.pallas_call(
        kernel,
        out_shape=[heads] * len(xs),
        compiler_params=pltpu.CompilerParams(vmem_limit_bytes=50 * 2**20),
        name=name,
    )(positions, *xs)


def load_blocks(sources, target, sems, then=()):
    copies = []
    at = 0
    for n, source in enumerate(sources):
        blocks = source.shape[0]
        copies.append(pltpu.make_async_copy(source, target.at[pl.ds(at, blocks)], sems.at[n]))
        at += blocks
    for copy in copies:
        copy.start()
    for copy in then:
        copy.start()
    for copy in copies:
        copy.wait()


def listed_pair(ref, lists_ref, row, pair):
    at = row * KMAX + 2 * pair
    return jnp.concatenate([ref[lists_ref[at]], ref[lists_ref[at + 1]]], axis=0)


def weights_kernel(sources, unroll, first, rows, lists_ref, counts_ref, q_ref, *refs):
    k_parts = refs[:sources]
    weights_out, inverse_ref, k_ref, s_ref, w_ref, sems, out_sems = refs[sources:]
    load_blocks(k_parts, k_ref, sems)
    turns = rows // unroll

    def leave(turn, slot):
        return pltpu.make_async_copy(
            w_ref.at[slot], weights_out.at[pl.ds(turn * unroll, unroll)], out_sems.at[slot]
        )

    def row_weights(row, slot, n):
        query = q_ref[first + row]
        largest = None
        for pair in range(KMAX // 2):
            scores = lax.dot_general(
                query,
                listed_pair(k_ref, lists_ref, first + row, pair),
                ROWS_BY_ROWS,
                preferred_element_type=F32,
            )
            s_ref[n, pair] = scores
            for half in range(2):
                part = scores[:, half * BLOCK : (half + 1) * BLOCK]
                largest = part if largest is None else jnp.maximum(largest, part)
        shift = jnp.broadcast_to(
            jnp.max(largest, axis=1, keepdims=True) * TO_EXP2, (BLOCK, BLOCK)
        )
        count = counts_ref[first + row]
        total = None
        for entry in range(KMAX):
            pair, half = divmod(entry, 2)
            shift_here = shift
            if entry >= MIN_LISTED:
                shift_here = shift + jnp.where(entry < count, 0.0, 1e30)
            lanes = slice(half * BLOCK, (half + 1) * BLOCK)
            part = jnp.exp2(s_ref[n, pair, :, lanes] * TO_EXP2 - shift_here)
            total = part if total is None else total + part
            w_ref[slot, n, pair, :, lanes] = part.astype(BF16)
        inverse_ref[row] = jnp.broadcast_to(
            1.0 / jnp.sum(total, axis=1, keepdims=True), (BLOCK, BLOCK)
        )

    def step(turn, carry):
        slot = turn & 1

        @pl.when(turn >= 2)
        def _():
            leave(turn - 2, slot).wait()

        for n in range(unroll):
            row_weights(turn * unroll + n, slot, n)
        leave(turn, slot).start()
        return carry

    lax.fori_loop(0, turns, step, 0)
    for turn in range(max(turns - 2, 0), turns):
        leave(turn, turn & 1).wait()


SMEM_SPEC = pl.BlockSpec(memory_space=pltpu.SMEM)
VMEM_SPEC = pl.BlockSpec(memory_space=pltpu.VMEM)
ANY_SPEC = pl.BlockSpec(memory_space=pl.ANY)


def weights_of(lists, counts, q, k_parts, first, rows, unroll=4):
    blocks = sum(part.shape[0] for part in k_parts)
    group = (unroll, KMAX // 2, BLOCK, 2 * BLOCK)
    return pl.pallas_call(
        functools.partial(weights_kernel, len(k_parts), unroll, first, rows),
        in_specs=[SMEM_SPEC, SMEM_SPEC, VMEM_SPEC] + [ANY_SPEC] * len(k_parts),
        out_specs=[ANY_SPEC, VMEM_SPEC],
        scratch_shapes=[
            pltpu.VMEM((blocks, BLOCK, HD), BF16),
            pltpu.VMEM(group, F32),
            pltpu.VMEM((2,) + group, BF16),
            pltpu.SemaphoreType.DMA((len(k_parts),)),
            pltpu.SemaphoreType.DMA((2,)),
        ],
        out_shape=[
            jax.ShapeDtypeStruct((rows,) + group[1:], BF16),
            jax.ShapeDtypeStruct((rows, BLOCK, BLOCK), F32),
        ],
        compiler_params=pltpu.CompilerParams(vmem_limit_bytes=48 * 2**20),
        cost_estimate=pl.CostEstimate(
            flops=2 * rows * KMAX * BLOCK * BLOCK * HD,
            bytes_accessed=rows * 3 * 2**20,
            transcendentals=rows * KMAX * BLOCK * BLOCK,
        ),
        name="weights",
    )(lists, counts, q, *k_parts)


def mix_of(lists, halves, v_parts, unroll=4, slots=4):
    groups = len(halves)
    group_rows = halves[0][0].shape[0]
    rows = groups * group_rows
    turns = rows // unroll
    blocks = sum(part.shape[0] for part in v_parts)

    def kernel(lists_ref, *refs):
        weights_refs = refs[:groups]
        inverse_refs = refs[groups : 2 * groups]
        v_refs = refs[2 * groups : 2 * groups + len(v_parts)]
        out_ref, v_ref, w_ref, sems, w_sems = refs[2 * groups + len(v_parts) :]

        def fetch(turn):
            group, at = divmod(turn * unroll, group_rows)
            slot = turn % slots
            return pltpu.make_async_copy(
                weights_refs[group].at[pl.ds(at, unroll)], w_ref.at[slot], w_sems.at[slot]
            )

        fetch(0).start()
        load_blocks(v_refs, v_ref, sems, [fetch(n) for n in range(1, slots - 1)])
        for turn in range(turns):
            fetch(turn).wait()
            if turn + slots - 1 < turns:
                fetch(turn + slots - 1).start()
            for n in range(unroll):
                row = turn * unroll + n
                group, at = divmod(row, group_rows)
                mixed = None
                for pair in range(KMAX // 2):
                    product = lax.dot_general(
                        w_ref[turn % slots, n, pair],
                        listed_pair(v_ref, lists_ref, row, pair),
                        ROWS_BY_COLS,
                        preferred_element_type=F32,
                    )
                    mixed = product if mixed is None else mixed + product
                out_ref[row] = (mixed * inverse_refs[group][at]).astype(BF16)

    return pl.pallas_call(
        kernel,
        in_specs=[SMEM_SPEC]
        + [ANY_SPEC] * groups
        + [VMEM_SPEC] * groups
        + [ANY_SPEC] * len(v_parts),
        out_specs=VMEM_SPEC,
        scratch_shapes=[
            pltpu.VMEM((blocks, BLOCK, HD), BF16),
            pltpu.VMEM((slots, unroll, KMAX // 2, BLOCK, 2 * BLOCK), BF16),
            pltpu.SemaphoreType.DMA((len(v_parts),)),
            pltpu.SemaphoreType.DMA((slots,)),
        ],
        out_shape=jax.ShapeDtypeStruct((rows, BLOCK, HD), BF16),
        compiler_params=pltpu.CompilerParams(vmem_limit_bytes=48 * 2**20),
        cost_estimate=pl.CostEstimate(
            flops=2 * rows * KMAX * BLOCK * BLOCK * HD,
            bytes_accessed=rows * 3 * 2**19,
            transcendentals=0,
        ),
        name="mix",
    )(lists, *[w for w, _ in halves], *[i for _, i in halves], *v_parts)


def after(x, *others):
    return lax.optimization_barrier((x,) + others)[0]


class Ring:
    def __init__(self):
        self.chips = lax.axis_size("narrow") // 2

    def along(self, x, turn):
        steps = [
            (2 * z + core, 2 * ((z + (turn if core == 0 else -turn)) % self.chips) + core)
            for z in range(self.chips)
            for core in range(2)
        ]
        return lax.ppermute(x, "narrow", steps)

    def across(self, x):
        return lax.ppermute(x, "narrow", [(n, n ^ 1) for n in range(2 * self.chips)])


def slots_of(source, part):
    core = part & 1
    apart = (lax.shift_right_logical(source, 1) - lax.shift_right_logical(part, 1)) & 3
    same = (source & 1) == core
    main = jnp.where(core == 0, 3, 1)
    slot_same = jnp.where(apart == 0, 0, jnp.where(apart == 2, 3, jnp.where(apart == main, 1, 2)))
    slot_other = jnp.where(apart == 0, 4, jnp.where(apart == 2, 7, jnp.where(apart == main, 6, 5)))
    return jnp.where(same, slot_same, slot_other)


def shards(query_proj, key_proj, value_proj, positions, key_lists, key_counts):
    frames = lax.axis_size("wide")
    parts = lax.axis_size("narrow")
    part = lax.axis_index("narrow")
    rows = query_proj.shape[0]
    halves = rows // BLOCK
    frame_blocks = parts * halves
    ring = Ring()

    def heads_out(x):
        return lax.all_to_all(x, "wide", split_axis=0, concat_axis=0, tiled=True)

    def blocks_of(x):
        return x.reshape(frames * halves, BLOCK, HD)

    shift = frame_blocks.bit_length() - 1
    frame = lax.shift_right_logical(key_lists, shift)
    inner = key_lists & (frame_blocks - 1)
    source = lax.shift_right_logical(inner, halves.bit_length() - 1)
    places = slots_of(source, part) * (frames * halves) + frame * halves + (inner & (halves - 1))
    mine = lax.dynamic_index_in_dim(
        places.reshape(frames, parts, halves * KMAX), part, 1, keepdims=False
    ).reshape(-1)
    counts = lax.dynamic_index_in_dim(
        key_counts.reshape(frames, parts, halves), part, 1, keepdims=False
    ).reshape(-1)

    (k_rot,) = by_heads(keys_kernel, "rotate_keys", positions, key_proj)
    q_rot, v_heads = by_heads(
        others_kernel, "rotate_queries", after(positions, k_rot), query_proj, value_proj
    )

    k_own = after(heads_out(k_rot), v_heads, mine, counts)
    k_main = ring.along(k_own, 1)
    k_opposite = ring.along(k_own, -1)
    k_other = ring.across(k_own)
    v_own = heads_out(after(v_heads, k_own))
    k_far = ring.along(after(k_main, v_own), 1)
    k_main_other = ring.across(k_main)
    k_opposite_other = ring.across(k_opposite)
    q_heads = heads_out(after(q_rot, v_own, k_main_other))
    q = blocks_of(q_heads)
    k_far_other = ring.across(after(k_far, q_heads))
    k_parts = [k_own, k_main, k_opposite, k_far, k_other, k_main_other, k_opposite_other, k_far_other]
    k_parts = [blocks_of(x) for x in k_parts]


    v_ring = after(v_own, k_main_other)
    v_main = ring.along(v_ring, 1)
    v_opposite = ring.along(v_ring, -1)
    v_other = ring.across(v_ring)

    half = frames * halves // 2
    first = weights_of(mine, counts, q, k_parts, 0, half)
    v_main, v_opposite = lax.optimization_barrier((v_main, v_opposite, first[1]))[:2]
    v_far = ring.along(v_main, 1)
    second = weights_of(after(mine, v_main), counts, q, k_parts, half, half)
    v_parts = [v_own, v_main, v_opposite, v_far, v_other]
    v_parts += [ring.across(x) for x in (v_main, v_opposite, after(v_far, second[1]))]
    v_parts = [blocks_of(x) for x in v_parts]
    mixed = mix_of(mine, [first, second], v_parts).reshape(frames, rows, HD)
    back = heads_out(mixed)
    return back.transpose(1, 0, 2).reshape(rows, HEADS * HD)


def solution(mesh):
    return jax.shard_map(
        shards,
        mesh=mesh,
        in_specs=(
            P(("wide", "narrow"), None),
            P(("wide", "narrow"), None),
            P(("wide", "narrow"), None),
            P(None, ("wide", "narrow")),
            P(),
            P(),
        ),
        out_specs=P(("wide", "narrow"), None),
        check_vma=False,
    )
```

time: 191 us -> 155 us (0.81)
  waiting for transfers between devices: 74 us -> 50.6 us
  local copies, waits for them, and re-layouts: 29 us -> 10.1 us
  Pallas kernels: 39.5 us -> 47.5 us
  starting transfers between devices: 26.2 us -> 24 us
    unnamed x28 -> x26, local copies, waits for them, and re-layouts: 24.5 us -> 7.79 us
    all_to_all x3, waiting for transfers between devices: 29.5 us -> 13.5 us  [heads_out(): return lax.all_to_all(x, 'wide', split_axis=0, concat_axis=0, tiled=True)]
    ppermute x6, waiting for transfers between devices: 44.5 us -> 34.8 us  [along(): return lax.ppermute(x, 'narrow', steps)]
    pallas_call x5, Pallas kernels: 39.5 us -> 47.5 us  [the longest x2 28.5 us: weights_of(): pl.pallas_call(functools.partial(weights_kernel, len(k_parts), unroll, fi...]
    ppermute x8, waiting for transfers between devices: 0.02 us -> 2.26 us  [across(): lax.ppermute(x, 'narrow', [(n, n ^ 1) for n in range(2 * self.chips)])]
  transfers between devices with their start and end apart: 17 -> 17, of which waited for: 7 -> 7; matrix products, arithmetic and copies ran while one was open for 2% -> 1% of each run, Pallas kernels for 14% -> 21%
where the time goes in v3:
time: 155 us; the launch traced here: 154 us
  waiting for transfers between devices  50.6 us (33%)
  Pallas kernels  47.5 us (31%)
  starting transfers between devices  24 us (15%)
  blocking collectives  20.9 us (13%)
  local copies, waits for them, and re-layouts  10.1 us (7%)
    ppermute x6, waiting for transfers between devices, along(): return lax.ppermute(x, 'narrow', steps)  34.8 us
    pallas_call x2, Pallas kernels, weights_of(): pl.pallas_call(functools.partial(weights_kernel, len(k_parts), unroll, fi...  28.5 us
    all_to_all x1, blocking collectives, heads_out(): return lax.all_to_all(x, 'wide', split_axis=0, concat_axis=0, tiled=True)  20.9 us
    all_to_all x3, starting transfers between devices, heads_out(): return lax.all_to_all(x, 'wide', split_axis=0, concat_axis=0, tiled=True)  14.4 us
    all_to_all x3, waiting for transfers between devices, heads_out(): return lax.all_to_all(x, 'wide', split_axis=0, concat_axis=0, tiled=True)  13.5 us
    pallas_call x1, Pallas kernels, mix_of(): pl.pallas_call(kernel, in_specs=[SMEM_SPEC] + [ANY_SPEC] * groups + [VMEM...  13.1 us
    ppermute x6, starting transfers between devices, along(): return lax.ppermute(x, 'narrow', steps)  8.38 us
    unnamed x26, local copies, waits for them, and re-layouts  7.79 us
  transfers between devices with their start and end apart: 17, of which 7 were waited for; matrix products, arithmetic and copies ran while one was open for 1% of the time, Pallas kernels for 21%

profile of v3, /device:TPU:0, one launch (start us, length us, event | category | flops | bytes accessed | tf_op | source)
XLA Modules:
  0.0 154.1 jit_solution(5808544481472542149)
XLA Ops:
  0.0 1.2 copy-done
  1.2 0.7 copy-done.3
  1.9 2.2 %rotate_keys.1 = bf16[16,256,128]{2,1,0:T(8,128)(2,1)} custom-call(s32[3,256]{1,0:T(4,128)S(1)} %copy-done.3, bf16[256,2048]{1,0:T(8,128)(2,1)S(1)} %copy-done), custom_call_target="tpu_custom_call" | custom-call | tf_op jit(solution)/shard_map/rotate_keys/pallas_call | solution.py:79
  4.1 7.1 %all-to-all-start = ((bf16[16,256,128]{2,1,0:T(8,128)(2,1)}), bf16[16,256,128]{2,1,0:T(8,128)(2,1)S(1)}, u32[]{:S(2)}, u32[]{:S(2)}) async-start(bf16[16,256,128]{2,1,0:T(8,128)(2,1)} %rotate_keys.1), calls=%async_computation | async-start | bytes 2097152 | tf_op jit(solution)/shard_map/all_to_all | solution.py:304
  11.3 0.8 and_add_fusion
  12.3 0.8 reshape.73
  13.3 1.2 copy-done.1
  14.5 0.7 copy-done.4
  15.2 3.6 %rotate_queries.1 = (bf16[16,256,128]{2,1,0:T(8,128)(2,1)S(1)}, bf16[16,256,128]{2,1,0:T(8,128)(2,1)}) custom-call(s32[3,256]{1,0:T(4,128)S(1)} %copy-done.4, bf16[256,2048]{1,0:T(8,128)(2,1)S(1)} %copy-done.1, bf16[256,2048]{1,0:T(8,128)(2,1)} %v_ref.1), custom_call_target="tpu_custom_call" | custom-call | tf_op jit(solution)/shard_map/rotate_queries/pallas_call | solution.py:79
  18.8 1.0 copy-done.2
  19.8 9.2 %all-to-all-done = bf16[16,256,128]{2,1,0:T(8,128)(2,1)S(1)} async-done(((bf16[16,256,128]{2,1,0:T(8,128)(2,1)}), bf16[16,256,128]{2,1,0:T(8,128)(2,1)S(1)}, u32[]{:S(2)}, u32[]{:S(2)}) %all-to-all-start) | async-done | bytes 1048608 | tf_op jit(solution)/shard_map/all_to_all | solution.py:304
  29.0 1.9 %collective-permute-start = (bf16[16,256,128]{2,1,0:T(8,128)(2,1)S(1)}, bf16[16,256,128]{2,1,0:T(8,128)(2,1)}, u32[]{:S(2)}, u32[]{:S(2)}) collective-permute-start(bf16[16,256,128]{2,1,0:T(8,128)(2,1)S(1)} %all-to-all-done), channel_id=1, source_target_pairs={{0,2},{1,7},{2,4},{3,1},{4,6},{5,3},{6,0},{7,5},{8,10},{9,15},{10,... | collective-permute-start | bytes 3145736 | tf_op jit(solution)/shard_map/ppermute | solution.py:278
  30.9 3.7 %all-to-all-start.1 = ((bf16[16,256,128]{2,1,0:T(8,128)(2,1)}), bf16[16,256,128]{2,1,0:T(8,128)(2,1)S(1)}, u32[]{:S(2)}, u32[]{:S(2)}) async-start(bf16[16,256,128]{2,1,0:T(8,128)(2,1)} %get-tuple-element.26), calls=%async_computation.1 | async-start | bytes 2097152 | tf_op jit(solution)/shard_map/all_to_all | solution.py:304
  34.5 11.3 %collective-permute-done = bf16[16,256,128]{2,1,0:T(8,128)(2,1)} collective-permute-done((bf16[16,256,128]{2,1,0:T(8,128)(2,1)S(1)}, bf16[16,256,128]{2,1,0:T(8,128)(2,1)}, u32[]{:S(2)}, u32[]{:S(2)}) %collective-permute-start) | collective-permute-done | bytes 1048608 | tf_op jit(solution)/shard_map/ppermute | solution.py:278
  45.9 2.0 %collective-permute-start.2 = (bf16[16,256,128]{2,1,0:T(8,128)(2,1)S(1)}, bf16[16,256,128]{2,1,0:T(8,128)(2,1)}, u32[]{:S(2)}, u32[]{:S(2)}) collective-permute-start(bf16[16,256,128]{2,1,0:T(8,128)(2,1)S(1)} %all-to-all-done), channel_id=1, source_target_pairs={{0,6},{1,3},{2,0},{3,5},{4,2},{5,7},{6,4},{7,1},{8,14},{9,11},{10,... | collective-permute-start | bytes 3145736 | tf_op jit(solution)/shard_map/ppermute | solution.py:278
  47.9 4.3 %all-to-all-done.1 = bf16[16,256,128]{2,1,0:T(8,128)(2,1)S(1)} async-done(((bf16[16,256,128]{2,1,0:T(8,128)(2,1)}), bf16[16,256,128]{2,1,0:T(8,128)(2,1)S(1)}, u32[]{:S(2)}, u32[]{:S(2)}) %all-to-all-start.1) | async-done | bytes 1048608 | tf_op jit(solution)/shard_map/all_to_all | solution.py:304
  52.2 1.0 copy-done.11
  53.2 3.7 %all-to-all-start.2 = ((bf16[16,256,128]{2,1,0:T(8,128)(2,1)}), bf16[16,256,128]{2,1,0:T(8,128)(2,1)S(1)}, u32[]{:S(2)}, u32[]{:S(2)}) async-start(bf16[16,256,128]{2,1,0:T(8,128)(2,1)} %copy-done.2), calls=%async_computation.2 | async-start | bytes 2097152 | tf_op jit(solution)/shard_map/all_to_all | solution.py:304
  57.0 13.3 %collective-permute-done.2 = bf16[16,256,128]{2,1,0:T(8,128)(2,1)} collective-permute-done((bf16[16,256,128]{2,1,0:T(8,128)(2,1)S(1)}, bf16[16,256,128]{2,1,0:T(8,128)(2,1)}, u32[]{:S(2)}, u32[]{:S(2)}) %collective-permute-start.2) | collective-permute-done | bytes 1048608 | tf_op jit(solution)/shard_map/ppermute | solution.py:278
  70.2 2.5 %collective-permute-done.3 = bf16[16,256,128]{2,1,0:T(8,128)(2,1)} collective-permute-done((bf16[16,256,128]{2,1,0:T(8,128)(2,1)}, bf16[16,256,128]{2,1,0:T(8,128)(2,1)}, u32[]{:S(2)}, u32[]{:S(2)}) %collective-permute-start.3) | collective-permute-done | bytes 1048608 | tf_op jit(solution)/shard_map/ppermute | solution.py:278
  72.8 1.7 %collective-permute-start.7 = (bf16[16,256,128]{2,1,0:T(8,128)(2,1)S(1)}, bf16[16,256,128]{2,1,0:T(8,128)(2,1)S(1)}, u32[]{:S(2)}, u32[]{:S(2)}) collective-permute-start(bf16[16,256,128]{2,1,0:T(8,128)(2,1)S(1)} %all-to-all-done.1), channel_id=1, source_target_pairs={{0,2},{1,7},{2,4},{3,1},{4,6},{5,3},{6,0},{7,5},{8,10},{9,15},{10,... | collective-permute-start | bytes 3145736 | tf_op jit(solution)/shard_map/ppermute | solution.py:278
  74.5 1.5 collective-permute-start.8
  76.0 1.0 copy-done.12
  77.0 14.2 %weights.2 = (bf16[16,12,128,256]{3,2,1,0:T(8,128)(2,1)}, f32[16,128,128]{2,1,0:T(8,128)S(1)}) custom-call(s32[768]{0:T(1024)S(1)} %reshape.72.lists_ref, s32[32]{0:T(128)S(1)} %reshape.74.counts_ref, bf16[32,128,128]{2,1,0:T(8,128)(2,1)S(1)} %bitcast.29, bf16[32,128,128]{2,1,0:T(8,128)(2,1)S(1)} %bitcast.27, bf16[32,128,128]{2,1,0:T(8,128)(2,1)} %bitcast.2.refs_1_, ...), custom_call_target="tpu_custom_call" | custom-call | flops 1610612736 | bytes 50331648 | tf_op jit(solution)/shard_map/weights/pallas_call | solution.py:175
  91.3 7.7 %collective-permute-done.7 = bf16[16,256,128]{2,1,0:T(8,128)(2,1)S(1)} collective-permute-done((bf16[16,256,128]{2,1,0:T(8,128)(2,1)S(1)}, bf16[16,256,128]{2,1,0:T(8,128)(2,1)S(1)}, u32[]{:S(2)}, u32[]{:S(2)}) %collective-permute-start.7) | collective-permute-done | bytes 1048608 | tf_op jit(solution)/shard_map/ppermute | solution.py:278
  99.0 1.2 collective-permute-start.9
  100.7 14.3 %weights.3 = (bf16[16,12,128,256]{3,2,1,0:T(8,128)(2,1)}, f32[16,128,128]{2,1,0:T(8,128)S(1)}) custom-call(s32[768]{0:T(1024)S(1)} %reshape.72.lists_ref, s32[32]{0:T(128)S(1)} %reshape.74.counts_ref, bf16[32,128,128]{2,1,0:T(8,128)(2,1)S(1)} %bitcast.30, bf16[32,128,128]{2,1,0:T(8,128)(2,1)S(1)} %bitcast.28, bf16[32,128,128]{2,1,0:T(8,128)(2,1)} %bitcast.2.refs_1_, ...), custom_call_target="tpu_custom_call" | custom-call | flops 1610612736 | bytes 50331648 | tf_op jit(solution)/shard_map/weights/pallas_call | solution.py:175
  115.6 2.2 %collective-permute-done.13 = bf16[16,256,128]{2,1,0:T(8,128)(2,1)S(1)} collective-permute-done((bf16[16,256,128]{2,1,0:T(8,128)(2,1)S(1)}, bf16[16,256,128]{2,1,0:T(8,128)(2,1)S(1)}, u32[]{:S(2)}, u32[]{:S(2)}) %collective-permute-start.13) | collective-permute-done | bytes 1048608 | tf_op jit(solution)/shard_map/ppermute | solution.py:281
  117.9 1.0 copy-done.10
  118.9 13.1 %mix.1 = bf16[32,128,128]{2,1,0:T(8,128)(2,1)S(1)} custom-call(s32[768]{0:T(1024)S(1)} %reshape.72.lists_ref, bf16[16,12,128,256]{3,2,1,0:T(8,128)(2,1)} %get-tuple-element.30.refs_0_, bf16[16,12,128,256]{3,2,1,0:T(8,128)(2,1)} %get-tuple-element.35.refs_1_, f32[16,128,128]{2,1,0:T(8,128)S(1)} %get-tuple-element.32.refs_2_, ...), custom_call_target="tpu_custom_call" | custom-call | flops 3221225472 | bytes 50331648 | tf_op jit(solution)/shard_map/mix/pallas_call | solution.py:240
  132.0 20.9 %all_to_all.20 = bf16[16,256,128]{2,1,0:T(8,128)(2,1)S(1)} all-to-all(bf16[16,256,128]{2,1,0:T(8,128)(2,1)S(1)} %bitcast.25), channel_id=1, replica_groups=mesh['wide'=16,'narrow'=8] {'wide'}, dimensions={0} | all-to-all | bytes 2097152 | tf_op jit(solution)/shard_map/all_to_all | solution.py:304
  152.9 1.1 copy_bitcast_fusion
  (43 shorter events, 1.7 us)
Async XLA Ops:
  0.0 1.2 copy-start
  1.2 0.7 copy-start.3
  4.1 24.8 %all-to-all-start = ((bf16[16,256,128]{2,1,0:T(8,128)(2,1)}), bf16[16,256,128]{2,1,0:T(8,128)(2,1)S(1)}, u32[]{:S(2)}, u32[]{:S(2)}) async-start(bf16[16,256,128]{2,1,0:T(8,128)(2,1)} %rotate_keys.1), calls=%async_computation | async-start | bytes 2097152 | tf_op jit(solution)/shard_map/all_to_all | solution.py:304
  13.3 1.2 copy-start.1
  14.5 0.7 copy-start.4
  18.8 1.0 copy-start.2
  29.0 16.9 %collective-permute-start = (bf16[16,256,128]{2,1,0:T(8,128)(2,1)S(1)}, bf16[16,256,128]{2,1,0:T(8,128)(2,1)}, u32[]{:S(2)}, u32[]{:S(2)}) collective-permute-start(bf16[16,256,128]{2,1,0:T(8,128)(2,1)S(1)} %all-to-all-done), channel_id=1, source_target_pairs={{0,2},{1,7},{2,4},{3,1},{4,6},{5,3},{6,0},{7,5},{8,10},{9,15},{10,... | collective-permute-start | bytes 3145736 | tf_op jit(solution)/shard_map/ppermute | solution.py:278
  30.9 21.3 %all-to-all-start.1 = ((bf16[16,256,128]{2,1,0:T(8,128)(2,1)}), bf16[16,256,128]{2,1,0:T(8,128)(2,1)S(1)}, u32[]{:S(2)}, u32[]{:S(2)}) async-start(bf16[16,256,128]{2,1,0:T(8,128)(2,1)} %get-tuple-element.26), calls=%async_computation.1 | async-start | bytes 2097152 | tf_op jit(solution)/shard_map/all_to_all | solution.py:304
  45.9 6.4 %collective-permute-start.1 = (bf16[16,256,128]{2,1,0:T(8,128)(2,1)}, bf16[16,256,128]{2,1,0:T(8,128)(2,1)S(1)}, u32[]{:S(2)}, u32[]{:S(2)}) collective-permute-start(bf16[16,256,128]{2,1,0:T(8,128)(2,1)} %collective-permute-done), channel_id=1, source_target_pairs={{0,1},{1,0},{2,3},{3,2},{4,5},{5,4},{6,7},{7,6},{8,9},{9,8},{10,11... | collective-permute-start | bytes 3145736 | tf_op jit(solution)/shard_map/ppermute | solution.py:281
  45.9 24.4 %collective-permute-start.2 = (bf16[16,256,128]{2,1,0:T(8,128)(2,1)S(1)}, bf16[16,256,128]{2,1,0:T(8,128)(2,1)}, u32[]{:S(2)}, u32[]{:S(2)}) collective-permute-start(bf16[16,256,128]{2,1,0:T(8,128)(2,1)S(1)} %all-to-all-done), channel_id=1, source_target_pairs={{0,6},{1,3},{2,0},{3,5},{4,2},{5,7},{6,4},{7,1},{8,14},{9,11},{10,... | collective-permute-start | bytes 3145736 | tf_op jit(solution)/shard_map/ppermute | solution.py:278
  52.2 20.5 %collective-permute-start.3 = (bf16[16,256,128]{2,1,0:T(8,128)(2,1)}, bf16[16,256,128]{2,1,0:T(8,128)(2,1)}, u32[]{:S(2)}, u32[]{:S(2)}) collective-permute-start(bf16[16,256,128]{2,1,0:T(8,128)(2,1)} %collective-permute-done), channel_id=1, source_target_pairs={{0,2},{1,7},{2,4},{3,1},{4,6},{5,3},{6,0},{7,5},{8,10},{9,15},{10,... | collective-permute-start | bytes 3145736 | tf_op jit(solution)/shard_map/ppermute | solution.py:278
  52.2 1.0 copy-start.11
  53.2 19.6 %all-to-all-start.2 = ((bf16[16,256,128]{2,1,0:T(8,128)(2,1)}), bf16[16,256,128]{2,1,0:T(8,128)(2,1)S(1)}, u32[]{:S(2)}, u32[]{:S(2)}) async-start(bf16[16,256,128]{2,1,0:T(8,128)(2,1)} %copy-done.2), calls=%async_computation.2 | async-start | bytes 2097152 | tf_op jit(solution)/shard_map/all_to_all | solution.py:304
  56.9 19.1 %collective-permute-start.4 = (bf16[16,256,128]{2,1,0:T(8,128)(2,1)S(1)}, bf16[16,256,128]{2,1,0:T(8,128)(2,1)}, u32[]{:S(2)}, u32[]{:S(2)}) collective-permute-start(bf16[16,256,128]{2,1,0:T(8,128)(2,1)S(1)} %all-to-all-done), channel_id=1, source_target_pairs={{0,1},{1,0},{2,3},{3,2},{4,5},{5,4},{6,7},{7,6},{8,9},{9,8},{10,11... | collective-permute-start | bytes 3145736 | tf_op jit(solution)/shard_map/ppermute | solution.py:281
  70.2 5.8 %collective-permute-start.5 = (bf16[16,256,128]{2,1,0:T(8,128)(2,1)}, bf16[16,256,128]{2,1,0:T(8,128)(2,1)}, u32[]{:S(2)}, u32[]{:S(2)}) collective-permute-start(bf16[16,256,128]{2,1,0:T(8,128)(2,1)} %collective-permute-done.2), channel_id=1, source_target_pairs={{0,1},{1,0},{2,3},{3,2},{4,5},{5,4},{6,7},{7,6},{8,9},{9,8},{10,11... | collective-permute-start | bytes 3145736 | tf_op jit(solution)/shard_map/ppermute | solution.py:281
  72.8 3.3 %collective-permute-start.6 = (bf16[16,256,128]{2,1,0:T(8,128)(2,1)}, bf16[16,256,128]{2,1,0:T(8,128)(2,1)S(1)}, u32[]{:S(2)}, u32[]{:S(2)}) collective-permute-start(bf16[16,256,128]{2,1,0:T(8,128)(2,1)} %collective-permute-done.3), channel_id=1, source_target_pairs={{0,1},{1,0},{2,3},{3,2},{4,5},{5,4},{6,7},{7,6},{8,9},{9,8},{10,11... | collective-permute-start | bytes 3145736 | tf_op jit(solution)/shard_map/ppermute | solution.py:281
  72.8 26.2 %collective-permute-start.7 = (bf16[16,256,128]{2,1,0:T(8,128)(2,1)S(1)}, bf16[16,256,128]{2,1,0:T(8,128)(2,1)S(1)}, u32[]{:S(2)}, u32[]{:S(2)}) collective-permute-start(bf16[16,256,128]{2,1,0:T(8,128)(2,1)S(1)} %all-to-all-done.1), channel_id=1, source_target_pairs={{0,2},{1,7},{2,4},{3,1},{4,6},{5,3},{6,0},{7,5},{8,10},{9,15},{10,... | collective-permute-start | bytes 3145736 | tf_op jit(solution)/shard_map/ppermute | solution.py:278
  74.5 24.4 %collective-permute-start.8 = (bf16[16,256,128]{2,1,0:T(8,128)(2,1)S(1)}, bf16[16,256,128]{2,1,0:T(8,128)(2,1)S(1)}, u32[]{:S(2)}, u32[]{:S(2)}) collective-permute-start(bf16[16,256,128]{2,1,0:T(8,128)(2,1)S(1)} %all-to-all-done.1), channel_id=1, source_target_pairs={{0,6},{1,3},{2,0},{3,5},{4,2},{5,7},{6,4},{7,1},{8,14},{9,11},{10,... | collective-permute-start | bytes 3145736 | tf_op jit(solution)/shard_map/ppermute | solution.py:278
  76.0 1.0 copy-start.12
  99.0 18.9 %copy-start.5 = (bf16[16,256,128]{2,1,0:T(8,128)(2,1)}, bf16[16,256,128]{2,1,0:T(8,128)(2,1)S(1)}, u32[]{:S(2)}) copy-start(bf16[16,256,128]{2,1,0:T(8,128)(2,1)S(1)} %collective-permute-done.8) | copy-start | bytes 3145732
  99.0 16.1 %collective-permute-start.9 = (bf16[16,256,128]{2,1,0:T(8,128)(2,1)S(1)}, bf16[16,256,128]{2,1,0:T(8,128)(2,1)S(1)}, u32[]{:S(2)}, u32[]{:S(2)}) collective-permute-start(bf16[16,256,128]{2,1,0:T(8,128)(2,1)S(1)} %collective-permute-done.7), channel_id=1, source_target_pairs={{0,2},{1,7},{2,4},{3,1},{4,6},{5,3},{6,0},{7,5},{8,10},{9,15},{10,... | collective-permute-start | bytes 3145736 | tf_op jit(solution)/shard_map/ppermute | solution.py:278
  100.2 15.4 %collective-permute-start.10 = (bf16[16,256,128]{2,1,0:T(8,128)(2,1)S(1)}, bf16[16,256,128]{2,1,0:T(8,128)(2,1)S(1)}, u32[]{:S(2)}, u32[]{:S(2)}) collective-permute-start(bf16[16,256,128]{2,1,0:T(8,128)(2,1)S(1)} %all-to-all-done.1), channel_id=1, source_target_pairs={{0,1},{1,0},{2,3},{3,2},{4,5},{5,4},{6,7},{7,6},{8,9},{9,8},{10,11... | collective-permute-start | bytes 3145736 | tf_op jit(solution)/shard_map/ppermute | solution.py:281
  100.2 15.4 %collective-permute-start.11 = (bf16[16,256,128]{2,1,0:T(8,128)(2,1)S(1)}, bf16[16,256,128]{2,1,0:T(8,128)(2,1)S(1)}, u32[]{:S(2)}, u32[]{:S(2)}) collective-permute-start(bf16[16,256,128]{2,1,0:T(8,128)(2,1)S(1)} %collective-permute-done.7), channel_id=1, source_target_pairs={{0,1},{1,0},{2,3},{3,2},{4,5},{5,4},{6,7},{7,6},{8,9},{9,8},{10,11... | collective-permute-start | bytes 3145736 | tf_op jit(solution)/shard_map/ppermute | solution.py:281
  100.7 14.9 %collective-permute-start.12 = (bf16[16,256,128]{2,1,0:T(8,128)(2,1)S(1)}, bf16[16,256,128]{2,1,0:T(8,128)(2,1)S(1)}, u32[]{:S(2)}, u32[]{:S(2)}) collective-permute-start(bf16[16,256,128]{2,1,0:T(8,128)(2,1)S(1)} %collective-permute-done.8), channel_id=1, source_target_pairs={{0,1},{1,0},{2,3},{3,2},{4,5},{5,4},{6,7},{7,6},{8,9},{9,8},{10,11... | collective-permute-start | bytes 3145736 | tf_op jit(solution)/shard_map/ppermute | solution.py:281
  115.0 2.9 %copy-start.6 = (bf16[16,256,128]{2,1,0:T(8,128)(2,1)}, bf16[16,256,128]{2,1,0:T(8,128)(2,1)S(1)}, u32[]{:S(2)}) copy-start(bf16[16,256,128]{2,1,0:T(8,128)(2,1)S(1)} %collective-permute-done.9) | copy-start | bytes 3145732
  115.0 2.8 %collective-permute-start.13 = (bf16[16,256,128]{2,1,0:T(8,128)(2,1)S(1)}, bf16[16,256,128]{2,1,0:T(8,128)(2,1)S(1)}, u32[]{:S(2)}, u32[]{:S(2)}) collective-permute-start(bf16[16,256,128]{2,1,0:T(8,128)(2,1)S(1)} %collective-permute-done.9), channel_id=1, source_target_pairs={{0,1},{1,0},{2,3},{3,2},{4,5},{5,4},{6,7},{7,6},{8,9},{9,8},{10,11... | collective-permute-start | bytes 3145736 | tf_op jit(solution)/shard_map/ppermute | solution.py:281
  115.6 2.3 %copy-start.7 = (bf16[16,256,128]{2,1,0:T(8,128)(2,1)}, bf16[16,256,128]{2,1,0:T(8,128)(2,1)S(1)}, u32[]{:S(2)}) copy-start(bf16[16,256,128]{2,1,0:T(8,128)(2,1)S(1)} %collective-permute-done.10) | copy-start | bytes 3145732
  115.6 2.3 %copy-start.8 = (bf16[16,256,128]{2,1,0:T(8,128)(2,1)}, bf16[16,256,128]{2,1,0:T(8,128)(2,1)S(1)}, u32[]{:S(2)}) copy-start(bf16[16,256,128]{2,1,0:T(8,128)(2,1)S(1)} %collective-permute-done.11) | copy-start | bytes 3145732
  115.6 2.3 %copy-start.9 = (bf16[16,256,128]{2,1,0:T(8,128)(2,1)}, bf16[16,256,128]{2,1,0:T(8,128)(2,1)S(1)}, u32[]{:S(2)}) copy-start(bf16[16,256,128]{2,1,0:T(8,128)(2,1)S(1)} %collective-permute-done.12) | copy-start | bytes 3145732
  117.9 1.0 copy-start.10

commit v4 on v3

--- a/solution.py
+++ b/solution.py
@@ -13,6 +13,7 @@
 BLOCK = 128
 KMAX = 24
 MIN_LISTED = 6
+PIECES = 4
 F32 = jnp.float32
 BF16 = jnp.bfloat16
 TO_EXP2 = HD**-0.5 * math.log2(math.e)
@@ -57,31 +58,64 @@
     return jnp.cos(angles), jnp.sin(angles), pairs
 
 
-def rotate_heads(x_ref, out_ref, cosine, sine, pairs):
-    for head in range(HEADS):
+def rotate_heads(x_ref, out_ref, cosine, sine, pairs, heads):
+    for head in heads:
         x = x_ref[:, head * HD : (head + 1) * HD]
         partner = lax.dot_general(x, pairs, ROWS_BY_COLS, preferred_element_type=F32)
         out_ref[head] = (x.astype(F32) * cosine + partner * sine).astype(BF16)
 
 
-def keys_kernel(pos_ref, k_ref, out_ref):
-    rotate_heads(k_ref, out_ref, *rotation_of(pos_ref))
+def keys_kernel(pos_hbm, k_hbm, out_ref, pos_ref, k_ref, sems):
+    positions = pltpu.make_async_copy(pos_hbm, pos_ref, sems.at[PIECES])
+    positions.start()
+    width = HEADS // PIECES * HD
+    pieces = [
+        pltpu.make_async_copy(
+            k_hbm.at[:, pl.ds(n * width, width)], k_ref.at[:, pl.ds(n * width, width)], sems.at[n]
+        )
+        for n in range(PIECES)
+    ]
+    for piece in pieces:
+        piece.start()
+    positions.wait()
+    rotation = rotation_of(pos_ref)
+    for n, piece in enumerate(pieces):
+        piece.wait()
+        heads = range(n * HEADS // PIECES, (n + 1) * HEADS // PIECES)
+        rotate_heads(k_ref, out_ref, *rotation, heads)
 
 
 def others_kernel(pos_ref, q_ref, v_ref, q_out, v_out):
     for head in range(HEADS):
         v_out[head] = v_ref[:, head * HD : (head + 1) * HD]
-    rotate_heads(q_ref, q_out, *rotation_of(pos_ref))
-
-
-def by_heads(kernel, name, positions, *xs):
-    heads = jax.ShapeDtypeStruct((HEADS, xs[0].shape[0], HD), BF16)
+    rotate_heads(q_ref, q_out, *rotation_of(pos_ref), range(HEADS))
+
+
+def keys_by_heads(positions, x):
+    rows = x.shape[0]
+    hbm = pl.BlockSpec(memory_space=pltpu.HBM)
     return pl.pallas_call(
-        kernel,
-        out_shape=[heads] * len(xs),
+        keys_kernel,
+        in_specs=[hbm, hbm],
+        out_shape=jax.ShapeDtypeStruct((HEADS, rows, HD), BF16),
+        scratch_shapes=[
+            pltpu.VMEM(positions.shape, jnp.int32),
+            pltpu.VMEM(x.shape, BF16),
+            pltpu.SemaphoreType.DMA((PIECES + 1,)),
+        ],
+        compiler_params=pltpu.CompilerParams(vmem_limit_bytes=60 * 2**20),
+        name="rotate_keys",
+    )(positions, x)
+
+
+def others_by_heads(positions, q, v):
+    heads = jax.ShapeDtypeStruct((HEADS, q.shape[0], HD), BF16)
+    return pl.pallas_call(
+        others_kernel,
+        out_shape=[heads, heads],
         compiler_params=pltpu.CompilerParams(vmem_limit_bytes=50 * 2**20),
-        name=name,
-    )(positions, *xs)
+        name="rotate_queries",
+    )(positions, q, v)
 
 
 def load_blocks(sources, target, sems, then=()):
@@ -105,9 +139,12 @@
 
 
 def weights_kernel(sources, unroll, first, rows, lists_ref, counts_ref, q_ref, *refs):
-    k_parts = refs[:sources]
-    weights_out, inverse_ref, k_ref, s_ref, w_ref, sems, out_sems = refs[sources:]
-    load_blocks(k_parts, k_ref, sems)
+    if sources:
+        k_parts = refs[:sources]
+        weights_out, inverse_ref, k_ref, s_ref, w_ref, out_sems, sems = refs[sources:]
+        load_blocks(k_parts, k_ref, sems)
+    else:
+        k_ref, weights_out, inverse_ref, s_ref, w_ref, out_sems = refs
     turns = rows // unroll
 
     def leave(turn, slot):
@@ -169,32 +206,45 @@
 ANY_SPEC = pl.BlockSpec(memory_space=pl.ANY)
 
 
+def part_specs(parts):
+    half = len(parts) // 2
+    return ([ANY_SPEC] * (half - 1) + [VMEM_SPEC]) * 2
+
+
 def weights_of(lists, counts, q, k_parts, first, rows, unroll=4):
-    blocks = sum(part.shape[0] for part in k_parts)
+    whole = not isinstance(k_parts, list)
+    parts = [k_parts] if whole else k_parts
+    sources = 0 if whole else len(parts)
+    blocks = sum(part.shape[0] for part in parts)
     group = (unroll, KMAX // 2, BLOCK, 2 * BLOCK)
+    out_shape = [
+        pltpu.HBM((rows,) + group[1:], BF16),
+        jax.ShapeDtypeStruct((rows, BLOCK, BLOCK), F32),
+    ]
+    scratch = [
+        pltpu.VMEM(group, F32),
+        pltpu.VMEM((2,) + group, BF16),
+        pltpu.SemaphoreType.DMA((2,)),
+    ]
+    out_specs = [pl.BlockSpec(memory_space=pltpu.HBM), VMEM_SPEC]
+    if not whole:
+        out_shape.append(pltpu.VMEM((blocks, BLOCK, HD), BF16))
+        out_specs.append(VMEM_SPEC)
+        scratch.append(pltpu.SemaphoreType.DMA((sources,)))
     return pl.pallas_call(
-        functools.partial(weights_kernel, len(k_parts), unroll, first, rows),
-        in_specs=[SMEM_SPEC, SMEM_SPEC, VMEM_SPEC] + [ANY_SPEC] * len(k_parts),
-        out_specs=[ANY_SPEC, VMEM_SPEC],
-        scratch_shapes=[
-            pltpu.VMEM((blocks, BLOCK, HD), BF16),
-            pltpu.VMEM(group, F32),
-            pltpu.VMEM((2,) + group, BF16),
-            pltpu.SemaphoreType.DMA((len(k_parts),)),
-            pltpu.SemaphoreType.DMA((2,)),
-        ],
-        out_shape=[
-            jax.ShapeDtypeStruct((rows,) + group[1:], BF16),
-            jax.ShapeDtypeStruct((rows, BLOCK, BLOCK), F32),
-        ],
-        compiler_params=pltpu.CompilerParams(vmem_limit_bytes=48 * 2**20),
+        functools.partial(weights_kernel, sources, unroll, first, rows),
+        in_specs=[SMEM_SPEC, SMEM_SPEC, VMEM_SPEC] + ([VMEM_SPEC] if whole else part_specs(parts)),
+        out_specs=out_specs,
+        scratch_shapes=scratch,
+        out_shape=out_shape,
+        compiler_params=pltpu.CompilerParams(vmem_limit_bytes=20 * 2**20),
         cost_estimate=pl.CostEstimate(
             flops=2 * rows * KMAX * BLOCK * BLOCK * HD,
             bytes_accessed=rows * 3 * 2**20,
             transcendentals=rows * KMAX * BLOCK * BLOCK,
         ),
         name="weights",
-    )(lists, counts, q, *k_parts)
+    )(lists, counts, q, *parts)
 
 
 def mix_of(lists, halves, v_parts, unroll=4, slots=4):
@@ -242,7 +292,7 @@
         in_specs=[SMEM_SPEC]
         + [ANY_SPEC] * groups
         + [VMEM_SPEC] * groups
-        + [ANY_SPEC] * len(v_parts),
+        + part_specs(v_parts),
         out_specs=VMEM_SPEC,
         scratch_shapes=[
             pltpu.VMEM((blocks, BLOCK, HD), BF16),
@@ -251,7 +301,7 @@
             pltpu.SemaphoreType.DMA((slots,)),
         ],
         out_shape=jax.ShapeDtypeStruct((rows, BLOCK, HD), BF16),
-        compiler_params=pltpu.CompilerParams(vmem_limit_bytes=48 * 2**20),
+        compiler_params=pltpu.CompilerParams(vmem_limit_bytes=44 * 2**20),
         cost_estimate=pl.CostEstimate(
             flops=2 * rows * KMAX * BLOCK * BLOCK * HD,
             bytes_accessed=rows * 3 * 2**19,
@@ -318,10 +368,8 @@
         key_counts.reshape(frames, parts, halves), part, 1, keepdims=False
     ).reshape(-1)
 
-    (k_rot,) = by_heads(keys_kernel, "rotate_keys", positions, key_proj)
-    q_rot, v_heads = by_heads(
-        others_kernel, "rotate_queries", after(positions, k_rot), query_proj, value_proj
-    )
+    k_rot = keys_by_heads(positions, key_proj)
+    q_rot, v_heads = others_by_heads(after(positions, k_rot), query_proj, value_proj)
 
     k_own = after(heads_out(k_rot), v_heads, mine, counts)
     k_main = ring.along(k_own, 1)
@@ -347,11 +395,11 @@
     first = weights_of(mine, counts, q, k_parts, 0, half)
     v_main, v_opposite = lax.optimization_barrier((v_main, v_opposite, first[1]))[:2]
     v_far = ring.along(v_main, 1)
-    second = weights_of(after(mine, v_main), counts, q, k_parts, half, half)
+    second = weights_of(after(mine, v_main), counts, q, first[2], half, half)
     v_parts = [v_own, v_main, v_opposite, v_far, v_other]
     v_parts += [ring.across(x) for x in (v_main, v_opposite, after(v_far, second[1]))]
     v_parts = [blocks_of(x) for x in v_parts]
-    mixed = mix_of(mine, [first, second], v_parts).reshape(frames, rows, HD)
+    mixed = mix_of(mine, [first[:2], second], v_parts).reshape(frames, rows, HD)
     back = heads_out(mixed)
     return back.transpose(1, 0, 2).reshape(rows, HEADS * HD)
 

time: 155 us -> 152 us (0.981)
  Pallas kernels: 47.5 us -> 43.8 us
  waiting for transfers between devices: 50.6 us -> 54.3 us
  local copies, waits for them, and re-layouts: 10.1 us -> 8.49 us
    ppermute x6, waiting for transfers between devices: 34.8 us -> 38.2 us  [along(): return lax.ppermute(x, 'narrow', steps)]
    pallas_call x4, Pallas kernels: 34.3 us -> 32 us  [the longest x2 24.9 us: weights_of(): pl.pallas_call(functools.partial(weights_kernel, sources, unroll, first,...]
    unnamed x26 -> x14, local copies, waits for them, and re-layouts: 7.79 us -> 6.15 us
  transfers between devices with their start and end apart: 17 -> 17, of which waited for: 7 -> 8; matrix products, arithmetic and copies ran while one was open for 1% -> 1% of each run, Pallas kernels for 21% -> 19%
where the time goes in v4:
time: 152 us; the launch traced here: 151 us
  waiting for transfers between devices  54.3 us (36%)
  Pallas kernels  43.8 us (29%)
  starting transfers between devices  23.4 us (15%)
  blocking collectives  20.5 us (13%)
  local copies, waits for them, and re-layouts  8.49 us (6%)
    ppermute x6, waiting for transfers between devices, along(): return lax.ppermute(x, 'narrow', steps)  38.2 us
    pallas_call x2, Pallas kernels, weights_of(): pl.pallas_call(functools.partial(weights_kernel, sources, unroll, first,...  24.9 us
    all_to_all x1, blocking collectives, heads_out(): return lax.all_to_all(x, 'wide', split_axis=0, concat_axis=0, tiled=True)  20.5 us
    all_to_all x3, starting transfers between devices, heads_out(): return lax.all_to_all(x, 'wide', split_axis=0, concat_axis=0, tiled=True)  14.4 us
    all_to_all x3, waiting for transfers between devices, heads_out(): return lax.all_to_all(x, 'wide', split_axis=0, concat_axis=0, tiled=True)  13.5 us
    pallas_call x1, Pallas kernels, mix_of(): pl.pallas_call(kernel, in_specs=[SMEM_SPEC] + [ANY_SPEC] * groups + [VMEM...  11.7 us
    ppermute x6, starting transfers between devices, along(): return lax.ppermute(x, 'narrow', steps)  8.38 us
    unnamed x14, local copies, waits for them, and re-layouts  6.15 us
  transfers between devices with their start and end apart: 17, of which 8 were waited for; matrix products, arithmetic and copies ran while one was open for 1% of the time, Pallas kernels for 19%

profile of v4, /device:TPU:0, one launch (start us, length us, event | category | flops | bytes accessed | tf_op | source)
XLA Modules:
  0.0 151.4 jit_solution(11755858928451326091)
XLA Ops:
  0.0 3.5 %rotate_keys.1 = bf16[16,256,128]{2,1,0:T(8,128)(2,1)} custom-call(s32[3,256]{1,0:T(4,128)} %pos_ref, bf16[256,2048]{1,0:T(8,128)(2,1)} %k_hbm.1), custom_call_target="tpu_custom_call" | custom-call | tf_op jit(solution)/shard_map/rotate_keys/pallas_call | solution.py:97
  3.5 7.1 %all-to-all-start = ((bf16[16,256,128]{2,1,0:T(8,128)(2,1)}), bf16[16,256,128]{2,1,0:T(8,128)(2,1)S(1)}, u32[]{:S(2)}, u32[]{:S(2)}) async-start(bf16[16,256,128]{2,1,0:T(8,128)(2,1)} %rotate_keys.1), calls=%async_computation | async-start | bytes 2097152 | tf_op jit(solution)/shard_map/all_to_all | solution.py:354
  10.7 0.8 and_add_fusion
  11.8 0.8 reshape.73
  12.7 1.2 copy-done
  13.9 0.7 copy-done.2
  14.6 3.6 %rotate_queries.1 = (bf16[16,256,128]{2,1,0:T(8,128)(2,1)S(1)}, bf16[16,256,128]{2,1,0:T(8,128)(2,1)}) custom-call(s32[3,256]{1,0:T(4,128)S(1)} %copy-done.2, bf16[256,2048]{1,0:T(8,128)(2,1)S(1)} %copy-done, bf16[256,2048]{1,0:T(8,128)(2,1)} %v_ref.1), custom_call_target="tpu_custom_call" | custom-call | tf_op jit(solution)/shard_map/rotate_queries/pallas_call | solution.py:113
  18.2 1.0 copy-done.1
  19.2 9.1 %all-to-all-done = bf16[16,256,128]{2,1,0:T(8,128)(2,1)S(1)} async-done(((bf16[16,256,128]{2,1,0:T(8,128)(2,1)}), bf16[16,256,128]{2,1,0:T(8,128)(2,1)S(1)}, u32[]{:S(2)}, u32[]{:S(2)}) %all-to-all-start) | async-done | bytes 1048608 | tf_op jit(solution)/shard_map/all_to_all | solution.py:354
  28.4 1.9 %collective-permute-start = (bf16[16,256,128]{2,1,0:T(8,128)(2,1)S(1)}, bf16[16,256,128]{2,1,0:T(8,128)(2,1)}, u32[]{:S(2)}, u32[]{:S(2)}) collective-permute-start(bf16[16,256,128]{2,1,0:T(8,128)(2,1)S(1)} %all-to-all-done), channel_id=1, source_target_pairs={{0,2},{1,7},{2,4},{3,1},{4,6},{5,3},{6,0},{7,5},{8,10},{9,15},{10,... | collective-permute-start | bytes 3145736 | tf_op jit(solution)/shard_map/ppermute | solution.py:328
  30.3 3.7 %all-to-all-start.1 = ((bf16[16,256,128]{2,1,0:T(8,128)(2,1)}), bf16[16,256,128]{2,1,0:T(8,128)(2,1)S(1)}, u32[]{:S(2)}, u32[]{:S(2)}) async-start(bf16[16,256,128]{2,1,0:T(8,128)(2,1)} %get-tuple-element.27), calls=%async_computation.1 | async-start | bytes 2097152 | tf_op jit(solution)/shard_map/all_to_all | solution.py:354
  33.9 11.3 %collective-permute-done = bf16[16,256,128]{2,1,0:T(8,128)(2,1)} collective-permute-done((bf16[16,256,128]{2,1,0:T(8,128)(2,1)S(1)}, bf16[16,256,128]{2,1,0:T(8,128)(2,1)}, u32[]{:S(2)}, u32[]{:S(2)}) %collective-permute-start) | collective-permute-done | bytes 1048608 | tf_op jit(solution)/shard_map/ppermute | solution.py:328
  45.3 2.0 %collective-permute-start.2 = (bf16[16,256,128]{2,1,0:T(8,128)(2,1)S(1)}, bf16[16,256,128]{2,1,0:T(8,128)(2,1)}, u32[]{:S(2)}, u32[]{:S(2)}) collective-permute-start(bf16[16,256,128]{2,1,0:T(8,128)(2,1)S(1)} %all-to-all-done), channel_id=1, source_target_pairs={{0,6},{1,3},{2,0},{3,5},{4,2},{5,7},{6,4},{7,1},{8,14},{9,11},{10,... | collective-permute-start | bytes 3145736 | tf_op jit(solution)/shard_map/ppermute | solution.py:328
  47.3 4.3 %all-to-all-done.1 = bf16[16,256,128]{2,1,0:T(8,128)(2,1)S(1)} async-done(((bf16[16,256,128]{2,1,0:T(8,128)(2,1)}), bf16[16,256,128]{2,1,0:T(8,128)(2,1)S(1)}, u32[]{:S(2)}, u32[]{:S(2)}) %all-to-all-start.1) | async-done | bytes 1048608 | tf_op jit(solution)/shard_map/all_to_all | solution.py:354
  51.6 1.0 copy-done.3
  52.6 3.7 %all-to-all-start.2 = ((bf16[16,256,128]{2,1,0:T(8,128)(2,1)}), bf16[16,256,128]{2,1,0:T(8,128)(2,1)S(1)}, u32[]{:S(2)}, u32[]{:S(2)}) async-start(bf16[16,256,128]{2,1,0:T(8,128)(2,1)} %copy-done.1), calls=%async_computation.2 | async-start | bytes 2097152 | tf_op jit(solution)/shard_map/all_to_all | solution.py:354
  56.4 13.3 %collective-permute-done.2 = bf16[16,256,128]{2,1,0:T(8,128)(2,1)} collective-permute-done((bf16[16,256,128]{2,1,0:T(8,128)(2,1)S(1)}, bf16[16,256,128]{2,1,0:T(8,128)(2,1)}, u32[]{:S(2)}, u32[]{:S(2)}) %collective-permute-start.2) | collective-permute-done | bytes 1048608 | tf_op jit(solution)/shard_map/ppermute | solution.py:328
  69.7 2.5 %collective-permute-done.3 = bf16[16,256,128]{2,1,0:T(8,128)(2,1)} collective-permute-done((bf16[16,256,128]{2,1,0:T(8,128)(2,1)}, bf16[16,256,128]{2,1,0:T(8,128)(2,1)}, u32[]{:S(2)}, u32[]{:S(2)}) %collective-permute-start.3) | collective-permute-done | bytes 1048608 | tf_op jit(solution)/shard_map/ppermute | solution.py:328
  72.2 1.7 %collective-permute-start.7 = (bf16[16,256,128]{2,1,0:T(8,128)(2,1)S(1)}, bf16[16,256,128]{2,1,0:T(8,128)(2,1)S(1)}, u32[]{:S(2)}, u32[]{:S(2)}) collective-permute-start(bf16[16,256,128]{2,1,0:T(8,128)(2,1)S(1)} %all-to-all-done.1), channel_id=1, source_target_pairs={{0,2},{1,7},{2,4},{3,1},{4,6},{5,3},{6,0},{7,5},{8,10},{9,15},{10,... | collective-permute-start | bytes 3145736 | tf_op jit(solution)/shard_map/ppermute | solution.py:328
  73.9 1.5 %collective-permute-start.8 = (bf16[16,256,128]{2,1,0:T(8,128)(2,1)S(1)}, bf16[16,256,128]{2,1,0:T(8,128)(2,1)S(1)}, u32[]{:S(2)}, u32[]{:S(2)}) collective-permute-start(bf16[16,256,128]{2,1,0:T(8,128)(2,1)S(1)} %all-to-all-done.1), channel_id=1, source_target_pairs={{0,6},{1,3},{2,0},{3,5},{4,2},{5,7},{6,4},{7,1},{8,14},{9,11},{10,... | collective-permute-start | bytes 3145736 | tf_op jit(solution)/shard_map/ppermute | solution.py:328
  75.4 1.2 copy-done.4
  76.7 13.9 %weights.2 = (bf16[16,12,128,256]{3,2,1,0:T(8,128)(2,1)}, f32[16,128,128]{2,1,0:T(8,128)S(1)}, bf16[256,128,128]{2,1,0:T(8,128)(2,1)S(1)}) custom-call(s32[768]{0:T(1024)S(1)} %reshape.72.lists_ref, s32[32]{0:T(128)S(1)} %reshape.74.counts_ref, bf16[32,128,128]{2,1,0:T(8,128)(2,1)S(1)} %bitcast.32, bf16[32,128,128]{2,1,0:T(8,128)(2,1)S(1)} %bitcast.31, ...), custom_call_target="tpu_custom_call" | custom-call | flops 1610612736 | bytes 50331648 | tf_op jit(solution)/shard_map/weights/pallas_call | solution.py:234
  90.6 7.8 %collective-permute-done.7 = bf16[16,256,128]{2,1,0:T(8,128)(2,1)S(1)} collective-permute-done((bf16[16,256,128]{2,1,0:T(8,128)(2,1)S(1)}, bf16[16,256,128]{2,1,0:T(8,128)(2,1)S(1)}, u32[]{:S(2)}, u32[]{:S(2)}) %collective-permute-start.7) | collective-permute-done | bytes 1048608 | tf_op jit(solution)/shard_map/ppermute | solution.py:328
  98.4 1.2 collective-permute-start.9
  99.6 0.5 collective-permute-start.11
  100.1 11.0 %weights.3 = (bf16[16,12,128,256]{3,2,1,0:T(8,128)(2,1)}, f32[16,128,128]{2,1,0:T(8,128)S(1)}) custom-call(s32[768]{0:T(1024)S(1)} %reshape.72.lists_ref, s32[32]{0:T(128)S(1)} %reshape.74.counts_ref, bf16[32,128,128]{2,1,0:T(8,128)(2,1)S(1)} %bitcast.33, bf16[256,128,128]{2,1,0:T(8,128)(2,1)S(1)} %get-tuple-element.36.refs_0_), custom_call_target="tpu_custom_call" | custom-call | flops 1610612736 | bytes 50331648 | tf_op jit(solution)/shard_map/weights/pallas_call | solution.py:234
  111.0 3.3 %collective-permute-done.9 = bf16[16,256,128]{2,1,0:T(8,128)(2,1)S(1)} collective-permute-done((bf16[16,256,128]{2,1,0:T(8,128)(2,1)S(1)}, bf16[16,256,128]{2,1,0:T(8,128)(2,1)S(1)}, u32[]{:S(2)}, u32[]{:S(2)}) %collective-permute-start.9) | collective-permute-done | bytes 1048608 | tf_op jit(solution)/shard_map/ppermute | solution.py:328
  114.4 2.6 %collective-permute-done.13 = bf16[16,256,128]{2,1,0:T(8,128)(2,1)S(1)} collective-permute-done((bf16[16,256,128]{2,1,0:T(8,128)(2,1)S(1)}, bf16[16,256,128]{2,1,0:T(8,128)(2,1)S(1)}, u32[]{:S(2)}, u32[]{:S(2)}) %collective-permute-start.13) | collective-permute-done | bytes 1048608 | tf_op jit(solution)/shard_map/ppermute | solution.py:331
  117.0 1.1 copy-done.6
  118.1 11.7 %mix.1 = bf16[32,128,128]{2,1,0:T(8,128)(2,1)S(1)} custom-call(s32[768]{0:T(1024)S(1)} %reshape.72.lists_ref, bf16[16,12,128,256]{3,2,1,0:T(8,128)(2,1)} %get-tuple-element.31.refs_0_, bf16[16,12,128,256]{3,2,1,0:T(8,128)(2,1)} %get-tuple-element.37.refs_1_, f32[16,128,128]{2,1,0:T(8,128)S(1)} %get-tuple-element.33.refs_2_, ...), custom_call_target="tpu_custom_call" | custom-call | flops 3221225472 | bytes 50331648 | tf_op jit(solution)/shard_map/mix/pallas_call | solution.py:290
  129.8 20.5 %all_to_all.20 = bf16[16,256,128]{2,1,0:T(8,128)(2,1)S(1)} all-to-all(bf16[16,256,128]{2,1,0:T(8,128)(2,1)S(1)} %bitcast.25), channel_id=1, replica_groups=mesh['wide'=16,'narrow'=8] {'wide'}, dimensions={0} | all-to-all | bytes 2097152 | tf_op jit(solution)/shard_map/all_to_all | solution.py:354
  150.3 1.1 copy_bitcast_fusion
  (31 shorter events, 0.6 us)
Async XLA Ops:
  3.5 24.8 %all-to-all-start = ((bf16[16,256,128]{2,1,0:T(8,128)(2,1)}), bf16[16,256,128]{2,1,0:T(8,128)(2,1)S(1)}, u32[]{:S(2)}, u32[]{:S(2)}) async-start(bf16[16,256,128]{2,1,0:T(8,128)(2,1)} %rotate_keys.1), calls=%async_computation | async-start | bytes 2097152 | tf_op jit(solution)/shard_map/all_to_all | solution.py:354
  12.7 1.2 copy-start
  13.9 0.7 copy-start.2
  18.2 1.0 copy-start.1
  28.4 16.9 %collective-permute-start = (bf16[16,256,128]{2,1,0:T(8,128)(2,1)S(1)}, bf16[16,256,128]{2,1,0:T(8,128)(2,1)}, u32[]{:S(2)}, u32[]{:S(2)}) collective-permute-start(bf16[16,256,128]{2,1,0:T(8,128)(2,1)S(1)} %all-to-all-done), channel_id=1, source_target_pairs={{0,2},{1,7},{2,4},{3,1},{4,6},{5,3},{6,0},{7,5},{8,10},{9,15},{10,... | collective-permute-start | bytes 3145736 | tf_op jit(solution)/shard_map/ppermute | solution.py:328
  30.3 21.3 %all-to-all-start.1 = ((bf16[16,256,128]{2,1,0:T(8,128)(2,1)}), bf16[16,256,128]{2,1,0:T(8,128)(2,1)S(1)}, u32[]{:S(2)}, u32[]{:S(2)}) async-start(bf16[16,256,128]{2,1,0:T(8,128)(2,1)} %get-tuple-element.27), calls=%async_computation.1 | async-start | bytes 2097152 | tf_op jit(solution)/shard_map/all_to_all | solution.py:354
  45.3 6.3 %collective-permute-start.1 = (bf16[16,256,128]{2,1,0:T(8,128)(2,1)}, bf16[16,256,128]{2,1,0:T(8,128)(2,1)S(1)}, u32[]{:S(2)}, u32[]{:S(2)}) collective-permute-start(bf16[16,256,128]{2,1,0:T(8,128)(2,1)} %collective-permute-done), channel_id=1, source_target_pairs={{0,1},{1,0},{2,3},{3,2},{4,5},{5,4},{6,7},{7,6},{8,9},{9,8},{10,11... | collective-permute-start | bytes 3145736 | tf_op jit(solution)/shard_map/ppermute | solution.py:331
  45.3 24.4 %collective-permute-start.2 = (bf16[16,256,128]{2,1,0:T(8,128)(2,1)S(1)}, bf16[16,256,128]{2,1,0:T(8,128)(2,1)}, u32[]{:S(2)}, u32[]{:S(2)}) collective-permute-start(bf16[16,256,128]{2,1,0:T(8,128)(2,1)S(1)} %all-to-all-done), channel_id=1, source_target_pairs={{0,6},{1,3},{2,0},{3,5},{4,2},{5,7},{6,4},{7,1},{8,14},{9,11},{10,... | collective-permute-start | bytes 3145736 | tf_op jit(solution)/shard_map/ppermute | solution.py:328
  51.6 20.6 %collective-permute-start.3 = (bf16[16,256,128]{2,1,0:T(8,128)(2,1)}, bf16[16,256,128]{2,1,0:T(8,128)(2,1)}, u32[]{:S(2)}, u32[]{:S(2)}) collective-permute-start(bf16[16,256,128]{2,1,0:T(8,128)(2,1)} %collective-permute-done), channel_id=1, source_target_pairs={{0,2},{1,7},{2,4},{3,1},{4,6},{5,3},{6,0},{7,5},{8,10},{9,15},{10,... | collective-permute-start | bytes 3145736 | tf_op jit(solution)/shard_map/ppermute | solution.py:328
  51.6 1.0 copy-start.3
  52.6 19.6 %all-to-all-start.2 = ((bf16[16,256,128]{2,1,0:T(8,128)(2,1)}), bf16[16,256,128]{2,1,0:T(8,128)(2,1)S(1)}, u32[]{:S(2)}, u32[]{:S(2)}) async-start(bf16[16,256,128]{2,1,0:T(8,128)(2,1)} %copy-done.1), calls=%async_computation.2 | async-start | bytes 2097152 | tf_op jit(solution)/shard_map/all_to_all | solution.py:354
  56.3 19.2 %collective-permute-start.4 = (bf16[16,256,128]{2,1,0:T(8,128)(2,1)S(1)}, bf16[16,256,128]{2,1,0:T(8,128)(2,1)}, u32[]{:S(2)}, u32[]{:S(2)}) collective-permute-start(bf16[16,256,128]{2,1,0:T(8,128)(2,1)S(1)} %all-to-all-done), channel_id=1, source_target_pairs={{0,1},{1,0},{2,3},{3,2},{4,5},{5,4},{6,7},{7,6},{8,9},{9,8},{10,11... | collective-permute-start | bytes 3145736 | tf_op jit(solution)/shard_map/ppermute | solution.py:331
  69.7 5.8 %collective-permute-start.5 = (bf16[16,256,128]{2,1,0:T(8,128)(2,1)}, bf16[16,256,128]{2,1,0:T(8,128)(2,1)}, u32[]{:S(2)}, u32[]{:S(2)}) collective-permute-start(bf16[16,256,128]{2,1,0:T(8,128)(2,1)} %collective-permute-done.2), channel_id=1, source_target_pairs={{0,1},{1,0},{2,3},{3,2},{4,5},{5,4},{6,7},{7,6},{8,9},{9,8},{10,11... | collective-permute-start | bytes 3145736 | tf_op jit(solution)/shard_map/ppermute | solution.py:331
  72.2 3.3 %collective-permute-start.6 = (bf16[16,256,128]{2,1,0:T(8,128)(2,1)}, bf16[16,256,128]{2,1,0:T(8,128)(2,1)S(1)}, u32[]{:S(2)}, u32[]{:S(2)}) collective-permute-start(bf16[16,256,128]{2,1,0:T(8,128)(2,1)} %collective-permute-done.3), channel_id=1, source_target_pairs={{0,1},{1,0},{2,3},{3,2},{4,5},{5,4},{6,7},{7,6},{8,9},{9,8},{10,11... | collective-permute-start | bytes 3145736 | tf_op jit(solution)/shard_map/ppermute | solution.py:331
  72.2 26.2 %collective-permute-start.7 = (bf16[16,256,128]{2,1,0:T(8,128)(2,1)S(1)}, bf16[16,256,128]{2,1,0:T(8,128)(2,1)S(1)}, u32[]{:S(2)}, u32[]{:S(2)}) collective-permute-start(bf16[16,256,128]{2,1,0:T(8,128)(2,1)S(1)} %all-to-all-done.1), channel_id=1, source_target_pairs={{0,2},{1,7},{2,4},{3,1},{4,6},{5,3},{6,0},{7,5},{8,10},{9,15},{10,... | collective-permute-start | bytes 3145736 | tf_op jit(solution)/shard_map/ppermute | solution.py:328
  73.9 24.5 %collective-permute-start.8 = (bf16[16,256,128]{2,1,0:T(8,128)(2,1)S(1)}, bf16[16,256,128]{2,1,0:T(8,128)(2,1)S(1)}, u32[]{:S(2)}, u32[]{:S(2)}) collective-permute-start(bf16[16,256,128]{2,1,0:T(8,128)(2,1)S(1)} %all-to-all-done.1), channel_id=1, source_target_pairs={{0,6},{1,3},{2,0},{3,5},{4,2},{5,7},{6,4},{7,1},{8,14},{9,11},{10,... | collective-permute-start | bytes 3145736 | tf_op jit(solution)/shard_map/ppermute | solution.py:328
  75.4 1.2 copy-start.4
  98.4 16.0 %collective-permute-start.9 = (bf16[16,256,128]{2,1,0:T(8,128)(2,1)S(1)}, bf16[16,256,128]{2,1,0:T(8,128)(2,1)S(1)}, u32[]{:S(2)}, u32[]{:S(2)}) collective-permute-start(bf16[16,256,128]{2,1,0:T(8,128)(2,1)S(1)} %collective-permute-done.7), channel_id=1, source_target_pairs={{0,2},{1,7},{2,4},{3,1},{4,6},{5,3},{6,0},{7,5},{8,10},{9,15},{10,... | collective-permute-start | bytes 3145736 | tf_op jit(solution)/shard_map/ppermute | solution.py:328
  99.6 14.8 %collective-permute-start.10 = (bf16[16,256,128]{2,1,0:T(8,128)(2,1)S(1)}, bf16[16,256,128]{2,1,0:T(8,128)(2,1)S(1)}, u32[]{:S(2)}, u32[]{:S(2)}) collective-permute-start(bf16[16,256,128]{2,1,0:T(8,128)(2,1)S(1)} %all-to-all-done.1), channel_id=1, source_target_pairs={{0,1},{1,0},{2,3},{3,2},{4,5},{5,4},{6,7},{7,6},{8,9},{9,8},{10,11... | collective-permute-start | bytes 3145736 | tf_op jit(solution)/shard_map/ppermute | solution.py:331
  99.6 14.8 %collective-permute-start.11 = (bf16[16,256,128]{2,1,0:T(8,128)(2,1)S(1)}, bf16[16,256,128]{2,1,0:T(8,128)(2,1)S(1)}, u32[]{:S(2)}, u32[]{:S(2)}) collective-permute-start(bf16[16,256,128]{2,1,0:T(8,128)(2,1)S(1)} %collective-permute-done.7), channel_id=1, source_target_pairs={{0,1},{1,0},{2,3},{3,2},{4,5},{5,4},{6,7},{7,6},{8,9},{9,8},{10,11... | collective-permute-start | bytes 3145736 | tf_op jit(solution)/shard_map/ppermute | solution.py:331
  100.1 14.3 %collective-permute-start.12 = (bf16[16,256,128]{2,1,0:T(8,128)(2,1)S(1)}, bf16[16,256,128]{2,1,0:T(8,128)(2,1)S(1)}, u32[]{:S(2)}, u32[]{:S(2)}) collective-permute-start(bf16[16,256,128]{2,1,0:T(8,128)(2,1)S(1)} %collective-permute-done.8), channel_id=1, source_target_pairs={{0,1},{1,0},{2,3},{3,2},{4,5},{5,4},{6,7},{7,6},{8,9},{9,8},{10,11... | collective-permute-start | bytes 3145736 | tf_op jit(solution)/shard_map/ppermute | solution.py:331
  114.4 2.7 %collective-permute-start.13 = (bf16[16,256,128]{2,1,0:T(8,128)(2,1)S(1)}, bf16[16,256,128]{2,1,0:T(8,128)(2,1)S(1)}, u32[]{:S(2)}, u32[]{:S(2)}) collective-permute-start(bf16[16,256,128]{2,1,0:T(8,128)(2,1)S(1)} %collective-permute-done.9), channel_id=1, source_target_pairs={{0,1},{1,0},{2,3},{3,2},{4,5},{5,4},{6,7},{7,6},{8,9},{9,8},{10,11... | collective-permute-start | bytes 3145736 | tf_op jit(solution)/shard_map/ppermute | solution.py:331
  114.4 2.6 %copy-start.5 = (bf16[16,256,128]{2,1,0:T(8,128)(2,1)}, bf16[16,256,128]{2,1,0:T(8,128)(2,1)S(1)}, u32[]{:S(2)}) copy-start(bf16[16,256,128]{2,1,0:T(8,128)(2,1)S(1)} %collective-permute-done.12) | copy-start | bytes 3145732
  117.0 1.1 copy-start.6

commit v5 on v4

--- a/solution.py
+++ b/solution.py
@@ -247,18 +247,48 @@
     )(lists, counts, q, *parts)
 
 
-def mix_of(lists, halves, v_parts, unroll=4, slots=4):
+def near_values(v_parts):
+    blocks = sum(part.shape[0] for part in v_parts)
+    size = v_parts[0].shape[0]
+    far = len(v_parts) // 2 - 1
+    near = [n for n in range(len(v_parts)) if n % (far + 1) != far]
+
+    def kernel(*refs):
+        parts, whole, sems = refs[: len(near)], refs[-2], refs[-1]
+        copies = [
+            pltpu.make_async_copy(part, whole.at[pl.ds(n * size, size)], sems.at[at])
+            for at, (n, part) in enumerate(zip(near, parts))
+        ]
+        for copy in copies:
+            copy.start()
+        for copy in copies:
+            copy.wait()
+
+    return pl.pallas_call(
+        kernel,
+        in_specs=[ANY_SPEC] * len(near),
+        out_specs=VMEM_SPEC,
+        scratch_shapes=[pltpu.SemaphoreType.DMA((len(near),))],
+        out_shape=pltpu.VMEM((blocks, BLOCK, HD), BF16),
+        compiler_params=pltpu.CompilerParams(vmem_limit_bytes=10 * 2**20),
+        cost_estimate=pl.CostEstimate(flops=0, bytes_accessed=12 * 2**20, transcendentals=0),
+        name="near_values",
+    )(*[v_parts[n] for n in near])
+
+
+def mix_of(lists, halves, v_near, v_parts, unroll=4, slots=4):
     groups = len(halves)
     group_rows = halves[0][0].shape[0]
     rows = groups * group_rows
     turns = rows // unroll
-    blocks = sum(part.shape[0] for part in v_parts)
+    size = v_parts[0].shape[0]
+    places = [len(v_parts) * 2 - 1, len(v_parts) * 4 - 1]
 
     def kernel(lists_ref, *refs):
         weights_refs = refs[:groups]
         inverse_refs = refs[groups : 2 * groups]
-        v_refs = refs[2 * groups : 2 * groups + len(v_parts)]
-        out_ref, v_ref, w_ref, sems, w_sems = refs[2 * groups + len(v_parts) :]
+        v_refs = refs[2 * groups + 1 : 2 * groups + 1 + len(v_parts)]
+        out_ref, v_ref, w_ref, sems, w_sems = refs[2 * groups + 1 + len(v_parts) :]
 
         def fetch(turn):
             group, at = divmod(turn * unroll, group_rows)
@@ -268,7 +298,14 @@
             )
 
         fetch(0).start()
-        load_blocks(v_refs, v_ref, sems, [fetch(n) for n in range(1, slots - 1)])
+        copies = [
+            pltpu.make_async_copy(part, v_ref.at[pl.ds(n * size, size)], sems.at[at])
+            for at, (n, part) in enumerate(zip(places, v_refs))
+        ]
+        for copy in copies + [fetch(n) for n in range(1, slots - 1)]:
+            copy.start()
+        for copy in copies:
+            copy.wait()
         for turn in range(turns):
             fetch(turn).wait()
             if turn + slots - 1 < turns:
@@ -292,23 +329,23 @@
         in_specs=[SMEM_SPEC]
         + [ANY_SPEC] * groups
         + [VMEM_SPEC] * groups
-        + part_specs(v_parts),
-        out_specs=VMEM_SPEC,
+        + [VMEM_SPEC] * (1 + len(v_parts)),
+        out_specs=[VMEM_SPEC, VMEM_SPEC],
+        input_output_aliases={1 + 2 * groups: 1},
         scratch_shapes=[
-            pltpu.VMEM((blocks, BLOCK, HD), BF16),
             pltpu.VMEM((slots, unroll, KMAX // 2, BLOCK, 2 * BLOCK), BF16),
             pltpu.SemaphoreType.DMA((len(v_parts),)),
             pltpu.SemaphoreType.DMA((slots,)),
         ],
-        out_shape=jax.ShapeDtypeStruct((rows, BLOCK, HD), BF16),
-        compiler_params=pltpu.CompilerParams(vmem_limit_bytes=44 * 2**20),
+        out_shape=[jax.ShapeDtypeStruct((rows, BLOCK, HD), BF16), pltpu.VMEM(v_near.shape, BF16)],
+        compiler_params=pltpu.CompilerParams(vmem_limit_bytes=26 * 2**20),
         cost_estimate=pl.CostEstimate(
             flops=2 * rows * KMAX * BLOCK * BLOCK * HD,
             bytes_accessed=rows * 3 * 2**19,
             transcendentals=0,
         ),
         name="mix",
-    )(lists, *[w for w, _ in halves], *[i for _, i in halves], *v_parts)
+    )(lists, *[w for w, _ in halves], *[i for _, i in halves], v_near, *v_parts)[0]
 
 
 def after(x, *others):
@@ -399,7 +436,9 @@
     v_parts = [v_own, v_main, v_opposite, v_far, v_other]
     v_parts += [ring.across(x) for x in (v_main, v_opposite, after(v_far, second[1]))]
     v_parts = [blocks_of(x) for x in v_parts]
-    mixed = mix_of(mine, [first[:2], second], v_parts).reshape(frames, rows, HD)
+    v_near = near_values([after(v_parts[0], second[1])] + v_parts[1:])
+    mixed = mix_of(mine, [first[:2], second], v_near, [v_parts[3], v_parts[7]])
+    mixed = mixed.reshape(frames, rows, HD)
     back = heads_out(mixed)
     return back.transpose(1, 0, 2).reshape(rows, HEADS * HD)
 

time: 152 us -> 151 us (level)
  waiting for transfers between devices: 54.3 us -> 51.9 us
  local copies, waits for them, and re-layouts: 8.49 us -> 10.4 us
    unnamed x14 -> x24, local copies, waits for them, and re-layouts: 6.15 us -> 8.07 us
    ppermute x8, starting transfers between devices: 0.61 us -> 2.5 us  [across(): lax.ppermute(x, 'narrow', [(n, n ^ 1) for n in range(2 * self.chips)])]
    pallas_call x1, Pallas kernels: 11.7 us -> 9.95 us  [mix_of(): pl.pallas_call(kernel, in_specs=[SMEM_SPEC] + [ANY_SPEC] * groups + [VMEM...]
    ppermute x6, starting transfers between devices: 8.38 us -> 6.77 us  [along(): return lax.ppermute(x, 'narrow', steps)]
  transfers between devices with their start and end apart: 17 -> 17, of which waited for: 8 -> 10; matrix products, arithmetic and copies ran while one was open for 1% -> 1% of each run, Pallas kernels for 19% -> 19%
where the time goes in v5:
time: 151 us; the launch traced here: 150 us
  waiting for transfers between devices  51.9 us (34%)
  Pallas kernels  42.5 us (28%)
  starting transfers between devices  23.7 us (16%)
  blocking collectives  20.8 us (14%)
  local copies, waits for them, and re-layouts  10.4 us (7%)
    ppermute x6, waiting for transfers between devices, along(): return lax.ppermute(x, 'narrow', steps)  37 us
    pallas_call x2, Pallas kernels, weights_of(): pl.pallas_call(functools.partial(weights_kernel, sources, unroll, first,...  24.9 us
    all_to_all x1, blocking collectives, heads_out(): return lax.all_to_all(x, 'wide', split_axis=0, concat_axis=0, tiled=True)  20.8 us
    all_to_all x3, starting transfers between devices, heads_out(): return lax.all_to_all(x, 'wide', split_axis=0, concat_axis=0, tiled=True)  14.4 us
    all_to_all x3, waiting for transfers between devices, heads_out(): return lax.all_to_all(x, 'wide', split_axis=0, concat_axis=0, tiled=True)  13.5 us
    pallas_call x1, Pallas kernels, mix_of(): pl.pallas_call(kernel, in_specs=[SMEM_SPEC] + [ANY_SPEC] * groups + [VMEM...  9.95 us
    unnamed x24, local copies, waits for them, and re-layouts  8.07 us
    ppermute x6, starting transfers between devices, along(): return lax.ppermute(x, 'narrow', steps)  6.77 us
  transfers between devices with their start and end apart: 17, of which 10 were waited for; matrix products, arithmetic and copies ran while one was open for 1% of the time, Pallas kernels for 19%

profile of v5, /device:TPU:0, one launch (start us, length us, event | category | flops | bytes accessed | tf_op | source)
XLA Modules:
  0.0 150.3 jit_solution(1783706677730969054)
XLA Ops:
  0.0 3.5 %rotate_keys.1 = bf16[16,256,128]{2,1,0:T(8,128)(2,1)} custom-call(s32[3,256]{1,0:T(4,128)} %pos_ref, bf16[256,2048]{1,0:T(8,128)(2,1)} %k_hbm.1), custom_call_target="tpu_custom_call" | custom-call | tf_op jit(solution)/shard_map/rotate_keys/pallas_call | solution.py:97
  3.5 7.1 %all-to-all-start = ((bf16[16,256,128]{2,1,0:T(8,128)(2,1)}), bf16[16,256,128]{2,1,0:T(8,128)(2,1)S(1)}, u32[]{:S(2)}, u32[]{:S(2)}) async-start(bf16[16,256,128]{2,1,0:T(8,128)(2,1)} %rotate_keys.1), calls=%async_computation | async-start | bytes 2097152 | tf_op jit(solution)/shard_map/all_to_all | solution.py:391
  10.7 0.8 reshape.73
  11.6 0.8 and_add_fusion
  12.7 1.2 copy-done.4
  14.6 3.6 %rotate_queries.1 = (bf16[16,256,128]{2,1,0:T(8,128)(2,1)S(1)}, bf16[16,256,128]{2,1,0:T(8,128)(2,1)}) custom-call(s32[3,256]{1,0:T(4,128)S(1)} %copy-done.6, bf16[256,2048]{1,0:T(8,128)(2,1)S(1)} %copy-done.4, bf16[256,2048]{1,0:T(8,128)(2,1)} %v_ref.1), custom_call_target="tpu_custom_call" | custom-call | tf_op jit(solution)/shard_map/rotate_queries/pallas_call | solution.py:113
  18.2 1.0 copy-done.5
  19.2 9.2 %all-to-all-done = bf16[16,256,128]{2,1,0:T(8,128)(2,1)S(1)} async-done(((bf16[16,256,128]{2,1,0:T(8,128)(2,1)}), bf16[16,256,128]{2,1,0:T(8,128)(2,1)S(1)}, u32[]{:S(2)}, u32[]{:S(2)}) %all-to-all-start) | async-done | bytes 1048608 | tf_op jit(solution)/shard_map/all_to_all | solution.py:391
  28.4 1.9 %collective-permute-start = (bf16[16,256,128]{2,1,0:T(8,128)(2,1)S(1)}, bf16[16,256,128]{2,1,0:T(8,128)(2,1)}, u32[]{:S(2)}, u32[]{:S(2)}) collective-permute-start(bf16[16,256,128]{2,1,0:T(8,128)(2,1)S(1)} %all-to-all-done), channel_id=1, source_target_pairs={{0,2},{1,7},{2,4},{3,1},{4,6},{5,3},{6,0},{7,5},{8,10},{9,15},{10,... | collective-permute-start | bytes 3145736 | tf_op jit(solution)/shard_map/ppermute | solution.py:365
  30.3 3.7 %all-to-all-start.1 = ((bf16[16,256,128]{2,1,0:T(8,128)(2,1)}), bf16[16,256,128]{2,1,0:T(8,128)(2,1)S(1)}, u32[]{:S(2)}, u32[]{:S(2)}) async-start(bf16[16,256,128]{2,1,0:T(8,128)(2,1)} %get-tuple-element.29), calls=%async_computation.1 | async-start | bytes 2097152 | tf_op jit(solution)/shard_map/all_to_all | solution.py:391
  33.9 11.3 %collective-permute-done = bf16[16,256,128]{2,1,0:T(8,128)(2,1)} collective-permute-done((bf16[16,256,128]{2,1,0:T(8,128)(2,1)S(1)}, bf16[16,256,128]{2,1,0:T(8,128)(2,1)}, u32[]{:S(2)}, u32[]{:S(2)}) %collective-permute-start) | collective-permute-done | bytes 1048608 | tf_op jit(solution)/shard_map/ppermute | solution.py:365
  45.3 2.0 %collective-permute-start.2 = (bf16[16,256,128]{2,1,0:T(8,128)(2,1)S(1)}, bf16[16,256,128]{2,1,0:T(8,128)(2,1)}, u32[]{:S(2)}, u32[]{:S(2)}) collective-permute-start(bf16[16,256,128]{2,1,0:T(8,128)(2,1)S(1)} %all-to-all-done), channel_id=1, source_target_pairs={{0,6},{1,3},{2,0},{3,5},{4,2},{5,7},{6,4},{7,1},{8,14},{9,11},{10,... | collective-permute-start | bytes 3145736 | tf_op jit(solution)/shard_map/ppermute | solution.py:365
  47.3 4.3 %all-to-all-done.1 = bf16[16,256,128]{2,1,0:T(8,128)(2,1)S(1)} async-done(((bf16[16,256,128]{2,1,0:T(8,128)(2,1)}), bf16[16,256,128]{2,1,0:T(8,128)(2,1)S(1)}, u32[]{:S(2)}, u32[]{:S(2)}) %all-to-all-start.1) | async-done | bytes 1048608 | tf_op jit(solution)/shard_map/all_to_all | solution.py:391
  51.6 1.0 copy-done.7
  52.6 3.7 %all-to-all-start.2 = ((bf16[16,256,128]{2,1,0:T(8,128)(2,1)}), bf16[16,256,128]{2,1,0:T(8,128)(2,1)S(1)}, u32[]{:S(2)}, u32[]{:S(2)}) async-start(bf16[16,256,128]{2,1,0:T(8,128)(2,1)} %copy-done.5), calls=%async_computation.2 | async-start | bytes 2097152 | tf_op jit(solution)/shard_map/all_to_all | solution.py:391
  56.4 13.3 %collective-permute-done.2 = bf16[16,256,128]{2,1,0:T(8,128)(2,1)} collective-permute-done((bf16[16,256,128]{2,1,0:T(8,128)(2,1)S(1)}, bf16[16,256,128]{2,1,0:T(8,128)(2,1)}, u32[]{:S(2)}, u32[]{:S(2)}) %collective-permute-start.2) | collective-permute-done | bytes 1048608 | tf_op jit(solution)/shard_map/ppermute | solution.py:365
  69.7 2.5 %collective-permute-done.3 = bf16[16,256,128]{2,1,0:T(8,128)(2,1)} collective-permute-done((bf16[16,256,128]{2,1,0:T(8,128)(2,1)}, bf16[16,256,128]{2,1,0:T(8,128)(2,1)}, u32[]{:S(2)}, u32[]{:S(2)}) %collective-permute-start.3) | collective-permute-done | bytes 1048608 | tf_op jit(solution)/shard_map/ppermute | solution.py:365
  72.2 2.3 %collective-permute-start.8 = (bf16[16,256,128]{2,1,0:T(8,128)(2,1)S(1)}, bf16[16,256,128]{2,1,0:T(8,128)(2,1)S(1)}, u32[]{:S(2)}, u32[]{:S(2)}) collective-permute-start(bf16[16,256,128]{2,1,0:T(8,128)(2,1)S(1)} %all-to-all-done.1), channel_id=1, source_target_pairs={{0,6},{1,3},{2,0},{3,5},{4,2},{5,7},{6,4},{7,1},{8,14},{9,11},{10,... | collective-permute-start | bytes 3145736 | tf_op jit(solution)/shard_map/ppermute | solution.py:365
  75.1 1.2 copy-done.8
  76.3 13.9 %weights.2 = (bf16[16,12,128,256]{3,2,1,0:T(8,128)(2,1)}, f32[16,128,128]{2,1,0:T(8,128)S(1)}, bf16[256,128,128]{2,1,0:T(8,128)(2,1)S(1)}) custom-call(s32[768]{0:T(1024)S(1)} %reshape.72.lists_ref, s32[32]{0:T(128)S(1)} %reshape.74.counts_ref, bf16[32,128,128]{2,1,0:T(8,128)(2,1)S(1)} %bitcast.35, bf16[32,128,128]{2,1,0:T(8,128)(2,1)S(1)} %bitcast.34, ...), custom_call_target="tpu_custom_call" | custom-call | flops 1610612736 | bytes 50331648 | tf_op jit(solution)/shard_map/weights/pallas_call | solution.py:234
  90.2 1.0 copy-done.2
  91.2 6.7 %collective-permute-done.8 = bf16[16,256,128]{2,1,0:T(8,128)(2,1)S(1)} collective-permute-done((bf16[16,256,128]{2,1,0:T(8,128)(2,1)S(1)}, bf16[16,256,128]{2,1,0:T(8,128)(2,1)S(1)}, u32[]{:S(2)}, u32[]{:S(2)}) %collective-permute-start.8) | collective-permute-done | bytes 1048608 | tf_op jit(solution)/shard_map/ppermute | solution.py:365
  97.8 1.1 collective-permute-done.7
  99.5 1.9 %collective-permute-start.9 = (bf16[16,256,128]{2,1,0:T(8,128)(2,1)S(1)}, bf16[16,256,128]{2,1,0:T(8,128)(2,1)S(1)}, u32[]{:S(2)}, u32[]{:S(2)}) collective-permute-start(bf16[16,256,128]{2,1,0:T(8,128)(2,1)S(1)} %all-to-all-done.1), channel_id=1, source_target_pairs={{0,1},{1,0},{2,3},{3,2},{4,5},{5,4},{6,7},{7,6},{8,9},{9,8},{10,11... | collective-permute-start | bytes 3145736 | tf_op jit(solution)/shard_map/ppermute | solution.py:368
  101.9 11.0 %weights.3 = (bf16[16,12,128,256]{3,2,1,0:T(8,128)(2,1)}, f32[16,128,128]{2,1,0:T(8,128)S(1)}) custom-call(s32[768]{0:T(1024)S(1)} %reshape.72.lists_ref, s32[32]{0:T(128)S(1)} %reshape.74.counts_ref, bf16[32,128,128]{2,1,0:T(8,128)(2,1)S(1)} %bitcast.36, bf16[256,128,128]{2,1,0:T(8,128)(2,1)S(1)} %get-tuple-element.38.refs_0_), custom_call_target="tpu_custom_call" | custom-call | flops 1610612736 | bytes 50331648 | tf_op jit(solution)/shard_map/weights/pallas_call | solution.py:234
  112.9 2.1 %collective-permute-done.12 = bf16[16,256,128]{2,1,0:T(8,128)(2,1)S(1)} collective-permute-done((bf16[16,256,128]{2,1,0:T(8,128)(2,1)S(1)}, bf16[16,256,128]{2,1,0:T(8,128)(2,1)S(1)}, u32[]{:S(2)}, u32[]{:S(2)}) %collective-permute-start.12) | collective-permute-done | bytes 1048608 | tf_op jit(solution)/shard_map/ppermute | solution.py:365
  115.0 1.2 copy-done.1
  116.7 0.9 collective-permute-done.13
  117.6 0.8 slice-done.2
  118.4 10.0 %mix.1 = (bf16[32,128,128]{2,1,0:T(8,128)(2,1)S(1)}, bf16[256,128,128]{2,1,0:T(8,128)(2,1)S(1)}) custom-call(s32[768]{0:T(1024)S(1)} %reshape.72.lists_ref, bf16[16,12,128,256]{3,2,1,0:T(8,128)(2,1)S(1)} %bitcast.25, bf16[16,12,128,256]{3,2,1,0:T(8,128)(2,1)} %get-tuple-element.39.refs_1_, ...), custom_call_target="tpu_custom_call", output_to_operand_aliasing={{1}: (5, {})} | custom-call | flops 3221225472 | bytes 50331648 | tf_op jit(solution)/shard_map/mix/pallas_call | solution.py:327
  128.4 20.8 %all_to_all.20 = bf16[16,256,128]{2,1,0:T(8,128)(2,1)S(1)} all-to-all(bf16[16,256,128]{2,1,0:T(8,128)(2,1)S(1)} %bitcast.37), channel_id=1, replica_groups=mesh['wide'=16,'narrow'=8] {'wide'}, dimensions={0} | all-to-all | bytes 2097152 | tf_op jit(solution)/shard_map/all_to_all | solution.py:391
  149.2 1.1 copy_bitcast_fusion
  (43 shorter events, 3.3 us)
Async XLA Ops:
  3.5 24.8 %all-to-all-start = ((bf16[16,256,128]{2,1,0:T(8,128)(2,1)}), bf16[16,256,128]{2,1,0:T(8,128)(2,1)S(1)}, u32[]{:S(2)}, u32[]{:S(2)}) async-start(bf16[16,256,128]{2,1,0:T(8,128)(2,1)} %rotate_keys.1), calls=%async_computation | async-start | bytes 2097152 | tf_op jit(solution)/shard_map/all_to_all | solution.py:391
  12.7 1.2 copy-start.4
  13.9 0.7 copy-start.6
  18.2 1.0 copy-start.5
  28.4 16.9 %collective-permute-start = (bf16[16,256,128]{2,1,0:T(8,128)(2,1)S(1)}, bf16[16,256,128]{2,1,0:T(8,128)(2,1)}, u32[]{:S(2)}, u32[]{:S(2)}) collective-permute-start(bf16[16,256,128]{2,1,0:T(8,128)(2,1)S(1)} %all-to-all-done), channel_id=1, source_target_pairs={{0,2},{1,7},{2,4},{3,1},{4,6},{5,3},{6,0},{7,5},{8,10},{9,15},{10,... | collective-permute-start | bytes 3145736 | tf_op jit(solution)/shard_map/ppermute | solution.py:365
  30.3 21.3 %all-to-all-start.1 = ((bf16[16,256,128]{2,1,0:T(8,128)(2,1)}), bf16[16,256,128]{2,1,0:T(8,128)(2,1)S(1)}, u32[]{:S(2)}, u32[]{:S(2)}) async-start(bf16[16,256,128]{2,1,0:T(8,128)(2,1)} %get-tuple-element.29), calls=%async_computation.1 | async-start | bytes 2097152 | tf_op jit(solution)/shard_map/all_to_all | solution.py:391
  45.3 6.3 %collective-permute-start.1 = (bf16[16,256,128]{2,1,0:T(8,128)(2,1)}, bf16[16,256,128]{2,1,0:T(8,128)(2,1)S(1)}, u32[]{:S(2)}, u32[]{:S(2)}) collective-permute-start(bf16[16,256,128]{2,1,0:T(8,128)(2,1)} %collective-permute-done), channel_id=1, source_target_pairs={{0,1},{1,0},{2,3},{3,2},{4,5},{5,4},{6,7},{7,6},{8,9},{9,8},{10,11... | collective-permute-start | bytes 3145736 | tf_op jit(solution)/shard_map/ppermute | solution.py:368
  45.3 24.4 %collective-permute-start.2 = (bf16[16,256,128]{2,1,0:T(8,128)(2,1)S(1)}, bf16[16,256,128]{2,1,0:T(8,128)(2,1)}, u32[]{:S(2)}, u32[]{:S(2)}) collective-permute-start(bf16[16,256,128]{2,1,0:T(8,128)(2,1)S(1)} %all-to-all-done), channel_id=1, source_target_pairs={{0,6},{1,3},{2,0},{3,5},{4,2},{5,7},{6,4},{7,1},{8,14},{9,11},{10,... | collective-permute-start | bytes 3145736 | tf_op jit(solution)/shard_map/ppermute | solution.py:365
  51.6 61.3 %copy-start = (bf16[16,256,128]{2,1,0:T(8,128)(2,1)}, bf16[16,256,128]{2,1,0:T(8,128)(2,1)S(1)}, u32[]{:S(2)}) copy-start(bf16[16,256,128]{2,1,0:T(8,128)(2,1)S(1)} %all-to-all-done.1) | copy-start | bytes 3145732
  51.6 20.6 %collective-permute-start.3 = (bf16[16,256,128]{2,1,0:T(8,128)(2,1)}, bf16[16,256,128]{2,1,0:T(8,128)(2,1)}, u32[]{:S(2)}, u32[]{:S(2)}) collective-permute-start(bf16[16,256,128]{2,1,0:T(8,128)(2,1)} %collective-permute-done), channel_id=1, source_target_pairs={{0,2},{1,7},{2,4},{3,1},{4,6},{5,3},{6,0},{7,5},{8,10},{9,15},{10,... | collective-permute-start | bytes 3145736 | tf_op jit(solution)/shard_map/ppermute | solution.py:365
  51.6 1.0 copy-start.7
  52.6 19.5 %all-to-all-start.2 = ((bf16[16,256,128]{2,1,0:T(8,128)(2,1)}), bf16[16,256,128]{2,1,0:T(8,128)(2,1)S(1)}, u32[]{:S(2)}, u32[]{:S(2)}) async-start(bf16[16,256,128]{2,1,0:T(8,128)(2,1)} %copy-done.5), calls=%async_computation.2 | async-start | bytes 2097152 | tf_op jit(solution)/shard_map/all_to_all | solution.py:391
  56.3 18.2 %collective-permute-start.4 = (bf16[16,256,128]{2,1,0:T(8,128)(2,1)S(1)}, bf16[16,256,128]{2,1,0:T(8,128)(2,1)}, u32[]{:S(2)}, u32[]{:S(2)}) collective-permute-start(bf16[16,256,128]{2,1,0:T(8,128)(2,1)S(1)} %all-to-all-done), channel_id=1, source_target_pairs={{0,1},{1,0},{2,3},{3,2},{4,5},{5,4},{6,7},{7,6},{8,9},{9,8},{10,11... | collective-permute-start | bytes 3145736 | tf_op jit(solution)/shard_map/ppermute | solution.py:368
  69.7 4.8 %collective-permute-start.5 = (bf16[16,256,128]{2,1,0:T(8,128)(2,1)}, bf16[16,256,128]{2,1,0:T(8,128)(2,1)}, u32[]{:S(2)}, u32[]{:S(2)}) collective-permute-start(bf16[16,256,128]{2,1,0:T(8,128)(2,1)} %collective-permute-done.2), channel_id=1, source_target_pairs={{0,1},{1,0},{2,3},{3,2},{4,5},{5,4},{6,7},{7,6},{8,9},{9,8},{10,11... | collective-permute-start | bytes 3145736 | tf_op jit(solution)/shard_map/ppermute | solution.py:368
  72.2 2.9 %collective-permute-start.6 = (bf16[16,256,128]{2,1,0:T(8,128)(2,1)}, bf16[16,256,128]{2,1,0:T(8,128)(2,1)S(1)}, u32[]{:S(2)}, u32[]{:S(2)}) collective-permute-start(bf16[16,256,128]{2,1,0:T(8,128)(2,1)} %collective-permute-done.3), channel_id=1, source_target_pairs={{0,1},{1,0},{2,3},{3,2},{4,5},{5,4},{6,7},{7,6},{8,9},{9,8},{10,11... | collective-permute-start | bytes 3145736 | tf_op jit(solution)/shard_map/ppermute | solution.py:368
  72.2 25.7 %collective-permute-start.8 = (bf16[16,256,128]{2,1,0:T(8,128)(2,1)S(1)}, bf16[16,256,128]{2,1,0:T(8,128)(2,1)S(1)}, u32[]{:S(2)}, u32[]{:S(2)}) collective-permute-start(bf16[16,256,128]{2,1,0:T(8,128)(2,1)S(1)} %all-to-all-done.1), channel_id=1, source_target_pairs={{0,6},{1,3},{2,0},{3,5},{4,2},{5,7},{6,4},{7,1},{8,14},{9,11},{10,... | collective-permute-start | bytes 3145736 | tf_op jit(solution)/shard_map/ppermute | solution.py:365
  74.5 24.5 %collective-permute-start.7 = (bf16[16,256,128]{2,1,0:T(8,128)(2,1)S(1)}, bf16[16,256,128]{2,1,0:T(8,128)(2,1)S(1)}, u32[]{:S(2)}, u32[]{:S(2)}) collective-permute-start(bf16[16,256,128]{2,1,0:T(8,128)(2,1)S(1)} %all-to-all-done.1), channel_id=1, source_target_pairs={{0,2},{1,7},{2,4},{3,1},{4,6},{5,3},{6,0},{7,5},{8,10},{9,15},{10,... | collective-permute-start | bytes 3145736 | tf_op jit(solution)/shard_map/ppermute | solution.py:365
  75.1 1.2 copy-start.8
  90.2 1.0 copy-start.2
  99.0 16.0 %collective-permute-start.12 = (bf16[16,256,128]{2,1,0:T(8,128)(2,1)S(1)}, bf16[16,256,128]{2,1,0:T(8,128)(2,1)S(1)}, u32[]{:S(2)}, u32[]{:S(2)}) collective-permute-start(bf16[16,256,128]{2,1,0:T(8,128)(2,1)S(1)} %collective-permute-done.7), channel_id=1, source_target_pairs={{0,2},{1,7},{2,4},{3,1},{4,6},{5,3},{6,0},{7,5},{8,10},{9,15},{10,... | collective-permute-start | bytes 3145736 | tf_op jit(solution)/shard_map/ppermute | solution.py:365
  99.5 15.5 %collective-permute-start.9 = (bf16[16,256,128]{2,1,0:T(8,128)(2,1)S(1)}, bf16[16,256,128]{2,1,0:T(8,128)(2,1)S(1)}, u32[]{:S(2)}, u32[]{:S(2)}) collective-permute-start(bf16[16,256,128]{2,1,0:T(8,128)(2,1)S(1)} %all-to-all-done.1), channel_id=1, source_target_pairs={{0,1},{1,0},{2,3},{3,2},{4,5},{5,4},{6,7},{7,6},{8,9},{9,8},{10,11... | collective-permute-start | bytes 3145736 | tf_op jit(solution)/shard_map/ppermute | solution.py:368
  101.4 13.6 %collective-permute-start.10 = (bf16[16,256,128]{2,1,0:T(8,128)(2,1)S(1)}, bf16[16,256,128]{2,1,0:T(8,128)(2,1)S(1)}, u32[]{:S(2)}, u32[]{:S(2)}) collective-permute-start(bf16[16,256,128]{2,1,0:T(8,128)(2,1)S(1)} %collective-permute-done.7), channel_id=1, source_target_pairs={{0,1},{1,0},{2,3},{3,2},{4,5},{5,4},{6,7},{7,6},{8,9},{9,8},{10,11... | collective-permute-start | bytes 3145736 | tf_op jit(solution)/shard_map/ppermute | solution.py:368
  101.4 13.6 %collective-permute-start.11 = (bf16[16,256,128]{2,1,0:T(8,128)(2,1)S(1)}, bf16[16,256,128]{2,1,0:T(8,128)(2,1)S(1)}, u32[]{:S(2)}, u32[]{:S(2)}) collective-permute-start(bf16[16,256,128]{2,1,0:T(8,128)(2,1)S(1)} %collective-permute-done.8), channel_id=1, source_target_pairs={{0,1},{1,0},{2,3},{3,2},{4,5},{5,4},{6,7},{7,6},{8,9},{9,8},{10,11... | collective-permute-start | bytes 3145736 | tf_op jit(solution)/shard_map/ppermute | solution.py:368
  101.9 15.8 %slice-start = ((s8[12582912]{0:T(1024)(128)(4,1)}), s8[4194304]{0:T(1024)(128)(4,1)S(1)}, s32[]{:S(2)}) async-start(s8[12582912]{0:T(1024)(128)(4,1)} %bitcast.24), calls=%async_computation.4 | async-start | bytes 8388608
  101.9 15.8 %slice-start.1 = ((s8[12582912]{0:T(1024)(128)(4,1)}), s8[4194304]{0:T(1024)(128)(4,1)S(1)}, s32[]{:S(2)}) async-start(s8[12582912]{0:T(1024)(128)(4,1)} %bitcast.24), calls=%async_computation.5 | async-start | bytes 8388608
  101.9 15.8 %copy-start.3 = (f32[16,128,128]{2,1,0:T(8,128)S(1)}, f32[16,128,128]{2,1,0:T(8,128)}, u32[]{:S(2)}) copy-start(f32[16,128,128]{2,1,0:T(8,128)} %copy-done.2) | copy-start | bytes 3145732
  115.0 2.7 %collective-permute-start.13 = (bf16[16,256,128]{2,1,0:T(8,128)(2,1)S(1)}, bf16[16,256,128]{2,1,0:T(8,128)(2,1)S(1)}, u32[]{:S(2)}, u32[]{:S(2)}) collective-permute-start(bf16[16,256,128]{2,1,0:T(8,128)(2,1)S(1)} %collective-permute-done.12), channel_id=1, source_target_pairs={{0,1},{1,0},{2,3},{3,2},{4,5},{5,4},{6,7},{7,6},{8,9},{9,8},{10,11... | collective-permute-start | bytes 3145736 | tf_op jit(solution)/shard_map/ppermute | solution.py:368
  115.0 1.2 copy-start.1
  116.2 2.2 %slice-start.2 = ((s8[12582912]{0:T(1024)(128)(4,1)}), s8[4194304]{0:T(1024)(128)(4,1)S(1)}, s32[]{:S(2)}) async-start(s8[12582912]{0:T(1024)(128)(4,1)} %bitcast.24), calls=%async_computation.6 | async-start | bytes 8388608

commit v6 on v5

--- a/solution.py
+++ b/solution.py
@@ -278,8 +278,8 @@
 
 def mix_of(lists, halves, v_near, v_parts, unroll=4, slots=4):
     groups = len(halves)
-    group_rows = halves[0][0].shape[0]
-    rows = groups * group_rows
+    rows = sum(weights.shape[0] for weights, _ in halves)
+    places_of = [(n, at) for n in range(groups) for at in range(halves[n][0].shape[0])]
     turns = rows // unroll
     size = v_parts[0].shape[0]
     places = [len(v_parts) * 2 - 1, len(v_parts) * 4 - 1]
@@ -291,7 +291,7 @@
         out_ref, v_ref, w_ref, sems, w_sems = refs[2 * groups + 1 + len(v_parts) :]
 
         def fetch(turn):
-            group, at = divmod(turn * unroll, group_rows)
+            group, at = places_of[turn * unroll]
             slot = turn % slots
             return pltpu.make_async_copy(
                 weights_refs[group].at[pl.ds(at, unroll)], w_ref.at[slot], w_sems.at[slot]
@@ -312,7 +312,7 @@
                 fetch(turn + slots - 1).start()
             for n in range(unroll):
                 row = turn * unroll + n
-                group, at = divmod(row, group_rows)
+                group, at = places_of[row]
                 mixed = None
                 for pair in range(KMAX // 2):
                     product = lax.dot_general(
@@ -428,11 +428,12 @@
     v_opposite = ring.along(v_ring, -1)
     v_other = ring.across(v_ring)
 
-    half = frames * halves // 2
-    first = weights_of(mine, counts, q, k_parts, 0, half)
-    v_main, v_opposite = lax.optimization_barrier((v_main, v_opposite, first[1]))[:2]
+    early = frames * halves * 5 // 8
+    late = frames * halves - early
+    first = weights_of(mine, counts, q, k_parts, 0, early)
+    v_main = after(v_main, first[1])
     v_far = ring.along(v_main, 1)
-    second = weights_of(after(mine, v_main), counts, q, first[2], half, half)
+    second = weights_of(after(mine, v_main), counts, q, first[2], early, late)
     v_parts = [v_own, v_main, v_opposite, v_far, v_other]
     v_parts += [ring.across(x) for x in (v_main, v_opposite, after(v_far, second[1]))]
     v_parts = [blocks_of(x) for x in v_parts]

time: 151 us -> 151 us (level)
  local copies, waits for them, and re-layouts: 10.4 us -> 7.44 us
  waiting for transfers between devices: 51.9 us -> 53.9 us
    unnamed x24 -> x12, local copies, waits for them, and re-layouts: 8.07 us -> 5.1 us
    ppermute x8, starting transfers between devices: 2.5 us -> 0.61 us  [across(): lax.ppermute(x, 'narrow', [(n, n ^ 1) for n in range(2 * self.chips)])]
    ppermute x6, starting transfers between devices: 6.77 us -> 8.38 us  [along(): return lax.ppermute(x, 'narrow', steps)]
    pallas_call x1, Pallas kernels: 9.95 us -> 11.5 us  [mix_of(): pl.pallas_call(kernel, in_specs=[SMEM_SPEC] + [ANY_SPEC] * groups + [VMEM...]
  transfers between devices with their start and end apart: 17 -> 17, of which waited for: 10 -> 8; matrix products, arithmetic and copies ran while one was open for 1% -> 1% of each run, Pallas kernels for 19% -> 19%
where the time goes in v6:
time: 151 us; the launch traced here: 150 us
  waiting for transfers between devices  53.9 us (36%)
  Pallas kernels  43.9 us (29%)
  starting transfers between devices  23.4 us (15%)
  blocking collectives  20.5 us (14%)
  local copies, waits for them, and re-layouts  7.44 us (5%)
    ppermute x6, waiting for transfers between devices, along(): return lax.ppermute(x, 'narrow', steps)  38.3 us
    pallas_call x2, Pallas kernels, weights_of(): pl.pallas_call(functools.partial(weights_kernel, sources, unroll, first,...  24.8 us
    all_to_all x1, blocking collectives, heads_out(): return lax.all_to_all(x, 'wide', split_axis=0, concat_axis=0, tiled=True)  20.5 us
    all_to_all x3, starting transfers between devices, heads_out(): return lax.all_to_all(x, 'wide', split_axis=0, concat_axis=0, tiled=True)  14.4 us
    all_to_all x3, waiting for transfers between devices, heads_out(): return lax.all_to_all(x, 'wide', split_axis=0, concat_axis=0, tiled=True)  13.4 us
    pallas_call x1, Pallas kernels, mix_of(): pl.pallas_call(kernel, in_specs=[SMEM_SPEC] + [ANY_SPEC] * groups + [VMEM...  11.5 us
    ppermute x6, starting transfers between devices, along(): return lax.ppermute(x, 'narrow', steps)  8.38 us
    unnamed x12, local copies, waits for them, and re-layouts  5.1 us
  transfers between devices with their start and end apart: 17, of which 8 were waited for; matrix products, arithmetic and copies ran while one was open for 1% of the time, Pallas kernels for 19%

profile of v6, /device:TPU:0, one launch (start us, length us, event | category | flops | bytes accessed | tf_op | source)
XLA Modules:
  0.0 150.1 jit_solution(2993422815343349494)
XLA Ops:
  0.0 3.5 %rotate_keys.1 = bf16[16,256,128]{2,1,0:T(8,128)(2,1)} custom-call(s32[3,256]{1,0:T(4,128)} %pos_ref, bf16[256,2048]{1,0:T(8,128)(2,1)} %k_hbm.1), custom_call_target="tpu_custom_call" | custom-call | tf_op jit(solution)/shard_map/rotate_keys/pallas_call | solution.py:97
  3.5 7.1 %all-to-all-start = ((bf16[16,256,128]{2,1,0:T(8,128)(2,1)}), bf16[16,256,128]{2,1,0:T(8,128)(2,1)S(1)}, u32[]{:S(2)}, u32[]{:S(2)}) async-start(bf16[16,256,128]{2,1,0:T(8,128)(2,1)} %rotate_keys.1), calls=%async_computation | async-start | bytes 2097152 | tf_op jit(solution)/shard_map/all_to_all | solution.py:391
  10.7 0.8 reshape.73
  11.6 0.8 and_add_fusion
  12.7 1.2 copy-done.1
  13.9 0.7 copy-done.3
  14.6 3.6 %rotate_queries.1 = (bf16[16,256,128]{2,1,0:T(8,128)(2,1)S(1)}, bf16[16,256,128]{2,1,0:T(8,128)(2,1)}) custom-call(s32[3,256]{1,0:T(4,128)S(1)} %copy-done.3, bf16[256,2048]{1,0:T(8,128)(2,1)S(1)} %copy-done.1, bf16[256,2048]{1,0:T(8,128)(2,1)} %v_ref.1), custom_call_target="tpu_custom_call" | custom-call | tf_op jit(solution)/shard_map/rotate_queries/pallas_call | solution.py:113
  18.2 1.0 copy-done.2
  19.2 9.1 %all-to-all-done = bf16[16,256,128]{2,1,0:T(8,128)(2,1)S(1)} async-done(((bf16[16,256,128]{2,1,0:T(8,128)(2,1)}), bf16[16,256,128]{2,1,0:T(8,128)(2,1)S(1)}, u32[]{:S(2)}, u32[]{:S(2)}) %all-to-all-start) | async-done | bytes 1048608 | tf_op jit(solution)/shard_map/all_to_all | solution.py:391
  28.4 1.9 %collective-permute-start = (bf16[16,256,128]{2,1,0:T(8,128)(2,1)S(1)}, bf16[16,256,128]{2,1,0:T(8,128)(2,1)}, u32[]{:S(2)}, u32[]{:S(2)}) collective-permute-start(bf16[16,256,128]{2,1,0:T(8,128)(2,1)S(1)} %all-to-all-done), channel_id=1, source_target_pairs={{0,2},{1,7},{2,4},{3,1},{4,6},{5,3},{6,0},{7,5},{8,10},{9,15},{10,... | collective-permute-start | bytes 3145736 | tf_op jit(solution)/shard_map/ppermute | solution.py:365
  30.3 3.7 %all-to-all-start.1 = ((bf16[16,256,128]{2,1,0:T(8,128)(2,1)}), bf16[16,256,128]{2,1,0:T(8,128)(2,1)S(1)}, u32[]{:S(2)}, u32[]{:S(2)}) async-start(bf16[16,256,128]{2,1,0:T(8,128)(2,1)} %get-tuple-element.28), calls=%async_computation.1 | async-start | bytes 2097152 | tf_op jit(solution)/shard_map/all_to_all | solution.py:391
  33.9 11.3 %collective-permute-done = bf16[16,256,128]{2,1,0:T(8,128)(2,1)} collective-permute-done((bf16[16,256,128]{2,1,0:T(8,128)(2,1)S(1)}, bf16[16,256,128]{2,1,0:T(8,128)(2,1)}, u32[]{:S(2)}, u32[]{:S(2)}) %collective-permute-start) | collective-permute-done | bytes 1048608 | tf_op jit(solution)/shard_map/ppermute | solution.py:365
  45.3 2.0 %collective-permute-start.2 = (bf16[16,256,128]{2,1,0:T(8,128)(2,1)S(1)}, bf16[16,256,128]{2,1,0:T(8,128)(2,1)}, u32[]{:S(2)}, u32[]{:S(2)}) collective-permute-start(bf16[16,256,128]{2,1,0:T(8,128)(2,1)S(1)} %all-to-all-done), channel_id=1, source_target_pairs={{0,6},{1,3},{2,0},{3,5},{4,2},{5,7},{6,4},{7,1},{8,14},{9,11},{10,... | collective-permute-start | bytes 3145736 | tf_op jit(solution)/shard_map/ppermute | solution.py:365
  47.3 4.3 %all-to-all-done.1 = bf16[16,256,128]{2,1,0:T(8,128)(2,1)S(1)} async-done(((bf16[16,256,128]{2,1,0:T(8,128)(2,1)}), bf16[16,256,128]{2,1,0:T(8,128)(2,1)S(1)}, u32[]{:S(2)}, u32[]{:S(2)}) %all-to-all-start.1) | async-done | bytes 1048608 | tf_op jit(solution)/shard_map/all_to_all | solution.py:391
  51.6 1.0 copy-done.4
  52.6 3.7 %all-to-all-start.2 = ((bf16[16,256,128]{2,1,0:T(8,128)(2,1)}), bf16[16,256,128]{2,1,0:T(8,128)(2,1)S(1)}, u32[]{:S(2)}, u32[]{:S(2)}) async-start(bf16[16,256,128]{2,1,0:T(8,128)(2,1)} %copy-done.2), calls=%async_computation.2 | async-start | bytes 2097152 | tf_op jit(solution)/shard_map/all_to_all | solution.py:391
  56.4 13.3 %collective-permute-done.2 = bf16[16,256,128]{2,1,0:T(8,128)(2,1)} collective-permute-done((bf16[16,256,128]{2,1,0:T(8,128)(2,1)S(1)}, bf16[16,256,128]{2,1,0:T(8,128)(2,1)}, u32[]{:S(2)}, u32[]{:S(2)}) %collective-permute-start.2) | collective-permute-done | bytes 1048608 | tf_op jit(solution)/shard_map/ppermute | solution.py:365
  69.7 2.5 %collective-permute-done.3 = bf16[16,256,128]{2,1,0:T(8,128)(2,1)} collective-permute-done((bf16[16,256,128]{2,1,0:T(8,128)(2,1)}, bf16[16,256,128]{2,1,0:T(8,128)(2,1)}, u32[]{:S(2)}, u32[]{:S(2)}) %collective-permute-start.3) | collective-permute-done | bytes 1048608 | tf_op jit(solution)/shard_map/ppermute | solution.py:365
  72.2 1.7 %collective-permute-start.7 = (bf16[16,256,128]{2,1,0:T(8,128)(2,1)S(1)}, bf16[16,256,128]{2,1,0:T(8,128)(2,1)S(1)}, u32[]{:S(2)}, u32[]{:S(2)}) collective-permute-start(bf16[16,256,128]{2,1,0:T(8,128)(2,1)S(1)} %all-to-all-done.1), channel_id=1, source_target_pairs={{0,2},{1,7},{2,4},{3,1},{4,6},{5,3},{6,0},{7,5},{8,10},{9,15},{10,... | collective-permute-start | bytes 3145736 | tf_op jit(solution)/shard_map/ppermute | solution.py:365
  73.9 1.5 %collective-permute-start.8 = (bf16[16,256,128]{2,1,0:T(8,128)(2,1)S(1)}, bf16[16,256,128]{2,1,0:T(8,128)(2,1)S(1)}, u32[]{:S(2)}, u32[]{:S(2)}) collective-permute-start(bf16[16,256,128]{2,1,0:T(8,128)(2,1)S(1)} %all-to-all-done.1), channel_id=1, source_target_pairs={{0,6},{1,3},{2,0},{3,5},{4,2},{5,7},{6,4},{7,1},{8,14},{9,11},{10,... | collective-permute-start | bytes 3145736 | tf_op jit(solution)/shard_map/ppermute | solution.py:365
  75.4 1.2 copy-done.5
  76.7 16.1 %weights.2 = (bf16[20,12,128,256]{3,2,1,0:T(8,128)(2,1)}, f32[20,128,128]{2,1,0:T(8,128)S(1)}, bf16[256,128,128]{2,1,0:T(8,128)(2,1)S(1)}) custom-call(s32[768]{0:T(1024)S(1)} %reshape.72.lists_ref, s32[32]{0:T(128)S(1)} %reshape.74.counts_ref, bf16[32,128,128]{2,1,0:T(8,128)(2,1)S(1)} %bitcast.25, bf16[32,128,128]{2,1,0:T(8,128)(2,1)S(1)} %bitcast.34, ...), custom_call_target="tpu_custom_call" | custom-call | flops 2013265920 | bytes 62914560 | tf_op jit(solution)/shard_map/weights/pallas_call | solution.py:234
  92.7 5.6 %collective-permute-done.7 = bf16[16,256,128]{2,1,0:T(8,128)(2,1)S(1)} collective-permute-done((bf16[16,256,128]{2,1,0:T(8,128)(2,1)S(1)}, bf16[16,256,128]{2,1,0:T(8,128)(2,1)S(1)}, u32[]{:S(2)}, u32[]{:S(2)}) %collective-permute-start.7) | collective-permute-done | bytes 1048608 | tf_op jit(solution)/shard_map/ppermute | solution.py:365
  98.4 1.2 collective-permute-start.12
  99.6 0.5 collective-permute-start.11
  100.1 8.8 %weights.3 = (bf16[12,12,128,256]{3,2,1,0:T(8,128)(2,1)}, f32[12,128,128]{2,1,0:T(8,128)S(1)}) custom-call(s32[768]{0:T(1024)S(1)} %reshape.72.lists_ref, s32[32]{0:T(128)S(1)} %reshape.74.counts_ref, bf16[32,128,128]{2,1,0:T(8,128)(2,1)S(1)} %bitcast.26, bf16[256,128,128]{2,1,0:T(8,128)(2,1)S(1)} %get-tuple-element.37.refs_0_), custom_call_target="tpu_custom_call" | custom-call | flops 1207959552 | bytes 37748736 | tf_op jit(solution)/shard_map/weights/pallas_call | solution.py:234
  108.9 5.5 %collective-permute-done.12 = bf16[16,256,128]{2,1,0:T(8,128)(2,1)S(1)} collective-permute-done((bf16[16,256,128]{2,1,0:T(8,128)(2,1)S(1)}, bf16[16,256,128]{2,1,0:T(8,128)(2,1)S(1)}, u32[]{:S(2)}, u32[]{:S(2)}) %collective-permute-start.12) | collective-permute-done | bytes 1048608 | tf_op jit(solution)/shard_map/ppermute | solution.py:365
  114.4 0.5 near_values.1.refs_4_
  114.9 2.1 %collective-permute-done.13 = bf16[16,256,128]{2,1,0:T(8,128)(2,1)S(1)} collective-permute-done((bf16[16,256,128]{2,1,0:T(8,128)(2,1)S(1)}, bf16[16,256,128]{2,1,0:T(8,128)(2,1)S(1)}, u32[]{:S(2)}, u32[]{:S(2)}) %collective-permute-start.13) | collective-permute-done | bytes 1048608 | tf_op jit(solution)/shard_map/ppermute | solution.py:368
  117.0 11.5 %mix.1 = (bf16[32,128,128]{2,1,0:T(8,128)(2,1)S(1)}, bf16[256,128,128]{2,1,0:T(8,128)(2,1)S(1)}) custom-call(s32[768]{0:T(1024)S(1)} %reshape.72.lists_ref, bf16[20,12,128,256]{3,2,1,0:T(8,128)(2,1)} %get-tuple-element.32.refs_0_, bf16[12,12,128,256]{3,2,1,0:T(8,128)(2,1)S(1)} %copy-done, ...), custom_call_target="tpu_custom_call", output_to_operand_aliasing={{1}: (5, {})} | custom-call | flops 3221225472 | bytes 50331648 | tf_op jit(solution)/shard_map/mix/pallas_call | solution.py:327
  128.5 20.5 %all_to_all.20 = bf16[16,256,128]{2,1,0:T(8,128)(2,1)S(1)} all-to-all(bf16[16,256,128]{2,1,0:T(8,128)(2,1)S(1)} %bitcast.35), channel_id=1, replica_groups=mesh['wide'=16,'narrow'=8] {'wide'}, dimensions={0} | all-to-all | bytes 2097152 | tf_op jit(solution)/shard_map/all_to_all | solution.py:391
  149.0 1.1 copy_bitcast_fusion
  (30 shorter events, 0.5 us)
Async XLA Ops:
  3.5 24.8 %all-to-all-start = ((bf16[16,256,128]{2,1,0:T(8,128)(2,1)}), bf16[16,256,128]{2,1,0:T(8,128)(2,1)S(1)}, u32[]{:S(2)}, u32[]{:S(2)}) async-start(bf16[16,256,128]{2,1,0:T(8,128)(2,1)} %rotate_keys.1), calls=%async_computation | async-start | bytes 2097152 | tf_op jit(solution)/shard_map/all_to_all | solution.py:391
  12.7 1.2 copy-start.1
  13.9 0.7 copy-start.3
  18.2 1.0 copy-start.2
  28.4 16.9 %collective-permute-start = (bf16[16,256,128]{2,1,0:T(8,128)(2,1)S(1)}, bf16[16,256,128]{2,1,0:T(8,128)(2,1)}, u32[]{:S(2)}, u32[]{:S(2)}) collective-permute-start(bf16[16,256,128]{2,1,0:T(8,128)(2,1)S(1)} %all-to-all-done), channel_id=1, source_target_pairs={{0,2},{1,7},{2,4},{3,1},{4,6},{5,3},{6,0},{7,5},{8,10},{9,15},{10,... | collective-permute-start | bytes 3145736 | tf_op jit(solution)/shard_map/ppermute | solution.py:365
  30.3 21.3 %all-to-all-start.1 = ((bf16[16,256,128]{2,1,0:T(8,128)(2,1)}), bf16[16,256,128]{2,1,0:T(8,128)(2,1)S(1)}, u32[]{:S(2)}, u32[]{:S(2)}) async-start(bf16[16,256,128]{2,1,0:T(8,128)(2,1)} %get-tuple-element.28), calls=%async_computation.1 | async-start | bytes 2097152 | tf_op jit(solution)/shard_map/all_to_all | solution.py:391
  45.3 6.3 %collective-permute-start.1 = (bf16[16,256,128]{2,1,0:T(8,128)(2,1)}, bf16[16,256,128]{2,1,0:T(8,128)(2,1)S(1)}, u32[]{:S(2)}, u32[]{:S(2)}) collective-permute-start(bf16[16,256,128]{2,1,0:T(8,128)(2,1)} %collective-permute-done), channel_id=1, source_target_pairs={{0,1},{1,0},{2,3},{3,2},{4,5},{5,4},{6,7},{7,6},{8,9},{9,8},{10,11... | collective-permute-start | bytes 3145736 | tf_op jit(solution)/shard_map/ppermute | solution.py:368
  45.3 24.4 %collective-permute-start.2 = (bf16[16,256,128]{2,1,0:T(8,128)(2,1)S(1)}, bf16[16,256,128]{2,1,0:T(8,128)(2,1)}, u32[]{:S(2)}, u32[]{:S(2)}) collective-permute-start(bf16[16,256,128]{2,1,0:T(8,128)(2,1)S(1)} %all-to-all-done), channel_id=1, source_target_pairs={{0,6},{1,3},{2,0},{3,5},{4,2},{5,7},{6,4},{7,1},{8,14},{9,11},{10,... | collective-permute-start | bytes 3145736 | tf_op jit(solution)/shard_map/ppermute | solution.py:365
  51.6 20.6 %collective-permute-start.3 = (bf16[16,256,128]{2,1,0:T(8,128)(2,1)}, bf16[16,256,128]{2,1,0:T(8,128)(2,1)}, u32[]{:S(2)}, u32[]{:S(2)}) collective-permute-start(bf16[16,256,128]{2,1,0:T(8,128)(2,1)} %collective-permute-done), channel_id=1, source_target_pairs={{0,2},{1,7},{2,4},{3,1},{4,6},{5,3},{6,0},{7,5},{8,10},{9,15},{10,... | collective-permute-start | bytes 3145736 | tf_op jit(solution)/shard_map/ppermute | solution.py:365
  51.6 1.0 copy-start.4
  52.6 19.6 %all-to-all-start.2 = ((bf16[16,256,128]{2,1,0:T(8,128)(2,1)}), bf16[16,256,128]{2,1,0:T(8,128)(2,1)S(1)}, u32[]{:S(2)}, u32[]{:S(2)}) async-start(bf16[16,256,128]{2,1,0:T(8,128)(2,1)} %copy-done.2), calls=%async_computation.2 | async-start | bytes 2097152 | tf_op jit(solution)/shard_map/all_to_all | solution.py:391
  56.3 19.2 %collective-permute-start.4 = (bf16[16,256,128]{2,1,0:T(8,128)(2,1)S(1)}, bf16[16,256,128]{2,1,0:T(8,128)(2,1)}, u32[]{:S(2)}, u32[]{:S(2)}) collective-permute-start(bf16[16,256,128]{2,1,0:T(8,128)(2,1)S(1)} %all-to-all-done), channel_id=1, source_target_pairs={{0,1},{1,0},{2,3},{3,2},{4,5},{5,4},{6,7},{7,6},{8,9},{9,8},{10,11... | collective-permute-start | bytes 3145736 | tf_op jit(solution)/shard_map/ppermute | solution.py:368
  69.7 5.8 %collective-permute-start.5 = (bf16[16,256,128]{2,1,0:T(8,128)(2,1)}, bf16[16,256,128]{2,1,0:T(8,128)(2,1)}, u32[]{:S(2)}, u32[]{:S(2)}) collective-permute-start(bf16[16,256,128]{2,1,0:T(8,128)(2,1)} %collective-permute-done.2), channel_id=1, source_target_pairs={{0,1},{1,0},{2,3},{3,2},{4,5},{5,4},{6,7},{7,6},{8,9},{9,8},{10,11... | collective-permute-start | bytes 3145736 | tf_op jit(solution)/shard_map/ppermute | solution.py:368
  72.2 3.3 %collective-permute-start.6 = (bf16[16,256,128]{2,1,0:T(8,128)(2,1)}, bf16[16,256,128]{2,1,0:T(8,128)(2,1)S(1)}, u32[]{:S(2)}, u32[]{:S(2)}) collective-permute-start(bf16[16,256,128]{2,1,0:T(8,128)(2,1)} %collective-permute-done.3), channel_id=1, source_target_pairs={{0,1},{1,0},{2,3},{3,2},{4,5},{5,4},{6,7},{7,6},{8,9},{9,8},{10,11... | collective-permute-start | bytes 3145736 | tf_op jit(solution)/shard_map/ppermute | solution.py:368
  72.2 26.2 %collective-permute-start.7 = (bf16[16,256,128]{2,1,0:T(8,128)(2,1)S(1)}, bf16[16,256,128]{2,1,0:T(8,128)(2,1)S(1)}, u32[]{:S(2)}, u32[]{:S(2)}) collective-permute-start(bf16[16,256,128]{2,1,0:T(8,128)(2,1)S(1)} %all-to-all-done.1), channel_id=1, source_target_pairs={{0,2},{1,7},{2,4},{3,1},{4,6},{5,3},{6,0},{7,5},{8,10},{9,15},{10,... | collective-permute-start | bytes 3145736 | tf_op jit(solution)/shard_map/ppermute | solution.py:365
  73.9 25.7 %collective-permute-start.8 = (bf16[16,256,128]{2,1,0:T(8,128)(2,1)S(1)}, bf16[16,256,128]{2,1,0:T(8,128)(2,1)S(1)}, u32[]{:S(2)}, u32[]{:S(2)}) collective-permute-start(bf16[16,256,128]{2,1,0:T(8,128)(2,1)S(1)} %all-to-all-done.1), channel_id=1, source_target_pairs={{0,6},{1,3},{2,0},{3,5},{4,2},{5,7},{6,4},{7,1},{8,14},{9,11},{10,... | collective-permute-start | bytes 3145736 | tf_op jit(solution)/shard_map/ppermute | solution.py:365
  75.4 1.2 copy-start.5
  98.4 16.0 %collective-permute-start.12 = (bf16[16,256,128]{2,1,0:T(8,128)(2,1)S(1)}, bf16[16,256,128]{2,1,0:T(8,128)(2,1)S(1)}, u32[]{:S(2)}, u32[]{:S(2)}) collective-permute-start(bf16[16,256,128]{2,1,0:T(8,128)(2,1)S(1)} %collective-permute-done.7), channel_id=1, source_target_pairs={{0,2},{1,7},{2,4},{3,1},{4,6},{5,3},{6,0},{7,5},{8,10},{9,15},{10,... | collective-permute-start | bytes 3145736 | tf_op jit(solution)/shard_map/ppermute | solution.py:365
  99.6 14.8 %collective-permute-start.9 = (bf16[16,256,128]{2,1,0:T(8,128)(2,1)S(1)}, bf16[16,256,128]{2,1,0:T(8,128)(2,1)S(1)}, u32[]{:S(2)}, u32[]{:S(2)}) collective-permute-start(bf16[16,256,128]{2,1,0:T(8,128)(2,1)S(1)} %all-to-all-done.1), channel_id=1, source_target_pairs={{0,1},{1,0},{2,3},{3,2},{4,5},{5,4},{6,7},{7,6},{8,9},{9,8},{10,11... | collective-permute-start | bytes 3145736 | tf_op jit(solution)/shard_map/ppermute | solution.py:368
  99.6 14.8 %collective-permute-start.11 = (bf16[16,256,128]{2,1,0:T(8,128)(2,1)S(1)}, bf16[16,256,128]{2,1,0:T(8,128)(2,1)S(1)}, u32[]{:S(2)}, u32[]{:S(2)}) collective-permute-start(bf16[16,256,128]{2,1,0:T(8,128)(2,1)S(1)} %collective-permute-done.8), channel_id=1, source_target_pairs={{0,1},{1,0},{2,3},{3,2},{4,5},{5,4},{6,7},{7,6},{8,9},{9,8},{10,11... | collective-permute-start | bytes 3145736 | tf_op jit(solution)/shard_map/ppermute | solution.py:368
  100.1 14.3 %collective-permute-start.10 = (bf16[16,256,128]{2,1,0:T(8,128)(2,1)S(1)}, bf16[16,256,128]{2,1,0:T(8,128)(2,1)S(1)}, u32[]{:S(2)}, u32[]{:S(2)}) collective-permute-start(bf16[16,256,128]{2,1,0:T(8,128)(2,1)S(1)} %collective-permute-done.7), channel_id=1, source_target_pairs={{0,1},{1,0},{2,3},{3,2},{4,5},{5,4},{6,7},{7,6},{8,9},{9,8},{10,11... | collective-permute-start | bytes 3145736 | tf_op jit(solution)/shard_map/ppermute | solution.py:368
  108.9 8.2 %copy-start = (bf16[12,12,128,256]{3,2,1,0:T(8,128)(2,1)S(1)}, bf16[12,12,128,256]{3,2,1,0:T(8,128)(2,1)}, u32[]{:S(2)}) copy-start(bf16[12,12,128,256]{3,2,1,0:T(8,128)(2,1)} %get-tuple-element.38.refs_1_) | copy-start | bytes 28311556
  114.4 2.7 %collective-permute-start.13 = (bf16[16,256,128]{2,1,0:T(8,128)(2,1)S(1)}, bf16[16,256,128]{2,1,0:T(8,128)(2,1)S(1)}, u32[]{:S(2)}, u32[]{:S(2)}) collective-permute-start(bf16[16,256,128]{2,1,0:T(8,128)(2,1)S(1)} %collective-permute-done.12), channel_id=1, source_target_pairs={{0,1},{1,0},{2,3},{3,2},{4,5},{5,4},{6,7},{7,6},{8,9},{9,8},{10,11... | collective-permute-start | bytes 3145736 | tf_op jit(solution)/shard_map/ppermute | solution.py:368
